TPU v7x, 128 devices: a whole 4x4x4 slice. The times are simulated.
128 devices in a mesh: batch: 2 (over core), seq: 8 (over y_lo, x), mp: 8 (over y_hi, z).
Axes of the slice: x: 4, y: 4 (y_hi: 2, y_lo: 2; y = y_hi * 2 + y_lo), z: 4, core: 2. Of those that a mesh axis runs over, the one named last changes fastest.
Arguments:
- inputs: bfloat16 [2, 2, 2048, 2048], P(None, 'batch', 'seq'), may hold values from -6 to 6
- cotangent: bfloat16 [2, 2, 2048, 2048], P(None, 'batch', 'seq'), may hold values from -6 to 6
- segments: int32 [2, 2, 2048], P(None, 'batch'), may hold values from 0 to 2, as said below
- query_weight: bfloat16 [2048, 2048], P(('batch', 'seq'), 'mp'), may hold values from -0.1875 to 0.1875
- key_weight: bfloat16 [2048, 2048], P(('batch', 'seq'), 'mp'), may hold values from -0.125 to 0.125
- value_weight: bfloat16 [2048, 2048], P(('batch', 'seq'), 'mp'), may hold values from -0.125 to 0.125
- out_weight: bfloat16 [2048, 2048], P('mp', ('batch', 'seq')), may hold values from -2 to 2
- up_weight: bfloat16 [2048, 8192], P(('batch', 'seq'), 'mp'), may hold values from -0.125 to 0.125
- down_weight: bfloat16 [8192, 2048], P('mp', ('batch', 'seq')), may hold values from -0.0625 to 0.0625
- query_bias: float32 [2048], P('mp'), may hold values from -3 to 3
- value_bias: float32 [2048], P('mp'), may hold values from -0.3 to 0.3
- out_bias: float32 [2048], replicated, may hold values from -2 to 2
- up_bias: float32 [8192], P('mp'), may hold values from -3 to 3
- down_bias: float32 [2048], replicated, may hold values from -2 to 2
- attn_gain: float32 [2048], replicated, may hold values from 0.5 to 1.5
- attn_shift: float32 [2048], replicated, may hold values from -2 to 2
- ffn_gain: float32 [2048], replicated, may hold values from 0.5 to 1.5
- ffn_shift: float32 [2048], replicated, may hold values from -2 to 2
Outputs:
- outputs: bfloat16 [2, 2, 2048, 2048], P(None, 'batch', 'seq')
- input_grad: bfloat16 [2, 2, 2048, 2048], P(None, 'batch', 'seq')
- query_weight_grad: float32 [2048, 2048], P(('batch', 'seq'), 'mp')
- key_weight_grad: float32 [2048, 2048], P(('batch', 'seq'), 'mp')
- value_weight_grad: float32 [2048, 2048], P(('batch', 'seq'), 'mp')
- out_weight_grad: float32 [2048, 2048], P('mp', ('batch', 'seq'))
- up_weight_grad: float32 [2048, 8192], P(('batch', 'seq'), 'mp')
- down_weight_grad: float32 [8192, 2048], P('mp', ('batch', 'seq'))
- query_bias_grad: float32 [2048], P('mp')
- value_bias_grad: float32 [2048], P('mp')
- out_bias_grad: float32 [2048], replicated
- up_bias_grad: float32 [8192], P('mp')
- down_bias_grad: float32 [2048], replicated
- attn_gain_grad: float32 [2048], replicated
- attn_shift_grad: float32 [2048], replicated
- ffn_gain_grad: float32 [2048], replicated
- ffn_shift_grad: float32 [2048], replicated
Inputs may be any that keep to these rules, and one draw needn't show every extreme that they name: `segments`: each pack holds three documents, numbered 0, 1, 2 in order; the first ends within the pack's first 256 tokens and the last begins within its last 256 tokens, both ends drawn afresh for each pack.
All inputs are finite; a program needn't handle non-finite values.
Results may differ from a plain program's by a relative error of at most 0.029.
Values may be sent and summed in bfloat16 or wider, within the bound.
No kernel may reach another device: no remote copies, remote signals or barrier semaphores. Data moves between devices by JAX's collectives and lax.ppermute only.
A program may use at most 256 MiB of HBM per device.

v0:
```python
import jax
import jax.numpy as jnp
from jax import lax
from jax.sharding import PartitionSpec as P

HD = 128
WINDOW = 1024


NORM_EPSILON = 1e-05
BLOCKED = -1e30


def norm_rows(values, gain_row, shift_row):
    center = jnp.mean(values, axis=-1, keepdims=True)
    centered = values - center
    spread = jnp.mean(centered * centered, axis=-1, keepdims=True)
    return centered * lax.rsqrt(spread + NORM_EPSILON) * gain_row + shift_row


def smooth_unit(values):
    return jax.nn.gelu(values, approximate=True)


def allowed_keys(pack_segs, first_row, row_count, windowed):
    query_places = first_row + jnp.arange(row_count, dtype=jnp.int32)
    key_places = jnp.arange(pack_segs.shape[0], dtype=jnp.int32)
    query_segs = lax.dynamic_slice_in_dim(pack_segs, first_row, row_count)
    allowed = query_segs[:, None] == pack_segs[None, :]
    if windowed:
        allowed = allowed & (jnp.abs(query_places[:, None] - key_places[None, :]) <= WINDOW // 2)
    return allowed


def attend_scores(queries, all_keys, allowed):
    row_count = queries.shape[0]
    head_count = queries.shape[1] // HD
    query_heads = queries.reshape(row_count, head_count, HD)
    key_heads = all_keys.reshape(-1, head_count, HD)
    scores = jnp.einsum(
        "qhd,khd->hqk", query_heads, key_heads, preferred_element_type=jnp.float32
    ) * HD ** (-0.5)
    scores = jnp.where(allowed[None], scores, BLOCKED)
    row_max = jnp.max(scores, axis=-1, keepdims=True)
    exp_scores = jnp.exp(scores - row_max)
    return exp_scores / jnp.sum(exp_scores, axis=-1, keepdims=True)


def fetch_rows(matrices):
    return (
        lax.all_gather(matrices[0], ("batch", "seq"), axis=0, tiled=True),
        lax.all_gather(matrices[1], ("batch", "seq"), axis=0, tiled=True),
        lax.all_gather(matrices[2], ("batch", "seq"), axis=0, tiled=True),
        lax.all_gather(matrices[3], ("batch", "seq"), axis=1, tiled=True),
        lax.all_gather(matrices[4], ("batch", "seq"), axis=0, tiled=True),
        lax.all_gather(matrices[5], ("batch", "seq"), axis=1, tiled=True),
    )


def row_terms(pairs):
    total = None
    for left, right in pairs:
        part_sum = jnp.dot(left, right, preferred_element_type=jnp.float32)
        total = part_sum if total is None else total + part_sum
    return total


def layer_forward(stream, stream_low, matrices, vectors, pack_segs, first_row, windowed):
    query_weight, key_weight, value_weight, out_weight, up_weight, down_weight = matrices
    (
        query_bias,
        value_bias,
        out_bias,
        up_bias,
        down_bias,
        attn_gain,
        attn_shift,
        ffn_gain,
        ffn_shift,
    ) = vectors
    row_count = stream_low.shape[0]
    queries = (
        jnp.dot(stream_low, query_weight, preferred_element_type=jnp.float32) + query_bias
    ).astype(jnp.bfloat16)
    key_rows = jnp.dot(stream_low, key_weight, preferred_element_type=jnp.float32).astype(
        jnp.bfloat16
    )
    value_rows = (
        jnp.dot(stream_low, value_weight, preferred_element_type=jnp.float32) + value_bias
    ).astype(jnp.bfloat16)
    all_keys, all_values = (
        lax.all_gather(key_rows, "seq", axis=0, tiled=True),
        lax.all_gather(value_rows, "seq", axis=0, tiled=True),
    )
    allowed = allowed_keys(pack_segs, first_row, row_count, windowed)
    weights = attend_scores(queries, all_keys, allowed)
    head_count = queries.shape[1] // HD
    attended = jnp.einsum(
        "hqk,khd->qhd",
        weights.astype(jnp.bfloat16),
        all_values.reshape(-1, head_count, HD),
        preferred_element_type=jnp.float32,
    ).reshape(row_count, -1)
    attended_low = attended.astype(jnp.bfloat16)
    branch = lax.psum(jnp.dot(attended_low, out_weight, preferred_element_type=jnp.float32), "mp")
    residual = stream + branch + out_bias
    first_norm = norm_rows(residual, attn_gain, attn_shift)
    first_low = first_norm.astype(jnp.bfloat16)
    up_values = jnp.dot(first_low, up_weight, preferred_element_type=jnp.float32) + up_bias
    active = smooth_unit(up_values).astype(jnp.bfloat16)
    second = lax.psum(jnp.dot(active, down_weight, preferred_element_type=jnp.float32), "mp")
    summed = first_norm + second + down_bias
    saved = (
        stream_low,
        queries,
        all_keys,
        all_values,
        allowed,
        attended_low,
        residual,
        first_low,
        up_values,
        active,
        summed,
    )
    return (norm_rows(summed, ffn_gain, ffn_shift), saved)


def layer_backward(gradient, saved, matrices, vectors):
    query_weight, key_weight, value_weight, out_weight, up_weight, down_weight = matrices
    (
        query_bias,
        value_bias,
        out_bias,
        up_bias,
        down_bias,
        attn_gain,
        attn_shift,
        ffn_gain,
        ffn_shift,
    ) = vectors
    (
        stream_low,
        queries,
        all_keys,
        all_values,
        allowed,
        attended_low,
        residual,
        first_low,
        up_values,
        active,
        summed,
    ) = saved
    row_count = stream_low.shape[0]
    head_count = queries.shape[1] // HD
    _, pull_second = jax.vjp(norm_rows, summed, ffn_gain, ffn_shift)
    grad_summed, grad_ffn_gain, grad_ffn_shift = pull_second(gradient)
    grad_second = grad_summed.astype(jnp.bfloat16)
    grad_down = jnp.dot(active.T, grad_second, preferred_element_type=jnp.float32)
    grad_down_bias = jnp.sum(grad_second.astype(jnp.float32), axis=0)
    grad_active = jnp.dot(grad_second, down_weight.T, preferred_element_type=jnp.float32)
    _, pull_unit = jax.vjp(smooth_unit, up_values)
    grad_up = pull_unit(grad_active)[0].astype(jnp.bfloat16)
    grad_up_weight = jnp.dot(first_low.T, grad_up, preferred_element_type=jnp.float32)
    grad_up_bias = jnp.sum(grad_up.astype(jnp.float32), axis=0)
    grad_first = lax.psum(jnp.dot(grad_up, up_weight.T, preferred_element_type=jnp.float32), "mp")
    grad_first = grad_first + grad_summed
    _, pull_first = jax.vjp(norm_rows, residual, attn_gain, attn_shift)
    grad_residual, grad_attn_gain, grad_attn_shift = pull_first(grad_first)
    grad_branch = grad_residual.astype(jnp.bfloat16)
    grad_out_weight = jnp.dot(attended_low.T, grad_branch, preferred_element_type=jnp.float32)
    grad_out_bias = jnp.sum(grad_branch.astype(jnp.float32), axis=0)
    grad_attended = jnp.dot(grad_branch, out_weight.T, preferred_element_type=jnp.float32).astype(
        jnp.bfloat16
    )
    grad_attended = grad_attended.reshape(row_count, head_count, HD)
    weights = attend_scores(queries, all_keys, allowed)
    key_heads = all_keys.reshape(-1, head_count, HD)
    value_heads = all_values.reshape(-1, head_count, HD)
    query_heads = queries.reshape(row_count, head_count, HD)
    grad_weights = jnp.einsum(
        "qhd,khd->hqk", grad_attended, value_heads, preferred_element_type=jnp.float32
    )
    grad_scores = (
        weights * (grad_weights - jnp.sum(weights * grad_weights, axis=-1, keepdims=True))
    ).astype(jnp.bfloat16)
    scaling = HD ** (-0.5)
    grad_queries = (
        jnp.einsum("hqk,khd->qhd", grad_scores, key_heads, preferred_element_type=jnp.float32)
        * scaling
    )
    grad_queries = grad_queries.astype(jnp.bfloat16).reshape(row_count, -1)
    key_terms = (
        jnp.einsum("hqk,qhd->khd", grad_scores, query_heads, preferred_element_type=jnp.float32)
        * scaling
    )
    key_terms = key_terms.reshape(-1, head_count * HD)
    value_terms = jnp.einsum(
        "hqk,qhd->khd",
        weights.astype(jnp.bfloat16),
        grad_attended,
        preferred_element_type=jnp.float32,
    ).reshape(-1, head_count * HD)
    grad_keys, grad_values = (
        lax.psum_scatter(key_terms, "seq", scatter_dimension=0, tiled=True),
        lax.psum_scatter(value_terms, "seq", scatter_dimension=0, tiled=True),
    )
    grad_keys = grad_keys.astype(jnp.bfloat16)
    grad_values = grad_values.astype(jnp.bfloat16)
    grad_query_weight = jnp.dot(stream_low.T, grad_queries, preferred_element_type=jnp.float32)
    grad_key_weight = jnp.dot(stream_low.T, grad_keys, preferred_element_type=jnp.float32)
    grad_value_weight = jnp.dot(stream_low.T, grad_values, preferred_element_type=jnp.float32)
    grad_query_bias = jnp.sum(grad_queries.astype(jnp.float32), axis=0)
    grad_value_bias = jnp.sum(grad_values.astype(jnp.float32), axis=0)
    pairs = (
        (grad_queries, query_weight.T),
        (grad_keys, key_weight.T),
        (grad_values, value_weight.T),
    )
    input_terms = lax.psum(row_terms(pairs), "mp")
    grad_stream = input_terms + grad_residual
    matrix_grads = (
        grad_query_weight,
        grad_key_weight,
        grad_value_weight,
        grad_out_weight,
        grad_up_weight,
        grad_down,
    )
    vector_grads = (
        grad_query_bias,
        grad_value_bias,
        grad_out_bias,
        grad_up_bias,
        grad_down_bias,
        grad_attn_gain,
        grad_attn_shift,
        grad_ffn_gain,
        grad_ffn_shift,
    )
    return (grad_stream, matrix_grads, vector_grads)


def add_tuples(totals, additions):
    if totals is None:
        return additions
    return tuple((total_part + new_part for total_part, new_part in zip(totals, additions)))


def shards(
    inputs,
    cotangent,
    segments,
    query_weight,
    key_weight,
    value_weight,
    out_weight,
    up_weight,
    down_weight,
    query_bias,
    value_bias,
    out_bias,
    up_bias,
    down_bias,
    attn_gain,
    attn_shift,
    ffn_gain,
    ffn_shift,
):
    local_matrices = (query_weight, key_weight, value_weight, out_weight, up_weight, down_weight)
    vectors = (
        query_bias,
        value_bias,
        out_bias,
        up_bias,
        down_bias,
        attn_gain,
        attn_shift,
        ffn_gain,
        ffn_shift,
    )
    row_count = inputs.shape[2]
    first_row = lax.axis_index("seq") * row_count

    def weights_now():
        return fetch_rows(local_matrices)

    matrix_totals = None
    vector_totals = None
    results = []
    input_grads = []
    for micro_step in range(inputs.shape[0]):
        pack_segs = segments[micro_step, 0]
        stream_low = inputs[micro_step, 0]
        stream = stream_low.astype(jnp.float32)
        middle, saved_first = layer_forward(
            stream, stream_low, weights_now(), vectors, pack_segs, first_row, True
        )
        middle_low = middle.astype(jnp.bfloat16)
        final, saved_second = layer_forward(
            middle, middle_low, weights_now(), vectors, pack_segs, first_row, False
        )
        results.append(final.astype(jnp.bfloat16))
        gradient = cotangent[micro_step, 0].astype(jnp.float32)
        gradient, matrix_grads, vector_grads = layer_backward(
            gradient, saved_second, weights_now(), vectors
        )
        matrix_totals = add_tuples(matrix_totals, matrix_grads)
        vector_totals = add_tuples(vector_totals, vector_grads)
        gradient, matrix_grads, vector_grads = layer_backward(
            gradient, saved_first, weights_now(), vectors
        )
        matrix_totals = add_tuples(matrix_totals, matrix_grads)
        vector_totals = add_tuples(vector_totals, vector_grads)
        input_grads.append(gradient.astype(jnp.bfloat16))
    matrix_shards = (
        lax.psum_scatter(matrix_totals[0], ("batch", "seq"), scatter_dimension=0, tiled=True),
        lax.psum_scatter(matrix_totals[1], ("batch", "seq"), scatter_dimension=0, tiled=True),
        lax.psum_scatter(matrix_totals[2], ("batch", "seq"), scatter_dimension=0, tiled=True),
        lax.psum_scatter(matrix_totals[3], ("batch", "seq"), scatter_dimension=1, tiled=True),
        lax.psum_scatter(matrix_totals[4], ("batch", "seq"), scatter_dimension=0, tiled=True),
        lax.psum_scatter(matrix_totals[5], ("batch", "seq"), scatter_dimension=1, tiled=True),
    )
    vector_full = lax.psum(vector_totals, ("batch", "seq"))
    return (
        jnp.stack(results)[:, None],
        jnp.stack(input_grads)[:, None],
        matrix_shards[0],
        matrix_shards[1],
        matrix_shards[2],
        matrix_shards[3],
        matrix_shards[4],
        matrix_shards[5],
        vector_full[0],
        vector_full[1],
        vector_full[2],
        vector_full[3],
        vector_full[4],
        vector_full[5],
        vector_full[6],
        vector_full[7],
        vector_full[8],
    )


def solution(mesh):
    in_specs = (
        P(None, "batch", "seq", None),
        P(None, "batch", "seq", None),
        P(None, "batch", None),
        P(("batch", "seq"), "mp"),
        P(("batch", "seq"), "mp"),
        P(("batch", "seq"), "mp"),
        P("mp", ("batch", "seq")),
        P(("batch", "seq"), "mp"),
        P("mp", ("batch", "seq")),
        P("mp"),
        P("mp"),
        P(),
        P("mp"),
        P(),
        P(),
        P(),
        P(),
        P(),
    )
    out_specs = (
        P(None, "batch", "seq", None),
        P(None, "batch", "seq", None),
        P(("batch", "seq"), "mp"),
        P(("batch", "seq"), "mp"),
        P(("batch", "seq"), "mp"),
        P("mp", ("batch", "seq")),
        P(("batch", "seq"), "mp"),
        P("mp", ("batch", "seq")),
        P("mp"),
        P("mp"),
        P(),
        P("mp"),
        P(),
        P(),
        P(),
        P(),
        P(),
    )
    return jax.shard_map(shards, mesh=mesh, in_specs=in_specs, out_specs=out_specs, check_vma=False)
```

profile of v0, /device:TPU:1, one launch (start us, length us, event | category | flops | bytes accessed | tf_op | source)
XLA Modules:
  0.0 2412.1 jit_solution(9019632323723833751)
XLA Ops:
  9.5 36.4 %all-gather.21.cloned.1.call-done = bf16[2048,256]{1,0:T(8,128)(2,1)} async-done(((bf16[128,256]{1,0:T(8,128)(2,1)}), bf16[2048,256]{1,0:T(8,128)(2,1)}) %all-gather.21.cloned.1.call-update) | async-done | bytes 1048592 | tf_op jit(solution)/shard_map/all_gather | solution.py:52
  51.2 28.9 %all-gather.15.cloned.1.call-done = bf16[2048,256]{1,0:T(8,128)(2,1)} async-done(((bf16[128,256]{1,0:T(8,128)(2,1)}), bf16[2048,256]{1,0:T(8,128)(2,1)}) %all-gather.15.cloned.1.call-update) | async-done | bytes 1048592 | tf_op jit(solution)/shard_map/all_gather | solution.py:53
  89.0 25.3 %all-gather.19.cloned.1.call-done = bf16[2048,256]{1,0:T(8,128)(2,1)} async-done(((bf16[128,256]{1,0:T(8,128)(2,1)}), bf16[2048,256]{1,0:T(8,128)(2,1)}) %all-gather.19.cloned.1.call-update) | async-done | bytes 1048592 | tf_op jit(solution)/shard_map/all_gather | solution.py:51
  116.8 33.1 %all-gather.37.cloned.1.call-done = bf16[2048,256]{1,0:T(8,128)(2,1)} async-done(((bf16[256,256]{1,0:T(8,128)(2,1)}), bf16[2048,256]{1,0:T(8,128)(2,1)}) %all-gather.37.cloned.1.call-update) | async-done | bytes 1048592 | tf_op jit(solution)/shard_map/all_gather | solution.py:92
  151.4 38.5 %all-gather.23.cloned.1.call-done = bf16[2048,256]{1,0:T(8,128)(2,1)} async-done(((bf16[256,256]{1,0:T(8,128)(2,1)}), bf16[2048,256]{1,0:T(8,128)(2,1)}) %all-gather.23.cloned.1.call-update) | async-done | bytes 1048592 | tf_op jit(solution)/shard_map/all_gather | solution.py:92
  191.4 3.7 fusion.232
  195.1 34.9 %all-gather.35.cloned.1.call-done = bf16[2048,256]{1,0:T(8,128)(2,1)} async-done(((bf16[256,256]{1,0:T(8,128)(2,1)}), bf16[2048,256]{1,0:T(8,128)(2,1)}) %all-gather.35.cloned.1.call-update) | async-done | bytes 1048592 | tf_op jit(solution)/shard_map/all_gather | solution.py:93
  233.4 36.7 %all-gather.25.cloned.1.call-done = bf16[256,2048]{1,0:T(8,128)(2,1)} async-done(((bf16[256,128]{1,0:T(8,128)(2,1)}), bf16[256,2048]{1,0:T(8,128)(2,1)}) %all-gather.25.cloned.1.call-update) | async-done | bytes 1048592 | tf_op jit(solution)/shard_map/all_gather | solution.py:54
  276.8 29.2 %all-gather.17.cloned.1.call-done = bf16[2048,256]{1,0:T(8,128)(2,1)} async-done(((bf16[256,256]{1,0:T(8,128)(2,1)}), bf16[2048,256]{1,0:T(8,128)(2,1)}) %all-gather.17.cloned.1.call-update) | async-done | bytes 1048592 | tf_op jit(solution)/shard_map/all_gather | solution.py:93
  312.8 113.0 %all-reduce.32.cloned.1.call-done = (f32[256,2048]{1,0:T(8,128)}, f32[256,2048]{1,0:T(8,128)}) async-done(((f32[256,2048]{1,0:T(8,128)}, f32[256,2048]{1,0:T(8,128)}), (f32[256,2048]{1,0:T(8,128)}, f32[256,2048]{1,0:T(8,128)})) %all-reduce.32.cloned.1.call-update) | async-done | bytes 4194320 | tf_op jit(solution)/shard_map/psum | solution.py:105
  430.7 32.9 %all-gather.27.cloned.1.call-done = bf16[2048,1024]{1,0:T(8,128)(2,1)} async-done(((bf16[128,1024]{1,0:T(8,128)(2,1)}), bf16[2048,1024]{1,0:T(8,128)(2,1)}) %all-gather.27.cloned.1.call-update) | async-done | bytes 4194320 | tf_op jit(solution)/shard_map/all_gather | solution.py:55
  463.6 5.3 convolution_add_fusion.12
  471.2 39.0 %all-gather.29.cloned.1.call-done = bf16[1024,2048]{1,0:T(8,128)(2,1)} async-done(((bf16[1024,128]{1,0:T(8,128)(2,1)}), bf16[1024,2048]{1,0:T(8,128)(2,1)}) %all-gather.29.cloned.1.call-update) | async-done | bytes 4194320 | tf_op jit(solution)/shard_map/all_gather | solution.py:56
  510.3 5.3 fusion.197
  518.4 110.4 %all-reduce.30.cloned.1.call-done = (f32[256,2048]{1,0:T(8,128)}, f32[256,2048]{1,0:T(8,128)}) async-done(((f32[256,2048]{1,0:T(8,128)}, f32[256,2048]{1,0:T(8,128)}), (f32[256,2048]{1,0:T(8,128)}, f32[256,2048]{1,0:T(8,128)})) %all-reduce.30.cloned.1.call-update) | async-done | bytes 4194320 | tf_op jit(solution)/shard_map/psum | solution.py:111
  628.9 4.0 fusion.227
  650.0 21.1 all-gather.41.cloned.1.call-done
  673.4 37.8 %all-gather.33.cloned.1.call-done = bf16[2048,256]{1,0:T(8,128)(2,1)} async-done(((bf16[256,256]{1,0:T(8,128)(2,1)}), bf16[2048,256]{1,0:T(8,128)(2,1)}) %all-gather.33.cloned.1.call-update) | async-done | bytes 1048592 | tf_op jit(solution)/shard_map/all_gather | solution.py:92
  713.4 5.0 fusion.234
  718.5 32.8 %all-gather.39.cloned.1.call-done = bf16[2048,256]{1,0:T(8,128)(2,1)} async-done(((bf16[256,256]{1,0:T(8,128)(2,1)}), bf16[2048,256]{1,0:T(8,128)(2,1)}) %all-gather.39.cloned.1.call-update) | async-done | bytes 1048592 | tf_op jit(solution)/shard_map/all_gather | solution.py:93
  751.2 4.5 convolution_convert_fusion
  758.4 5.0 fusion.235
  763.4 27.9 %all-gather.31.cloned.1.call-done = bf16[2048,256]{1,0:T(8,128)(2,1)} async-done(((bf16[256,256]{1,0:T(8,128)(2,1)}), bf16[2048,256]{1,0:T(8,128)(2,1)}) %all-gather.31.cloned.1.call-update) | async-done | bytes 1048592 | tf_op jit(solution)/shard_map/all_gather | solution.py:93
  791.3 3.8 convolution_convert_fusion.2
  797.4 114.1 %all-reduce.28.cloned.1.call-done = (f32[256,2048]{1,0:T(8,128)}, f32[256,2048]{1,0:T(8,128)}) async-done(((f32[256,2048]{1,0:T(8,128)}, f32[256,2048]{1,0:T(8,128)}), (f32[256,2048]{1,0:T(8,128)}, f32[256,2048]{1,0:T(8,128)})) %all-reduce.28.cloned.1.call-update) | async-done | bytes 4194320 | tf_op jit(solution)/shard_map/psum | solution.py:105
  911.5 4.7 fusion.225
  930.4 108.7 %all-reduce.26.cloned.1.call-done = (f32[256,2048]{1,0:T(8,128)}, f32[256,2048]{1,0:T(8,128)}) async-done(((f32[256,2048]{1,0:T(8,128)}, f32[256,2048]{1,0:T(8,128)}), (f32[256,2048]{1,0:T(8,128)}, f32[256,2048]{1,0:T(8,128)})) %all-reduce.26.cloned.1.call-update) | async-done | bytes 4194320 | tf_op jit(solution)/shard_map/psum | solution.py:111
  1039.1 4.6 fusion.223
  1066.1 108.8 %all-reduce.24.cloned.1.call-done = (f32[256,2048]{1,0:T(8,128)}, f32[256,2048]{1,0:T(8,128)}) async-done(((f32[256,2048]{1,0:T(8,128)}, f32[256,2048]{1,0:T(8,128)}), (f32[256,2048]{1,0:T(8,128)}, f32[256,2048]{1,0:T(8,128)})) %all-reduce.24.cloned.1.call-update) | async-done | bytes 4194320 | tf_op jit(solution)/shard_map/psum | solution.py:167
  1175.0 6.4 multiply_reduce_fusion.9
  1192.4 4.8 fusion.117
  1206.1 4.7 fusion.123
  1220.1 8.6 reduce-scatter.23.cloned.1.call-done
  1228.6 3.8 convolution_add_fusion.6
  1232.5 39.8 %reduce-scatter.25.cloned.1.call-done = f32[256,256]{0,1:T(8,128)} async-done(((f32[2048,256]{0,1:T(8,128)}), f32[256,256]{0,1:T(8,128)}) %reduce-scatter.25.cloned.1.call-update) | async-done | bytes 262160 | tf_op jit(solution)/shard_map/reduce_scatter | solution.py:207
  1272.3 3.8 convolution_add_fusion.5
  1276.1 39.9 %reduce-scatter.15.cloned.1.call-done = f32[256,256]{0,1:T(8,128)} async-done(((f32[2048,256]{0,1:T(8,128)}), f32[256,256]{0,1:T(8,128)}) %reduce-scatter.15.cloned.1.call-update) | async-done | bytes 262160 | tf_op jit(solution)/shard_map/reduce_scatter | solution.py:206
  1316.0 3.9 convolution_add_fusion.10
  1319.9 40.1 %reduce-scatter.17.cloned.1.call-done = f32[256,256]{0,1:T(8,128)} async-done(((f32[2048,256]{0,1:T(8,128)}), f32[256,256]{0,1:T(8,128)}) %reduce-scatter.17.cloned.1.call-update) | async-done | bytes 262160 | tf_op jit(solution)/shard_map/reduce_scatter | solution.py:207
  1360.0 3.9 convolution_add_fusion.9
  1364.0 114.2 %all-reduce.22.cloned.1.call-done = (f32[256,2048]{1,0:T(8,128)}, f32[256,2048]{1,0:T(8,128)}) async-done(((f32[256,2048]{1,0:T(8,128)}, f32[256,2048]{1,0:T(8,128)}), (f32[256,2048]{1,0:T(8,128)}, f32[256,2048]{1,0:T(8,128)})) %all-reduce.22.cloned.1.call-update) | async-done | bytes 4194320 | tf_op jit(solution)/shard_map/psum | solution.py:221
  1478.2 7.3 multiply_reduce_fusion.5
  1502.6 108.8 %all-reduce.20.cloned.1.call-done = (f32[256,2048]{1,0:T(8,128)}, f32[256,2048]{1,0:T(8,128)}) async-done(((f32[256,2048]{1,0:T(8,128)}, f32[256,2048]{1,0:T(8,128)}), (f32[256,2048]{1,0:T(8,128)}, f32[256,2048]{1,0:T(8,128)})) %all-reduce.20.cloned.1.call-update) | async-done | bytes 4194320 | tf_op jit(solution)/shard_map/psum | solution.py:167
  1611.5 6.5 multiply_reduce_fusion.8
  1629.0 4.8 fusion.120
  1643.5 4.4 fusion.126
  1657.5 7.6 reduce-scatter.27.cloned.1.call-done
  1668.7 39.9 %reduce-scatter.29.cloned.1.call-done = f32[256,256]{0,1:T(8,128)} async-done(((f32[2048,256]{0,1:T(8,128)}), f32[256,256]{0,1:T(8,128)}) %reduce-scatter.29.cloned.1.call-update) | async-done | bytes 262160 | tf_op jit(solution)/shard_map/reduce_scatter | solution.py:207
  1708.6 3.8 convolution_add_fusion.3
  1712.4 39.8 %reduce-scatter.19.cloned.1.call-done = f32[256,256]{0,1:T(8,128)} async-done(((f32[2048,256]{0,1:T(8,128)}), f32[256,256]{0,1:T(8,128)}) %reduce-scatter.19.cloned.1.call-update) | async-done | bytes 262160 | tf_op jit(solution)/shard_map/reduce_scatter | solution.py:206
  1755.7 40.2 %reduce-scatter.21.cloned.1.call-done = f32[256,256]{0,1:T(8,128)} async-done(((f32[2048,256]{0,1:T(8,128)}), f32[256,256]{0,1:T(8,128)}) %reduce-scatter.21.cloned.1.call-update) | async-done | bytes 262160 | tf_op jit(solution)/shard_map/reduce_scatter | solution.py:207
  1795.8 3.8 convolution_add_fusion.7
  1831.2 4.8 fusion.205
  1836.0 4.8 fusion.208
  1840.8 11.7 add_add_fusion.1
  1858.1 4.7 fusion.193
  1862.9 8.9 add_add_fusion
  1877.6 64.3 %all-reduce = (f32[256]{0:T(256)}, f32[256]{0:T(256)}, f32[2048]{0:T(1024)}, f32[1024]{0:T(1024)}, f32[2048]{0:T(1024)}, /*index=5*/f32[2048]{0:T(1024)}, f32[2048]{0:T(1024)}, f32[2048]{0:T(1024)}, f32[2048]{0:T(1024)}) all-reduce(f32[256]{0:T(256)S(1)} %add_bitcast_fusion, ...), channel_id=1, replica_groups=mesh['batch'=2,'seq'=8,'mp'=8] {'batch','seq'}, use_global_device_ids=true, to_apply=%region_78.79 | all-reduce | flops 13824 | bytes 110592 | tf_op jit(solution)/shard_map/psum | solution.py:325
  1946.5 36.8 %reduce-scatter.31.cloned.1.call-done = f32[128,256]{1,0:T(8,128)} async-done(((f32[2048,256]{1,0:T(8,128)}), f32[128,256]{1,0:T(8,128)}) %reduce-scatter.31.cloned.1.call-update) | async-done | bytes 131088 | tf_op jit(solution)/shard_map/reduce_scatter | solution.py:318
  1983.3 73.3 %reduce-scatter.37.cloned.1.call-done = f32[256,128]{1,0:T(8,128)} async-done(((f32[256,2048]{1,0:T(8,128)}), f32[256,128]{1,0:T(8,128)}) %reduce-scatter.37.cloned.1.call-update) | async-done | bytes 131088 | tf_op jit(solution)/shard_map/reduce_scatter | solution.py:321
  2056.6 72.5 %reduce-scatter.33.cloned.1.call-done = f32[128,256]{1,0:T(8,128)} async-done(((f32[2048,256]{1,0:T(8,128)}), f32[128,256]{1,0:T(8,128)}) %reduce-scatter.33.cloned.1.call-update) | async-done | bytes 131088 | tf_op jit(solution)/shard_map/reduce_scatter | solution.py:319
  2129.1 73.1 %reduce-scatter.35.cloned.1.call-done = f32[128,256]{1,0:T(8,128)} async-done(((f32[2048,256]{1,0:T(8,128)}), f32[128,256]{1,0:T(8,128)}) %reduce-scatter.35.cloned.1.call-update) | async-done | bytes 131088 | tf_op jit(solution)/shard_map/reduce_scatter | solution.py:320
  2202.2 103.5 %reduce-scatter.39.cloned.1.call-done = f32[128,1024]{1,0:T(8,128)} async-done(((f32[2048,1024]{1,0:T(8,128)}), f32[128,1024]{1,0:T(8,128)}) %reduce-scatter.39.cloned.1.call-update) | async-done | bytes 524304 | tf_op jit(solution)/shard_map/reduce_scatter | solution.py:322
  2305.7 99.7 %reduce-scatter.41.cloned.1.call-done = f32[1024,128]{1,0:T(8,128)} async-done(((f32[1024,2048]{1,0:T(8,128)}), f32[1024,128]{1,0:T(8,128)}) %reduce-scatter.41.cloned.1.call-update) | async-done | bytes 524304 | tf_op jit(solution)/shard_map/reduce_scatter | solution.py:323
  (681 shorter events, 241.1 us)
Async XLA Ops:
  7.2 38.6 %all-gather.21.cloned.1.call-start = ((), (), s32[]{:S(2)}) async-start(), calls=%async_computation.17 | async-start | bytes 1114112 | tf_op jit(solution)/shard_map/all_gather | solution.py:52
  7.9 72.1 %all-gather.15.cloned.1.call-start = ((), (), s32[]{:S(2)}) async-start(), calls=%async_computation.14 | async-start | bytes 1114112 | tf_op jit(solution)/shard_map/all_gather | solution.py:53
  8.7 105.6 %all-gather.19.cloned.1.call-start = ((), (), s32[]{:S(2)}) async-start(), calls=%async_computation.16 | async-start | bytes 1114112 | tf_op jit(solution)/shard_map/all_gather | solution.py:51
  9.4 140.5 %all-gather.37.cloned.1.call-start = ((), (), s32[]{:S(2)}) async-start(), calls=%async_computation.25 | async-start | bytes 1179648 | tf_op jit(solution)/shard_map/all_gather | solution.py:92
  48.6 141.4 %all-gather.23.cloned.1.call-start = ((), (), s32[]{:S(2)}) async-start(), calls=%async_computation.18 | async-start | bytes 1179648 | tf_op jit(solution)/shard_map/all_gather | solution.py:92
  51.1 178.9 %all-gather.35.cloned.1.call-start = ((), (), s32[]{:S(2)}) async-start(), calls=%async_computation.24 | async-start | bytes 1179648 | tf_op jit(solution)/shard_map/all_gather | solution.py:93
  82.5 187.6 %all-gather.25.cloned.1.call-start = ((), (), s32[]{:S(2)}) async-start(), calls=%async_computation.19 | async-start | bytes 1114112 | tf_op jit(solution)/shard_map/all_gather | solution.py:54
  83.2 222.7 %all-gather.17.cloned.1.call-start = ((), (), s32[]{:S(2)}) async-start(), calls=%async_computation.15 | async-start | bytes 1179648 | tf_op jit(solution)/shard_map/all_gather | solution.py:93
  88.5 337.3 %all-reduce.32.cloned.1.call-start = ((), (), s32[]{:S(2)}) async-start(), calls=%async_computation.49 | async-start | bytes 8388608 | tf_op jit(solution)/shard_map/psum | solution.py:105
  116.2 113.8 %copy-start.118 = (bf16[256,256]{0,1:T(8,128)(2,1)}, bf16[256,256]{0,1:T(8,128)(2,1)S(1)}, u32[]{:S(2)}) copy-start(bf16[256,256]{0,1:T(8,128)(2,1)S(1)} %fusion.54) | copy-start | bytes 393220
  116.8 189.2 %copy-start.116 = (bf16[256,256]{0,1:T(8,128)(2,1)}, bf16[256,256]{0,1:T(8,128)(2,1)S(1)}, u32[]{:S(2)}) copy-start(bf16[256,256]{0,1:T(8,128)(2,1)S(1)} %fusion.50) | copy-start | bytes 393220
  191.4 114.5 %copy-start.65 = (bf16[2048,256]{0,1:T(8,128)(2,1)}, bf16[2048,256]{0,1:T(8,128)(2,1)S(1)}, u32[]{:S(2)}) copy-start(bf16[2048,256]{0,1:T(8,128)(2,1)S(1)} %copy.81) | copy-start | bytes 3145732
  311.2 114.6 %copy-start.164 = (f32[2048]{0:T(1024)S(1)}, f32[2048]{0:T(1024)}, u32[]{:S(2)}) copy-start(f32[2048]{0:T(1024)} %param.29) | copy-start | bytes 24580
  311.2 152.4 %all-gather.27.cloned.1.call-start = ((), (), s32[]{:S(2)}) async-start(), calls=%async_computation.20 | async-start | bytes 4456448 | tf_op jit(solution)/shard_map/all_gather | solution.py:55
  311.8 198.4 %all-gather.29.cloned.1.call-start = ((), (), s32[]{:S(2)}) async-start(), calls=%async_computation.21 | async-start | bytes 4456448 | tf_op jit(solution)/shard_map/all_gather | solution.py:56
  312.6 316.3 %all-reduce.30.cloned.1.call-start = ((), (), s32[]{:S(2)}) async-start(), calls=%async_computation.48 | async-start | bytes 8388608 | tf_op jit(solution)/shard_map/psum | solution.py:111
  429.3 199.5 %copy-start.129 = (f32[256]{0:T(256)}, f32[256]{0:T(256)S(1)}, u32[]{:S(2)}) copy-start(f32[256]{0:T(256)S(1)} %broadcast_multiply_fusion.3) | copy-start | bytes 3076
  429.8 199.1 %copy-start.123 = (f32[256]{0:T(256)}, f32[256]{0:T(256)S(1)}, u32[]{:S(2)}) copy-start(f32[256]{0:T(256)S(1)} %broadcast_multiply_fusion.7) | copy-start | bytes 3076
  430.7 198.2 %copy-start.166 = (f32[256]{0:T(256)}, f32[256]{0:T(256)S(1)}, u32[]{:S(2)}) copy-start(f32[256]{0:T(256)S(1)} %fusion.171) | copy-start | bytes 3076
  430.7 198.2 %copy-start.131 = (f32[256]{0:T(256)}, f32[256]{0:T(256)S(1)}, u32[]{:S(2)}) copy-start(f32[256]{0:T(256)S(1)} %fusion.167) | copy-start | bytes 3076
  518.3 110.5 %copy-start.165 = (f32[2048]{0:T(1024)S(1)}, f32[2048]{0:T(1024)}, u32[]{:S(2)}) copy-start(f32[2048]{0:T(1024)} %param.31) | copy-start | bytes 24580
  518.4 152.8 %all-gather.41.cloned.1.call-start = ((), (), s32[]{:S(2)}) async-start(), calls=%async_computation.27 | async-start | bytes 1179648 | tf_op jit(solution)/shard_map/all_gather | solution.py:92
  632.9 278.6 %copy-start.138 = (f32[256]{0:T(256)}, f32[256]{0:T(256)S(1)}, u32[]{:S(2)}) copy-start(f32[256]{0:T(256)S(1)} %broadcast_multiply_fusion.6) | copy-start | bytes 3076
  634.1 277.4 %copy-start.169 = (f32[256]{0:T(256)}, f32[256]{0:T(256)S(1)}, u32[]{:S(2)}) copy-start(f32[256]{0:T(256)S(1)} %fusion.168) | copy-start | bytes 3076
  634.1 277.4 %copy-start.140 = (f32[256]{0:T(256)}, f32[256]{0:T(256)S(1)}, u32[]{:S(2)}) copy-start(f32[256]{0:T(256)S(1)} %broadcast_multiply_fusion.2) | copy-start | bytes 3076
  634.8 276.7 %copy-start.171 = (f32[256]{0:T(256)}, f32[256]{0:T(256)S(1)}, u32[]{:S(2)}) copy-start(f32[256]{0:T(256)S(1)} %fusion.172) | copy-start | bytes 3076
  638.7 72.5 %all-gather.33.cloned.1.call-start = ((), (), s32[]{:S(2)}) async-start(), calls=%async_computation.23 | async-start | bytes 1179648 | tf_op jit(solution)/shard_map/all_gather | solution.py:92
  641.4 109.8 %all-gather.39.cloned.1.call-start = ((), (), s32[]{:S(2)}) async-start(), calls=%async_computation.26 | async-start | bytes 1179648 | tf_op jit(solution)/shard_map/all_gather | solution.py:93
  644.1 147.1 %all-gather.31.cloned.1.call-start = ((), (), s32[]{:S(2)}) async-start(), calls=%async_computation.22 | async-start | bytes 1179648 | tf_op jit(solution)/shard_map/all_gather | solution.py:93
  646.8 264.7 %all-reduce.28.cloned.1.call-start = ((), (), s32[]{:S(2)}) async-start(), calls=%async_computation.47 | async-start | bytes 8388608 | tf_op jit(solution)/shard_map/psum | solution.py:105
  649.4 101.8 %copy-start.106 = (bf16[256,256]{0,1:T(8,128)(2,1)}, bf16[256,256]{0,1:T(8,128)(2,1)S(1)}, u32[]{:S(2)}) copy-start(bf16[256,256]{0,1:T(8,128)(2,1)S(1)} %fusion.56) | copy-start | bytes 393220
  796.9 242.1 %all-reduce.26.cloned.1.call-start = ((), (), s32[]{:S(2)}) async-start(), calls=%async_computation.46 | async-start | bytes 8388608 | tf_op jit(solution)/shard_map/psum | solution.py:111
  916.2 265.2 %copy-start.127 = (f32[256]{0:T(256)}, f32[256]{0:T(256)S(1)}, u32[]{:S(2)}) copy-start(f32[256]{0:T(256)S(1)} %broadcast_multiply_fusion.1) | copy-start | bytes 3076
  916.6 264.8 %copy-start.134 = (f32[256]{0:T(256)}, f32[256]{0:T(256)S(1)}, u32[]{:S(2)}) copy-start(f32[256]{0:T(256)S(1)} %fusion.173) | copy-start | bytes 3076
  916.7 264.8 %copy-start.125 = (f32[256]{0:T(256)}, f32[256]{0:T(256)S(1)}, u32[]{:S(2)}) copy-start(f32[256]{0:T(256)S(1)} %broadcast_multiply_fusion.5) | copy-start | bytes 3076
  919.9 261.5 %copy-start.136 = (f32[256]{0:T(256)}, f32[256]{0:T(256)S(1)}, u32[]{:S(2)}) copy-start(f32[256]{0:T(256)S(1)} %fusion.169) | copy-start | bytes 3076
  930.2 244.8 %all-reduce.24.cloned.1.call-start = ((), (), s32[]{:S(2)}) async-start(), calls=%async_computation.45 | async-start | bytes 8388608 | tf_op jit(solution)/shard_map/psum | solution.py:167
  1065.8 162.8 %reduce-scatter.23.cloned.1.call-start = ((), (), s32[]{:S(2)}) async-start(), calls=%async_computation.32 | async-start | bytes 2359296 | tf_op jit(solution)/shard_map/reduce_scatter | solution.py:206
  1192.4 79.9 %reduce-scatter.25.cloned.1.call-start = ((), (), s32[]{:S(2)}) async-start(), calls=%async_computation.33 | async-start | bytes 2359296 | tf_op jit(solution)/shard_map/reduce_scatter | solution.py:207
  1197.2 118.8 %reduce-scatter.15.cloned.1.call-start = ((), (), s32[]{:S(2)}) async-start(), calls=%async_computation.28 | async-start | bytes 2359296 | tf_op jit(solution)/shard_map/reduce_scatter | solution.py:206
  1206.1 153.9 %reduce-scatter.17.cloned.1.call-start = ((), (), s32[]{:S(2)}) async-start(), calls=%async_computation.29 | async-start | bytes 2359296 | tf_op jit(solution)/shard_map/reduce_scatter | solution.py:207
  1210.9 267.3 %all-reduce.22.cloned.1.call-start = ((), (), s32[]{:S(2)}) async-start(), calls=%async_computation.44 | async-start | bytes 8388608 | tf_op jit(solution)/shard_map/psum | solution.py:221
  1363.9 114.3 %copy-start.139 = (f32[256]{0:T(256)S(1)}, f32[256]{0:T(256)}, u32[]{:S(2)}) copy-start(f32[256]{0:T(256)} %copy-done.138) | copy-start | bytes 3076
  1363.9 114.3 %copy-start.141 = (f32[256]{0:T(256)S(1)}, f32[256]{0:T(256)}, u32[]{:S(2)}) copy-start(f32[256]{0:T(256)} %copy-done.140) | copy-start | bytes 3076
  1363.9 114.3 %copy-start.170 = (f32[256]{0:T(256)S(1)}, f32[256]{0:T(256)}, u32[]{:S(2)}) copy-start(f32[256]{0:T(256)} %copy-done.169) | copy-start | bytes 3076
  1363.9 114.3 %copy-start.172 = (f32[256]{0:T(256)S(1)}, f32[256]{0:T(256)}, u32[]{:S(2)}) copy-start(f32[256]{0:T(256)} %copy-done.171) | copy-start | bytes 3076
  1363.9 114.3 %copy-start.183 = (f32[256]{0:T(256)S(1)}, f32[256]{0:T(256)}, u32[]{:S(2)}) copy-start(f32[256]{0:T(256)} %copy-done.182) | copy-start | bytes 3076
  1363.9 114.3 %copy-start.185 = (f32[256]{0:T(256)S(1)}, f32[256]{0:T(256)}, u32[]{:S(2)}) copy-start(f32[256]{0:T(256)} %copy-done.184) | copy-start | bytes 3076
  1363.9 247.5 %all-reduce.20.cloned.1.call-start = ((), (), s32[]{:S(2)}) async-start(), calls=%async_computation.43 | async-start | bytes 8388608 | tf_op jit(solution)/shard_map/psum | solution.py:167
  1502.3 109.1 %copy-start.124 = (f32[256]{0:T(256)S(1)}, f32[256]{0:T(256)}, u32[]{:S(2)}) copy-start(f32[256]{0:T(256)} %copy-done.123) | copy-start | bytes 3076
  1502.3 109.1 %copy-start.130 = (f32[256]{0:T(256)S(1)}, f32[256]{0:T(256)}, u32[]{:S(2)}) copy-start(f32[256]{0:T(256)} %copy-done.129) | copy-start | bytes 3076
  1502.3 109.1 %copy-start.132 = (f32[256]{0:T(256)S(1)}, f32[256]{0:T(256)}, u32[]{:S(2)}) copy-start(f32[256]{0:T(256)} %copy-done.131) | copy-start | bytes 3076
  1502.3 109.1 %copy-start.167 = (f32[256]{0:T(256)S(1)}, f32[256]{0:T(256)}, u32[]{:S(2)}) copy-start(f32[256]{0:T(256)} %copy-done.166) | copy-start | bytes 3076
  1502.4 162.8 %reduce-scatter.27.cloned.1.call-start = ((), (), s32[]{:S(2)}) async-start(), calls=%async_computation.34 | async-start | bytes 2359296 | tf_op jit(solution)/shard_map/reduce_scatter | solution.py:206
  1628.9 79.7 %reduce-scatter.29.cloned.1.call-start = ((), (), s32[]{:S(2)}) async-start(), calls=%async_computation.35 | async-start | bytes 2359296 | tf_op jit(solution)/shard_map/reduce_scatter | solution.py:207
  1633.8 118.4 %reduce-scatter.19.cloned.1.call-start = ((), (), s32[]{:S(2)}) async-start(), calls=%async_computation.30 | async-start | bytes 2359296 | tf_op jit(solution)/shard_map/reduce_scatter | solution.py:206
  1642.3 153.6 %reduce-scatter.21.cloned.1.call-start = ((), (), s32[]{:S(2)}) async-start(), calls=%async_computation.31 | async-start | bytes 2359296 | tf_op jit(solution)/shard_map/reduce_scatter | solution.py:207
  1648.0 293.9 %all-reduce.18.cloned.1.call-start = ((), (), s32[]{:S(2)}) async-start(), calls=%async_computation.42 | async-start | bytes 8388608 | tf_op jit(solution)/shard_map/psum | solution.py:221
  1799.7 183.6 %reduce-scatter.31.cloned.1.call-start = ((), (), s32[]{:S(2)}) async-start(), calls=%async_computation.36 | async-start | bytes 2228224 | tf_op jit(solution)/shard_map/reduce_scatter | solution.py:318
  1805.7 251.0 %reduce-scatter.37.cloned.1.call-start = ((), (), s32[]{:S(2)}) async-start(), calls=%async_computation.39 | async-start | bytes 2228224 | tf_op jit(solution)/shard_map/reduce_scatter | solution.py:321
  1812.6 316.5 %reduce-scatter.33.cloned.1.call-start = ((), (), s32[]{:S(2)}) async-start(), calls=%async_computation.37 | async-start | bytes 2228224 | tf_op jit(solution)/shard_map/reduce_scatter | solution.py:319
  1819.8 382.4 %reduce-scatter.35.cloned.1.call-start = ((), (), s32[]{:S(2)}) async-start(), calls=%async_computation.38 | async-start | bytes 2228224 | tf_op jit(solution)/shard_map/reduce_scatter | solution.py:320
  1827.2 478.5 %reduce-scatter.39.cloned.1.call-start = ((), (), s32[]{:S(2)}) async-start(), calls=%async_computation.40 | async-start | bytes 8912896 | tf_op jit(solution)/shard_map/reduce_scatter | solution.py:322
  1852.6 552.8 %reduce-scatter.41.cloned.1.call-start = ((), (), s32[]{:S(2)}) async-start(), calls=%async_computation.41 | async-start | bytes 8912896 | tf_op jit(solution)/shard_map/reduce_scatter | solution.py:323
  (196 other events, 1306.4 us)
Sparse Core Ops, SparseCore 0:
  9.7 36.0 all-gather.20
  47.5 32.4 all-gather.14
  81.8 32.4 all-gather.18
  116.4 33.4 all-gather.36
  152.0 37.9 all-gather.22
  192.0 37.9 all-gather.34
  231.6 38.4 all-gather.24
  272.3 33.5 all-gather.16
  311.3 114.4 all-reduce.31
  427.4 36.1 all-gather.26
  465.2 44.9 all-gather.28
  518.5 110.3 all-reduce.29
  638.8 32.2 all-gather.40
  673.2 37.9 all-gather.32
  713.2 37.9 all-gather.38
  753.3 37.9 all-gather.30
  797.1 114.4 all-reduce.27
  930.3 108.7 all-reduce.25
  1066.0 108.9 all-reduce.23
  1192.5 36.0 reduce-scatter.22
  1231.0 41.1 reduce-scatter.24
  1274.7 41.2 reduce-scatter.14
  1318.4 41.5 reduce-scatter.16
  1364.0 114.0 all-reduce.21
  1502.5 108.8 all-reduce.19
  1629.0 36.0 reduce-scatter.26
  1667.4 41.1 reduce-scatter.28
  1711.0 41.1 reduce-scatter.18
  1754.6 41.1 reduce-scatter.20
  1799.8 114.7 all-reduce.17
  1917.6 65.6 reduce-scatter.30
  1986.3 70.3 reduce-scatter.36
  2059.4 69.6 reduce-scatter.32
  2132.1 70.0 reduce-scatter.34
  2205.2 100.4 reduce-scatter.38
  2308.5 96.7 reduce-scatter.40
where the time goes:
time: 2420 us; the launch traced here: 2410 us
  waiting for transfers between devices  1950 us (81%)
  matrix products  251 us (10%)
  other arithmetic  76.7 us (3%)
  blocking collectives  64.3 us (3%)
  local copies, waits for them, and re-layouts  47.4 us (2%)
    psum x2, waiting for transfers between devices, layer_forward(): lax.psum(jnp.dot(attended_low, out_weight, preferred_element_type=jnp.flo...  227 us
    psum x2, waiting for transfers between devices, layer_forward(): lax.psum(jnp.dot(active, down_weight, preferred_element_type=jnp.float32)...  219 us
    psum x2, waiting for transfers between devices, layer_backward(): lax.psum(jnp.dot(grad_up, up_weight.T, preferred_element_type=jnp.float32...  218 us
    reduce_scatter x4, waiting for transfers between devices, layer_backward(): lax.psum_scatter(value_terms, 'seq', scatter_dimension=0, tiled=True)  160 us
    all_gather x4, waiting for transfers between devices, layer_forward(): lax.all_gather(key_rows, 'seq', axis=0, tiled=True)  131 us
    all_gather x4, waiting for transfers between devices, layer_forward(): lax.all_gather(value_rows, 'seq', axis=0, tiled=True)  125 us
    psum x2, waiting for transfers between devices, layer_backward(): input_terms = lax.psum(row_terms(pairs), 'mp')  114 us
    reduce_scatter x1, waiting for transfers between devices, shards(): lax.psum_scatter(matrix_totals[4], ('batch', 'seq'), scatter_dimension=0,...  104 us
  transfers between devices with their start and end apart: 36, of which 35 were waited for; matrix products, arithmetic and copies ran while one was open for 9% of the time, Pallas kernels for 0%

commit v1 on v0

v1 whole, which is shorter than its diff:
```python
import functools

import jax
import jax.numpy as jnp
from jax import lax
from jax.experimental import pallas as pl
from jax.experimental.pallas import tpu as pltpu
from jax.sharding import Mesh, PartitionSpec as P

AXES = ("core", "ylo", "x", "yhi", "z")
Y = ("ylo", "yhi")
D = 2048
HD = 128
TOK = 256
OWN = 64
REACH = 512
LOW = jnp.bfloat16
F32 = jnp.float32
BLOCKED = -1e30
SCALE = HD ** (-0.5)
LOG2E = 1.4426950408889634
EPSILON = 1e-05
CURVE = 0.7978845608028654
CUBIC = 0.044715


def limit(mib):
    return pltpu.CompilerParams(vmem_limit_bytes=mib * 2**20)


def shape(dims, dtype=LOW):
    return jax.ShapeDtypeStruct(dims, dtype)


def whole(dims):
    return pl.BlockSpec(dims, lambda *_: (0,) * len(dims))


def dot_t(a, b, ca=1, cb=0):
    return lax.dot_general(a, b, (((ca,), (cb,)), ((), ())), preferred_element_type=F32)


def pack_heads_body(q, k, v, o, out):
    for j in range(2):
        at = slice(128 * j, 128 * j + 128)
        for t, part in enumerate((q, k, v)):
            out[:, 384 * j + 128 * t : 384 * j + 128 * t + 128] = part[:, at]
    out[:, 768:] = o[...].T


def pair_heads_body(own, far, out):
    for j in range(2):
        for h, part in enumerate((own, far)):
            slot = 2 * j + h
            out[:, 384 * slot : 384 * slot + 384] = part[:, 384 * j : 384 * j + 384]
            out[:, 1536 + 128 * slot : 1664 + 128 * slot] = part[:, 768 + 128 * j : 896 + 128 * j]


def turn_body(down, out):
    out[...] = down[...].T


def pair_body(own, far, out):
    n = own.shape[1]
    out[:, :n] = own[...]
    out[:, n:] = far[...]


def pack(body, width, *parts):
    return pl.pallas_call(
        body,
        out_shape=shape((128, width)),
        cost_estimate=pl.CostEstimate(flops=0, bytes_accessed=512 * width, transcendentals=0),
        name="pack",
    )(*parts)


def settle_body(spot, p0, p1, p2, p3, out):
    for d, part in enumerate((p0, p1, p2, p3)):
        at = pl.ds(pl.multiple_of((d ^ spot[3]) * OWN, OWN), OWN)
        if len(out.shape) == 2:
            out[at] = part[...]
        else:
            out[:, at] = part[...]


def settle(spot, parts):
    dims = parts[0].shape[:-2] + (TOK, D)
    return pl.pallas_call(
        settle_body,
        in_specs=[pl.BlockSpec(memory_space=pltpu.SMEM)] + [pl.BlockSpec(memory_space=pltpu.VMEM)] * 4,
        out_specs=pl.BlockSpec(memory_space=pltpu.VMEM),
        out_shape=shape(dims),
        cost_estimate=pl.CostEstimate(flops=0, bytes_accessed=2**22, transcendentals=0),
        name="settle",
    )(spot, *parts)


def rows_body(kind, spot, p0, p1, p2, p3, w, *refs):
    step = pl.program_id(0)
    kept = pl.multiple_of(spot[1] * (D // 2), D // 2)
    sent = pl.multiple_of((1 - spot[1]) * (D // 2), D // 2)
    extra = refs[0] if kind in ("qkv", "up", "slope") else None
    keep, send = refs[1:3] if extra is not None else refs[:2]
    outs = refs[3:] if extra is not None else refs[2:]

    @pl.when(step == 0)
    def _():
        for i, p in enumerate((p0, p1, p2, p3)):
            keep[OWN * i : OWN * i + OWN] = p[:, pl.ds(kept, D // 2)]
            send[OWN * i : OWN * i + OWN] = p[:, pl.ds(sent, D // 2)]

    values = dot_t(keep[...], w[pl.ds(kept, D // 2)]) + dot_t(send[...], w[pl.ds(sent, D // 2)])
    if kind == "qkv":
        values = values + extra[...]
    if kind in ("qkv", "heads"):
        low = values.astype(LOW)
        for d in range(4):

            @pl.when(step == d)
            def _():
                outs[d][...] = low
    elif kind == "up":
        values = values + extra[...]
        square = values * values
        bend = jnp.tanh(CURVE * (values + CUBIC * (square * values)))
        outs[0][...] = (0.5 * values * (1.0 + bend)).astype(LOW)
        slope = 0.5 * (1.0 + bend) + 0.5 * values * (1.0 - bend * bend) * (CURVE * (1.0 + 3.0 * CUBIC * square))
        outs[1][...] = slope.astype(LOW)
    else:
        low = (values * extra[...].astype(F32)).astype(LOW)
        outs[0][...] = low
        outs[1][...] = jnp.sum(low.astype(F32), axis=0, keepdims=True)


def rows_mm(kind, spot, pieces, weight, n, first, extra=None):
    tile = n // 4
    by_slot = kind in ("qkv", "heads")

    def column(i, spot):
        return (0, i ^ spot[0]) if by_slot else (0, i)

    def weight_column(i, spot):
        return (0, first // tile + column(i, spot)[1])

    in_specs = [whole((OWN, D))] * 4 + [pl.BlockSpec((D, tile), weight_column)]
    args = list(pieces) + [weight]
    if extra is not None:
        in_specs.append(pl.BlockSpec((extra.shape[0], tile), column))
        args.append(extra)
    half = shape((TOK, D // 2))
    if by_slot:
        outs = [half, half] + [shape((TOK, tile))] * 4
        out_specs = [whole((TOK, D // 2))] * 2 + [whole((TOK, tile))] * 4
    else:
        outs = [half, half, shape((TOK, n)), shape((TOK, n)) if kind == "up" else shape((1, n), F32)]
        block = pl.BlockSpec((TOK, tile), column)
        out_specs = [whole((TOK, D // 2))] * 2 + [block, block if kind == "up" else pl.BlockSpec((1, tile), column)]
    return pl.pallas_call(
        functools.partial(rows_body, kind),
        grid_spec=pltpu.PrefetchScalarGridSpec(num_scalar_prefetch=1, grid=(4,), in_specs=in_specs, out_specs=out_specs),
        out_shape=outs,
        compiler_params=limit(28),
        cost_estimate=pl.CostEstimate(flops=2 * TOK * D * n, bytes_accessed=2 * D * n + 8 * TOK * D, transcendentals=TOK * n),
        name="rows_" + kind,
    )(spot, *args)


def split_rows(values, outs, to):
    outs[0][:, to] = values[:OWN]
    for i in range(1, 4):
        outs[i][:, to] = values[OWN * i : OWN * i + OWN].astype(LOW)


def scatter_body(n_parts, spot, *refs):
    parts, w = refs[:n_parts], refs[n_parts]
    outs = refs[n_parts + 1 : n_parts + 5]
    if n_parts == 1:
        rows = parts[0]
    else:
        rows, sums = refs[n_parts + 5], refs[n_parts + 6]

        @pl.when(pl.program_id(0) == 0)
        def _():
            width = parts[0].shape[1]
            for d, part in enumerate(parts):
                at = pl.ds(pl.multiple_of((d ^ spot[0]) * width, 128), width)
                rows[:, at] = part[...]
                sums[:, at] = jnp.sum(part[...].astype(F32), axis=0, keepdims=True)

    split_rows(dot_t(rows[...], w[...], 1, 1), outs, slice(None))


def scatter_mm(spot, parts, weight, k, first):
    tile = 512
    in_specs = [whole(p.shape) for p in parts] + [pl.BlockSpec((tile, k), lambda i, spot: (i, first // k))]
    block = pl.BlockSpec((OWN, tile), lambda i, spot: (0, i))
    outs = [shape((OWN, D), F32)] + [shape((OWN, D))] * 3
    out_specs = [block] * 4
    if len(parts) > 1:
        outs += [shape((TOK, k)), shape((1, k), F32)]
        out_specs += [whole((TOK, k)), whole((1, k))]
    return pl.pallas_call(
        functools.partial(scatter_body, len(parts)),
        grid_spec=pltpu.PrefetchScalarGridSpec(
            num_scalar_prefetch=1, grid=(D // tile,), in_specs=in_specs, out_specs=out_specs
        ),
        out_shape=outs,
        compiler_params=limit(28),
        cost_estimate=pl.CostEstimate(flops=2 * TOK * D * k, bytes_accessed=2 * D * k + 4 * TOK * D, transcendentals=0),
        name="scatter_mm",
    )(spot, *parts, weight)


def term_body(groups, *refs):
    lefts = [refs[8 * g : 8 * g + 4] for g in range(groups)]
    rights = [refs[8 * g + 4 : 8 * g + 8] for g in range(groups)]
    out, turned = refs[8 * groups], refs[8 * groups + 1 :]
    step = pl.program_id(0)

    @pl.when(step == 0)
    def _():
        for g in range(groups):
            for i in range(4):
                turned[g][:, TOK * i : TOK * i + TOK] = lefts[g][i][...].T

    parts = []
    for g in range(groups):
        total = None
        for i in range(4):
            part = dot_t(turned[g][:, TOK * i : TOK * i + TOK], rights[g][i][...])
            total = part if total is None else total + part
        parts.append(total.astype(LOW))
    if groups == 1:
        out[...] = parts[0]
        return
    widths = [part.shape[1] for part in parts]
    for slot in range(4):

        @pl.when(step == slot)
        def _():
            first = (slot & 1) * 2 * sum(widths)
            for part, width in zip(parts, widths):
                at = first + (slot >> 1) * width
                out[:, at : at + width] = part
                first += 2 * width


def weight_terms(groups):
    widths = [rights[0].shape[1] // 4 for _, rights in groups]
    n = sum(widths)
    in_specs, args = [], []
    for (lefts, rights), width in zip(groups, widths):
        in_specs += [whole((TOK, 1024))] * 4 + [pl.BlockSpec((TOK, width), lambda i: (0, i))] * 4
        args += list(lefts) + list(rights)
    return pl.pallas_call(
        functools.partial(term_body, len(groups)),
        grid=(4,),
        in_specs=in_specs,
        out_specs=pl.BlockSpec((1024, n), lambda i: (0, i)) if len(groups) == 1 else whole((1024, 4 * n)),
        out_shape=shape((1024, 4 * n)),
        scratch_shapes=[pltpu.VMEM((1024, 1024), LOW)] * len(groups),
        compiler_params=limit(32),
        cost_estimate=pl.CostEstimate(flops=8 * 1024 * 1024 * n, bytes_accessed=8 * 1024 * n + 2**23, transcendentals=0),
        name="weight_terms",
    )(*args)


def near(marks, keys, windowed):
    return jnp.abs(marks - keys) <= (REACH if windowed else 2047.0)


def load_heads(pieces, queries, keys, values):
    for i, piece in enumerate(pieces):
        at = slice(TOK * i, TOK * i + TOK)
        if i < 4:
            queries[at] = piece[:, :HD]
        keys[at] = piece[:, HD : 2 * HD]
        values[at] = piece[:, 2 * HD :]


def fwd_body(windowed, *refs):
    pieces, qmark, kmark = refs[:8], refs[8], refs[9]
    outs, lse, queries, keys, values = refs[10:14], *refs[14:]
    step = pl.program_id(0)

    @pl.when(step == 0)
    def _():
        load_heads(pieces, queries, keys, values)

    query = queries[pl.ds(pl.multiple_of(step * TOK, TOK), TOK)]
    s = dot_t(keys[...], query, 1, 1)
    s = jnp.where(near(qmark[...], kmark[...], windowed), s, BLOCKED)
    top = jnp.max(s, axis=0, keepdims=True)
    p = jnp.exp2((s - top) * (SCALE * LOG2E))
    total = jnp.sum(p, axis=0, keepdims=True)
    mixed = (dot_t(values[...], p.astype(LOW), 0, 0) / total).T.astype(LOW)
    for d in range(4):

        @pl.when(step == d)
        def _():
            outs[d][...] = mixed

    lse[...] = top * (SCALE * LOG2E) + jnp.log2(total)


def mark_specs():
    return [pl.BlockSpec((1, TOK), lambda i: (0, i)), whole((8 * TOK, 1))]


def attend_fwd(pieces, mark, windowed):
    n = 4 * TOK
    *mixed, lse = pl.pallas_call(
        functools.partial(fwd_body, windowed),
        grid=(4,),
        in_specs=[whole((TOK, 3 * HD))] * 8 + mark_specs(),
        out_specs=[whole((TOK, HD))] * 4 + [pl.BlockSpec((1, TOK), lambda i: (0, i))],
        out_shape=[shape((TOK, HD))] * 4 + [shape((1, n), F32)],
        scratch_shapes=[pltpu.VMEM((n, HD), LOW), pltpu.VMEM((2 * n, HD), LOW), pltpu.VMEM((2 * n, HD), LOW)],
        compiler_params=limit(24),
        cost_estimate=pl.CostEstimate(flops=8 * n * n * HD, bytes_accessed=2**22, transcendentals=2 * n * n),
        name="attend_fwd",
    )(*pieces, *mark)
    return mixed, lse


def bwd_body(windowed, *refs):
    pieces, grads, outs, lse, qmark, kmark = refs[:8], refs[8:12], refs[12:16], *refs[16:19]
    dq, own, far, queries, keys, values, g_all, o_all, acc = refs[19:23], *refs[23:]
    step = pl.program_id(0)
    n = 4 * TOK

    @pl.when(step == 0)
    def _():
        load_heads(pieces, queries, keys, values)
        for i in range(4):
            g_all[TOK * i : TOK * i + TOK] = grads[i][...]
            o_all[TOK * i : TOK * i + TOK] = outs[i][...]
        acc[...] = jnp.zeros_like(acc)

    at = pl.ds(pl.multiple_of(step * TOK, TOK), TOK)
    query, grad, out = queries[at], g_all[at], o_all[at]
    dots = jnp.sum((grad.astype(F32) * out.astype(F32)).T, axis=0, keepdims=True)
    s = dot_t(keys[...], query, 1, 1)
    s = jnp.where(near(qmark[...], kmark[...], windowed), s, BLOCKED)
    p = jnp.exp2(s * (SCALE * LOG2E) - lse[...])
    ds = (p * (dot_t(values[...], grad, 1, 1) - dots)).astype(LOW)
    acc[:, :HD] += dot_t(ds, query)
    acc[:, HD:] += dot_t(p.astype(LOW), grad)
    turned = (dot_t(keys[...], ds, 0, 0) * SCALE).T.astype(LOW)
    for d in range(4):

        @pl.when(step == d)
        def _():
            dq[d][...] = turned

    @pl.when(step == 3)
    def _():
        for ref, start in ((own, 0), (far, n)):
            ref[:, :HD] = acc[start : start + n, :HD] * SCALE
            ref[:, HD:] = acc[start : start + n, HD:]


def attend_bwd(pieces, grads, mixed, lse, mark, windowed):
    n = 4 * TOK
    *dq, own, far = pl.pallas_call(
        functools.partial(bwd_body, windowed),
        grid=(4,),
        in_specs=[whole((TOK, 3 * HD))] * 8
        + [whole((TOK, HD))] * 8
        + [pl.BlockSpec((1, TOK), lambda i: (0, i))]
        + mark_specs(),
        out_specs=[whole((TOK, HD))] * 4 + [whole((n, 2 * HD))] * 2,
        out_shape=[shape((TOK, HD))] * 4 + [shape((n, 2 * HD), F32)] * 2,
        scratch_shapes=[pltpu.VMEM((n, HD), LOW), pltpu.VMEM((2 * n, HD), LOW), pltpu.VMEM((2 * n, HD), LOW)]
        + [pltpu.VMEM((n, HD), LOW)] * 2
        + [pltpu.VMEM((2 * n, 2 * HD), F32)],
        compiler_params=limit(36),
        cost_estimate=pl.CostEstimate(flops=20 * n * n * HD, bytes_accessed=2**23, transcendentals=2 * n * n),
        name="attend_bwd",
    )(*pieces, *grads, *mixed, lse, *mark)
    return dq, own, far


def join_body(*refs):
    dq, own, far, outs = refs[:4], refs[4], refs[5], refs[6:]
    for d in range(4):
        at = slice(TOK * d, TOK * d + TOK)
        outs[d][:, :HD] = dq[d][...]
        outs[d][:, HD:] = (own[at] + far[at]).astype(LOW)


def join_heads(dq, own, far):
    return pl.pallas_call(
        join_body,
        out_shape=[shape((TOK, 3 * HD))] * 4,
        compiler_params=limit(16),
        cost_estimate=pl.CostEstimate(flops=2**18, bytes_accessed=2**22, transcendentals=0),
        name="join_heads",
    )(*dq, own, far)


def swap(values, axis, bits, size=4):
    if axis == Y:
        bits = (bits & 1) * 2 + (bits >> 1)
    return lax.ppermute(values, axis, [(i, i ^ bits) for i in range(size)])


def sibling(values):
    return swap(values, "core", 1, 2)


def exchange(pieces, axis):
    got = {d: swap(pieces[d], axis, d) for d in (2, 1, 3)}
    return [pieces[0], got[1], got[2], got[3]]


def gather(piece, axis):
    return exchange([piece] * 4, axis)


def four_sum(parts):
    return (parts[0].astype(F32) + parts[2].astype(F32)) + (parts[1].astype(F32) + parts[3].astype(F32))


def tie(*values):
    return lax.optimization_barrier(values)


def pick(stacked, index):
    return lax.dynamic_index_in_dim(stacked, index, 0, keepdims=False)


def norm(values):
    center = jnp.mean(values, axis=-1, keepdims=True)
    centered = values - center
    spread = jnp.mean(centered * centered, axis=-1, keepdims=True)
    scale = lax.rsqrt(spread + EPSILON)
    return centered * scale, scale


def norm_back(grad, normed, scale, gain):
    terms = jnp.sum(grad * normed, axis=0), jnp.sum(grad, axis=0)
    tilted = grad * gain
    back = tilted - jnp.mean(tilted, axis=-1, keepdims=True)
    back = (back - normed * jnp.mean(tilted * normed, axis=-1, keepdims=True)) * scale
    return back, terms


def line_sum(values, axis):
    return four_sum(gather(values, axis))


def layer_forward(spot, stream, pieces, matrices, vectors, mark, windowed):
    heads_matrix, up_matrix, down_matrix = matrices
    qkv_bias, up_bias, out_bias, down_bias, attn_gain, attn_shift, ffn_gain, ffn_shift = vectors
    rows_keep, rows_send, *heads = rows_mm("qkv", spot, pieces, heads_matrix, 1536, 0, qkv_bias)
    heads = exchange(heads, "x")
    heads = heads + [sibling(h) for h in heads]
    mixed, lse = attend_fwd(heads, mark, windowed)
    *branch, attended, _ = scatter_mm(spot, exchange(mixed, "x"), heads_matrix, 512, 1536)
    normed, scale = norm(stream + four_sum(exchange(branch, "z")) + out_bias)
    first = normed * attn_gain + attn_shift
    first_keep, first_send, active, slope = rows_mm("up", spot, gather(first.astype(LOW), "z"), up_matrix, 2048, 0, up_bias)
    second = four_sum(exchange(scatter_mm(spot, [active], down_matrix, 2048, 0), "z"))
    normed_two, scale_two = norm(first + second + down_bias)
    result = normed_two * ffn_gain + ffn_shift
    saved = (heads, mixed, lse, normed, scale, slope, normed_two, scale_two)
    halves = [(rows_keep, sibling(rows_send)), (first_keep, sibling(first_send))]
    units = [(attended, sibling(attended)), (active, sibling(active))]
    return result, saved, halves, units


def layer_backward(spot, grad, saved, halves, units, matrices, vectors, mark, windowed, earlier=None):
    heads_matrix, up_matrix, down_matrix = matrices
    qkv_bias, up_bias, out_bias, down_bias, attn_gain, attn_shift, ffn_gain, ffn_shift = vectors
    heads, mixed, lse, normed, scale, slope, normed_two, scale_two = saved
    last = earlier is not None
    grad_summed, ffn_terms = norm_back(grad, normed_two, scale_two, ffn_gain)
    second_own = grad_summed.astype(LOW)
    second_keep, second_send, grad_up, up_sums = rows_mm("slope", spot, gather(second_own, "z"), down_matrix, 2048, 0, slope)
    down_pair = ((second_keep, sibling(second_send)), units[1])
    up_pair = (halves[1], (grad_up, sibling(grad_up)))
    partial = scatter_mm(spot, [grad_up], up_matrix, 2048, 0)
    if last:
        down_term = weight_terms([join_pairs(down_pair, earlier[3])])
        own_part, down_term = tie(partial[0], down_term)
        partial = [own_part, *partial[1:]]
        down_sum = lax.psum_scatter(down_term, ("ylo", "x"), scatter_dimension=0, tiled=True)
    grad_first = four_sum(exchange(partial, "z")) + grad_summed
    grad_residual, attn_terms = norm_back(grad_first, normed, scale, attn_gain)
    branch_own = grad_residual.astype(LOW)
    if last:
        up_term = weight_terms([join_pairs(up_pair, earlier[2])])
        branch_own, up_term = tie(branch_own, up_term)
        up_sum = lax.psum_scatter(up_term, ("ylo", "x"), scatter_dimension=0, tiled=True)
    branch_keep, branch_send, *grad_heads = rows_mm("heads", spot, gather(branch_own, "z"), heads_matrix, 512, 1536)
    out_pair = ((branch_keep, sibling(branch_send)), units[0])
    grad_queries, own_terms, far_terms = attend_bwd(heads, exchange(grad_heads, "x"), mixed, lse, mark, windowed)
    grad_parts = exchange(join_heads(grad_queries, own_terms, sibling(far_terms)), "x")
    *partial, grad_packed, head_sums = scatter_mm(spot, grad_parts, heads_matrix, 1536, 0)
    qkv_pair = (halves[0], (grad_packed, sibling(grad_packed)))
    own_sums = (
        jnp.sum(branch_own.astype(F32), axis=0),
        jnp.sum(second_own.astype(F32), axis=0),
        attn_terms[0],
        attn_terms[1],
        ffn_terms[0],
        ffn_terms[1],
    )
    sums = (jnp.stack(own_sums), head_sums, up_sums)
    if last:
        rest = weight_terms([join_pairs(qkv_pair, earlier[0]), join_pairs(out_pair, earlier[1])])
        own_part, rest, *sums = tie(partial[0], rest, *sums)
        partial = [own_part, *partial[1:]]
        rest = lax.psum_scatter(rest, ("ylo", "x"), scatter_dimension=0, tiled=True)
    grad_stream = four_sum(exchange(partial, "z")) + grad_residual
    if not last:
        return grad_stream, (qkv_pair, out_pair, up_pair, down_pair), sums
    return grad_stream, [add_far(total) for total in (rest, up_sum, down_sum)], sums


def add_far(total):
    n = total.shape[1] // 2
    return total[:, :n].astype(F32) + swap(total[:, n:], "yhi", 1, 2).astype(F32)


def join_pairs(one, two):
    return list(one[0]) + list(two[0]), list(one[1]) + list(two[1])


TURN = [(0, 0), (1, 2), (2, 1), (3, 3)]


def turn_same(values):
    return lax.ppermute(values, ("core", "ylo"), TURN)


def turn_other(values):
    perm = [(c * 4 + l * 2 + h, l * 4 + c * 2 + 1 - h) for c in range(2) for l in range(2) for h in range(2)]
    return lax.ppermute(values, ("core", "ylo", "yhi"), perm)


def by_micro(yhi, same, other):
    return jnp.stack([jnp.where(yhi == 0, same, other), jnp.where(yhi == 0, other, same)])


def absolute_yhi(values, yhi):
    return jnp.where(yhi == 0, values, values[::-1])


def deliver_z_first(yhi, spot, own):
    rows = settle(spot, gather(own, "z"))
    return by_micro(yhi, turn_same(rows), turn_other(rows))[:, None]


def deliver_y_first(yhi, spot, own):
    both = by_micro(yhi, turn_same(own), turn_other(own))
    return settle(spot, gather(both, "z"))[:, None]


def shards(
    inputs,
    cotangent,
    segments,
    query_weight,
    key_weight,
    value_weight,
    out_weight,
    up_weight,
    down_weight,
    query_bias,
    value_bias,
    out_bias,
    up_bias,
    down_bias,
    attn_gain,
    attn_shift,
    ffn_gain,
    ffn_shift,
):
    core, ylo, x, yhi, z = (lax.axis_index(name) for name in AXES)
    spot = jnp.stack([x, core, ylo, z]).astype(jnp.int32)
    local = pack(pack_heads_body, 1024, query_weight, key_weight, value_weight, out_weight)
    local = pack(pair_heads_body, 2048, local, swap(local, "yhi", 1, 2))
    own_rows = pick(pick(inputs, yhi)[0].reshape(4, OWN, D), z)
    own_rows, local = tie(own_rows, local)
    heads_matrix = lax.all_gather(local, ("core", "ylo", "x"), axis=0, tiled=True)
    own_rows = turn_same(own_rows)
    pieces = gather(own_rows, "z")
    *pieces, up_weight, down_weight = tie(*pieces, up_weight, down_weight)
    hidden_matrices = []
    for own in (up_weight, pack(turn_body, 1024, down_weight)):
        local = pack(pair_body, 2048, own, swap(own, "yhi", 1, 2))
        hidden_matrices.append(lax.all_gather(local, ("core", "ylo", "x"), axis=0, tiled=True))
    matrices = (heads_matrix, *hidden_matrices)
    bias_own = jnp.concatenate([query_bias, value_bias, up_bias])
    bias = (bias_own, swap(bias_own, "yhi", 1, 2))
    none = jnp.zeros((128,), F32)
    qkv_bias = jnp.concatenate(
        [
            part
            for j in range(2)
            for h in range(2)
            for part in (bias[h][128 * j : 128 * j + 128], none, bias[h][256 + 128 * j : 384 + 128 * j])
        ]
    )
    up_all = jnp.concatenate([bias[h][512:] for h in range(2)])
    vectors = (qkv_bias[None], up_all[None], out_bias, down_bias, attn_gain, attn_shift, ffn_gain, ffn_shift)
    top_grad = turn_same(pick(pick(cotangent, yhi)[0].reshape(4, OWN, D), z)).astype(F32)
    seg_here = pick(segments, yhi)[0].astype(F32)
    seg_pack = jnp.where(core == ylo, seg_here, sibling(seg_here)).astype(jnp.int32).reshape(2, 4, 4, 64)
    x_order = x ^ jnp.arange(4, dtype=jnp.int32)
    z_order = z ^ jnp.arange(4, dtype=jnp.int32)

    def seg_of(core):
        mine = pick(seg_pack, core)
        mine = jnp.concatenate([pick(mine, x_order[i])[None] for i in range(4)], axis=0)
        return jnp.concatenate([lax.dynamic_slice_in_dim(mine, z_order[i], 1, 1) for i in range(4)], axis=1).reshape(-1)

    def places(core):
        first = (core * 4 + x_order)[:, None, None] * 256 + z_order[None, :, None] * 64
        return (first + jnp.arange(64, dtype=jnp.int32)[None, None, :]).reshape(-1)

    mark = jnp.concatenate([8192 * seg_of(who) + places(who) for who in (core, 1 - core)]).astype(F32)
    mark = (mark[None, :1024], mark[:, None])
    stream = own_rows.astype(F32)
    middle, saved_one, halves_one, units_one = layer_forward(spot, stream, pieces, matrices, vectors, mark, True)
    pieces = gather(middle.astype(LOW), "z")
    final, saved_two, halves_two, units_two = layer_forward(spot, middle, pieces, matrices, vectors, mark, False)
    outputs = deliver_z_first(yhi, spot, final.astype(LOW))
    grad, pairs, sums_two = layer_backward(
        spot, top_grad, saved_two, halves_two, units_two, matrices, vectors, mark, False
    )
    grad, outputs = tie(grad, outputs)
    grad, scattered, sums_one = layer_backward(
        spot, grad, saved_one, halves_one, units_one, matrices, vectors, mark, True, pairs
    )
    input_grad = deliver_y_first(yhi, spot, grad.astype(LOW))
    rest, up_weight_grad, down_turned = scattered
    query_grad, key_grad, value_grad = (
        jnp.concatenate([rest[:, 384 * j + 128 * t : 384 * j + 128 * t + 128] for j in range(2)], axis=1) for t in range(3)
    )
    out_weight_grad = rest[:, 768:].T
    down_weight_grad = down_turned.T
    own_sums, head_sums, hidden_sums = (one + two for one, two in zip(sums_one, sums_two))
    own_sums = line_sum(own_sums, "z").reshape(-1, 128)
    head_sums = jnp.stack([absolute_yhi(head_sums.reshape(2, 2, 3, 128)[j], yhi) for j in range(2)])
    hidden_sums = absolute_yhi(hidden_sums.reshape(2, 1024), yhi)
    sums = jnp.concatenate([own_sums, head_sums.reshape(-1, 128), hidden_sums.reshape(-1, 128)])
    sums = line_sum(line_sum(sums + sibling(sums), "x"), Y).reshape(-1)
    own = sums[: 6 * D].reshape(6, D)
    heads = sums[6 * D : 6 * D + 1536].reshape(2, 2, 3, 128)
    heads = lax.dynamic_index_in_dim(heads, yhi, 1, keepdims=False)
    hidden_all = pick(sums[6 * D + 1536 :].reshape(2, 1024), yhi)
    return (
        outputs,
        input_grad,
        query_grad,
        key_grad,
        value_grad,
        out_weight_grad,
        up_weight_grad,
        down_weight_grad,
        heads[:, 0].reshape(-1),
        heads[:, 2].reshape(-1),
        own[0],
        hidden_all,
        own[1],
        own[2],
        own[3],
        own[4],
        own[5],
    )


def solution(mesh):
    split = Mesh(mesh.devices.reshape(2, 2, 4, 2, 4), AXES)
    token = P(None, "core", ("ylo", "x"), None)
    inner = P(("core", "ylo", "x"), ("yhi", "z"))
    outer = P(("yhi", "z"), ("core", "ylo", "x"))
    unit = P(("yhi", "z"))
    matrix = (inner, inner, inner, outer, inner, outer)
    vector = (unit, unit, P(), unit, P(), P(), P(), P(), P())
    in_specs = (token, token, P(None, "core", None)) + matrix + vector
    out_specs = (token, token) + matrix + vector
    return jax.shard_map(shards, mesh=split, in_specs=in_specs, out_specs=out_specs, check_vma=False)
```

time: 2420 us -> 784 us (0.32)
  waiting for transfers between devices: 1950 us -> 308 us
  matrix products: 251 us -> 0 us
  starting transfers between devices: 4.28 us -> 196 us
  Pallas kernels: 0 us -> 132 us
  blocking collectives: 64.3 us -> 0 us
  other arithmetic: 76.7 us -> 21.2 us
  local copies, waits for them, and re-layouts: 47.4 us -> 79.9 us
    psum x8 -> x0, waiting for transfers between devices: 778 us -> none  [the longest x2 227 us: layer_forward(): lax.psum(jnp.dot(attended_low, out_weight, preferred_element_type=jnp.flo...]
    reduce_scatter x14 -> x3, waiting for transfers between devices: 715 us -> 0.02 us  [the longest x1 0.02 us: layer_backward(): lax.psum_scatter(down_term, ('ylo', 'x'), scatter_dimension=0, tiled=True)]
    all_gather x14 -> x3, waiting for transfers between devices: 454 us -> 12.6 us  [shards(): lax.all_gather(local, ('core', 'ylo', 'x'), axis=0, tiled=True)]
    ppermute x0 -> x128, waiting for transfers between devices: none -> 295 us  [the longest x122 274 us: swap(): return lax.ppermute(values, axis, [(i, i ^ bits) for i in range(size)])]
    dot_general x92 -> x0, matrix products: 234 us -> none  [the longest x12 37.4 us: row_terms(): part_sum = jnp.dot(left, right, preferred_element_type=jnp.float32)]
    ppermute x0 -> x128, starting transfers between devices: none -> 196 us  [the longest x122 175 us: swap(): return lax.ppermute(values, axis, [(i, i ^ bits) for i in range(size)])]
    pallas_call x0 -> x32, Pallas kernels: none -> 132 us  [the longest x8 37.2 us: rows_mm(): pl.pallas_call(functools.partial(rows_body, kind), grid_spec=pltpu.Prefet...]
    psum x1 -> x0, blocking collectives: 64.3 us -> none  [shards(): vector_full = lax.psum(vector_totals, ('batch', 'seq'))]
  transfers between devices with their start and end apart: 36 -> 134, of which waited for: 35 -> 75; matrix products, arithmetic and copies ran while one was open for 9% -> 4% of each run, Pallas kernels for 0% -> 11%
where the time goes in v1:
time: 784 us; the launch traced here: 769 us
  waiting for transfers between devices  308 us (39%)
  starting transfers between devices  196 us (25%)
  Pallas kernels  132 us (17%)
  local copies, waits for them, and re-layouts  79.9 us (10%)
  between operations  32 us (4%)
  other arithmetic  21.2 us (3%)
    ppermute x122, waiting for transfers between devices, swap(): return lax.ppermute(values, axis, [(i, i ^ bits) for i in range(size)])  274 us
    ppermute x122, starting transfers between devices, swap(): return lax.ppermute(values, axis, [(i, i ^ bits) for i in range(size)])  175 us
    unnamed x299, local copies, waits for them, and re-layouts  67.3 us
    pallas_call x8, Pallas kernels, rows_mm(): pl.pallas_call(functools.partial(rows_body, kind), grid_spec=pltpu.Prefet...  37.2 us
    pallas_call x8, Pallas kernels, scatter_mm(): pl.pallas_call(functools.partial(scatter_body, len(parts)), grid_spec=plt...  27.9 us
    pallas_call x3, Pallas kernels, weight_terms(): pl.pallas_call(functools.partial(term_body, len(groups)), grid=(4,), in_s...  23.4 us
    ppermute x4, starting transfers between devices, turn_same(): return lax.ppermute(values, ('core', 'ylo'), TURN)  17.1 us
    pallas_call x2, Pallas kernels, attend_bwd(): pl.pallas_call(functools.partial(bwd_body, windowed), grid=(4,), in_specs...  16.4 us
  transfers between devices with their start and end apart: 134, of which 75 were waited for; matrix products, arithmetic and copies ran while one was open for 4% of the time, Pallas kernels for 11%

profile of v1, /device:TPU:1, one launch (start us, length us, event | category | flops | bytes accessed | tf_op | source)
XLA Modules:
  0.0 768.6 jit_solution(5822499543914417656)
XLA Ops:
  8.9 3.7 collective-permute-start
  21.3 4.7 collective-permute-start.1
  26.0 4.0 collective-permute-done.1.p0
  36.0 5.9 collective-permute-done.3.p2
  47.3 10.9 %collective-permute-done.23.far = bf16[128,1024]{1,0:T(8,128)(2,1)S(1)} collective-permute-done((bf16[128,1024]{1,0:T(8,128)(2,1)S(1)}, bf16[128,1024]{1,0:T(8,128)(2,1)S(1)}, u32[]{:S(2)}, u32[]{:S(2)}) %collective-permute-start.23) | collective-permute-done | bytes 262176 | tf_op jit(solution)/shard_map/ppermute | solution.py:406
  65.3 11.3 %collective-permute-done.24.far = bf16[128,1024]{1,0:T(8,128)(2,1)S(1)} collective-permute-done((bf16[128,1024]{1,0:T(8,128)(2,1)}, bf16[128,1024]{1,0:T(8,128)(2,1)S(1)}, u32[]{:S(2)}, u32[]{:S(2)}) %collective-permute-start.24) | collective-permute-done | bytes 262176 | tf_op jit(solution)/shard_map/ppermute | solution.py:406
  99.4 3.7 copy-done
  103.1 4.9 rows_qkv.2
  109.7 4.0 collective-permute-start.7
  115.0 5.6 collective-permute-done.6.refs_1_
  122.1 9.4 %collective-permute-done.7.refs_2_ = bf16[256,384]{1,0:T(8,128)(2,1)S(1)} collective-permute-done((bf16[256,384]{1,0:T(8,128)(2,1)S(1)}, bf16[256,384]{1,0:T(8,128)(2,1)S(1)}, u32[]{:S(2)}, u32[]{:S(2)}) %collective-permute-start.7) | collective-permute-done | bytes 196640 | tf_op jit(solution)/shard_map/ppermute | solution.py:406
  135.8 5.6 attend_fwd.2
  155.7 3.8 collective-permute-start.17
  159.5 3.8 collective-permute-done.19
  163.2 6.5 collective-permute-done.17
  176.7 5.3 collective-permute-done.21.p2
  182.0 4.3 collective-permute-done.22.p3
  189.8 5.5 rows_up.2
  197.0 12.5 %all-gather.8.cloned.1.call-done.refs_1_.w = bf16[2048,2048]{1,0:T(8,128)(2,1)} async-done(((bf16[128,2048]{1,0:T(8,128)(2,1)}), bf16[2048,2048]{1,0:T(8,128)(2,1)}) %all-gather.8.cloned.1.call-update) | async-done | bytes 8388624 | tf_op jit(solution)/shard_map/all_gather | solution.py:595
  220.6 4.9 collective-permute-done.27
  226.7 5.5 collective-permute-done.25
  239.6 7.8 %collective-permute-done.29.p2 = bf16[64,2048]{1,0:T(8,128)(2,1)S(1)} collective-permute-done((bf16[64,2048]{1,0:T(8,128)(2,1)S(1)}, bf16[64,2048]{1,0:T(8,128)(2,1)S(1)}, u32[]{:S(2)}, u32[]{:S(2)}) %collective-permute-start.29) | collective-permute-done | bytes 262176 | tf_op jit(solution)/shard_map/ppermute | solution.py:406
  253.5 4.9 rows_qkv.3
  276.8 5.6 attend_fwd.3
  291.9 3.7 collective-permute-start.42
  299.0 6.5 collective-permute-done.42
  311.6 4.9 collective-permute-done.46.p2
  316.5 4.7 collective-permute-done.47.p3
  321.2 5.5 rows_up.3
  336.0 5.9 collective-permute-start.38
  352.4 7.5 collective-permute-done.52.p2
  359.9 4.0 collective-permute-done.53.p3
  363.9 4.4 rows_slope.2
  379.0 6.2 collective-permute-done.54
  393.2 4.2 collective-permute-done.58.p2
  397.4 5.1 collective-permute-done.59.p3
  402.6 3.8 rows_heads.2
  411.1 3.7 collective-permute-start.71
  415.1 8.7 %attend_bwd.2 = (bf16[256,128]{1,0:T(8,128)(2,1)S(1)}, bf16[256,128]{1,0:T(8,128)(2,1)S(1)}, bf16[256,128]{1,0:T(8,128)(2,1)S(1)}, bf16[256,128]{1,0:T(8,128)(2,...) custom-call(bf16[256,384]{1,0:T(8,128)(2,1)S(1)} %get-tuple-element.169.refs_0_, ...), custom_call_target="tpu_custom_call" | custom-call | flops 2684354560 | bytes 8388608 | tf_op jit(solution)/shard_map/attend_bwd/pallas_call | solution.py:366
  424.8 4.0 collective-permute-start.63
  437.5 7.5 collective-permute-start.80
  447.7 6.4 collective-permute-done.73
  456.6 4.9 collective-permute-done.74
  464.7 4.6 collective-permute-done.66.refs_3_
  472.7 3.8 scatter_mm.13
  485.9 5.5 collective-permute-done.67
  500.0 5.2 collective-permute-start.79
  511.1 4.4 rows_slope.3
  523.7 6.3 weight_terms.3
  537.1 4.2 collective-permute-done.84
  542.2 5.7 collective-permute-done.82
  551.2 6.3 weight_terms.4
  566.6 6.8 collective-permute-done.90.p2
  578.9 3.8 rows_heads.3
  594.2 7.7 %attend_bwd.3 = (bf16[256,128]{1,0:T(8,128)(2,1)S(1)}, bf16[256,128]{1,0:T(8,128)(2,1)S(1)}, bf16[256,128]{1,0:T(8,128)(2,1)S(1)}, bf16[256,128]{1,0:T(8,128)(2,...) custom-call(bf16[256,384]{1,0:T(8,128)(2,1)S(1)} %copy-done.64, bf16[256,384]{1,0:T(8,128)(2,1)S(1)} %copy-done.66, ...), custom_call_target="tpu_custom_call" | custom-call | flops 2684354560 | bytes 8388608 | tf_op jit(solution)/shard_map/attend_bwd/pallas_call | solution.py:366
  612.6 6.0 collective-permute-done.96.refs_1_
  619.8 8.1 %collective-permute-done.97.refs_2_ = bf16[256,384]{1,0:T(8,128)(2,1)S(1)} collective-permute-done((bf16[256,384]{1,0:T(8,128)(2,1)S(1)}, bf16[256,384]{1,0:T(8,128)(2,1)S(1)}, u32[]{:S(2)}, u32[]{:S(2)}) %collective-permute-start.97) | collective-permute-done | bytes 196640 | tf_op jit(solution)/shard_map/ppermute | solution.py:406
  629.0 3.8 scatter_mm.15
  647.2 10.8 %weight_terms.5 = bf16[1024,2048]{1,0:T(8,128)(2,1)S(1)} custom-call(bf16[256,1024]{1,0:T(8,128)(2,1)S(1)} %copy-done.26, bf16[256,1024]{1,0:T(8,128)(2,1)S(1)} %copy-done.46, bf16[256,1024]{1,0:T(8,128)(2,1)S(1)} %copy-done.30, bf16[256,1024]{1,0:T(8,128)(2,1)S(1)} %copy-done.48, bf16[256,1536]{1,0:T(8,128)(2,1)S(1)} %get-tuple-element.249.refs_4_, ...), custom_call_target="tpu_custom_call" | custom-call | flops 4294967296 | bytes 12582912 | tf_op jit(solution)/shard_map/weight_terms/pallas_call | solution.py:256
  682.9 5.0 collective-permute-done.107
  688.1 4.6 collective-permute-start.110
  692.8 20.7 %collective-permute-done.126 = f32[124,128]{1,0:T(8,128)S(1)} collective-permute-done((f32[124,128]{1,0:T(8,128)S(1)}, f32[124,128]{1,0:T(8,128)S(1)}, u32[]{:S(2)}, u32[]{:S(2)}) %collective-permute-start.126) | collective-permute-done | bytes 63520 | tf_op jit(solution)/shard_map/ppermute | solution.py:406
  716.4 4.2 collective-permute-done.110
  732.3 13.7 %collective-permute-done.113.p2 = bf16[2,64,2048]{2,1,0:T(8,128)(2,1)S(1)} collective-permute-done((bf16[2,64,2048]{2,1,0:T(8,128)(2,1)S(1)}, bf16[2,64,2048]{2,1,0:T(8,128)(2,1)S(1)}, u32[]{:S(2)}, u32[]{:S(2)}) %collective-permute-start.113) | collective-permute-done | bytes 524320 | tf_op jit(solution)/shard_map/ppermute | solution.py:406
  (662 shorter events, 349.9 us)
Async XLA Ops:
  7.2 92.2 %all-gather.4.cloned.1.call-start = ((), (), s32[]{:S(2)}) async-start(), calls=%async_computation.3 | async-start | bytes 8912896 | tf_op jit(solution)/shard_map/all_gather | solution.py:588
  21.3 153.9 %all-gather.6.cloned.1.call-start = ((), (), s32[]{:S(2)}) async-start(), calls=%async_computation.4 | async-start | bytes 8912896 | tf_op jit(solution)/shard_map/all_gather | solution.py:595
  44.8 13.4 %collective-permute-start.23 = (bf16[128,1024]{1,0:T(8,128)(2,1)S(1)}, bf16[128,1024]{1,0:T(8,128)(2,1)S(1)}, u32[]{:S(2)}, u32[]{:S(2)}) collective-permute-start(bf16[128,1024]{1,0:T(8,128)(2,1)S(1)} %copy-done.105), channel_id=1, source_target_pairs={{0,4},{4,0},{1,5},{5,1},{2,6},{6,2},{3,7},{7,3},{8,12},{12,8},{9,1... | collective-permute-start | bytes 786440 | tf_op jit(solution)/shard_map/ppermute | solution.py:406
  60.8 148.8 %all-gather.8.cloned.1.call-start = ((), (), s32[]{:S(2)}) async-start(), calls=%async_computation.5 | async-start | bytes 8912896 | tf_op jit(solution)/shard_map/all_gather | solution.py:595
  62.6 14.0 %collective-permute-start.24 = (bf16[128,1024]{1,0:T(8,128)(2,1)}, bf16[128,1024]{1,0:T(8,128)(2,1)S(1)}, u32[]{:S(2)}, u32[]{:S(2)}) collective-permute-start(bf16[128,1024]{1,0:T(8,128)(2,1)} %pack.8.own), channel_id=1, source_target_pairs={{0,4},{4,0},{1,5},{5,1},{2,6},{6,2},{3,7},{7,3},{8,12},{12,8},{9,1... | collective-permute-start | bytes 786440 | tf_op jit(solution)/shard_map/ppermute | solution.py:406
  79.2 646.2 %reduce-scatter.8.cloned.1.call-start = ((), (), s32[]{:S(2)}) async-start(), calls=%async_computation.8 | async-start | bytes 4718592 | tf_op jit(solution)/shard_map/reduce_scatter | solution.py:489
  79.3 19.6 %collective-permute-start.5 = (f32[1536]{0:T(1024)S(1)}, f32[1536]{0:T(1024)S(1)}, u32[]{:S(2)}, u32[]{:S(2)}) collective-permute-start(f32[1536]{0:T(1024)S(1)} %pad_maximum_fusion.5), channel_id=1, source_target_pairs={{0,4},{4,0},{1,5},{5,1},{2,6},{6,2},{3,7},{7,3},{8,12},{12,8},{9,1... | collective-permute-start | bytes 18440 | tf_op jit(solution)/shard_map/ppermute | solution.py:406
  81.8 17.2 %collective-permute-start.13 = (f32[2048]{0:T(1024)S(1)}, f32[2048]{0:T(1024)S(1)}, u32[]{:S(2)}, u32[]{:S(2)}) collective-permute-start(f32[2048]{0:T(1024)S(1)} %bitcast.122), channel_id=1, source_target_pairs={{0,64},{64,0},{1,65},{65,1},{2,66},{66,2},{3,67},{67,3},{4,68},{68... | collective-permute-start | bytes 24584 | tf_op jit(solution)/shard_map/ppermute | solution.py:406
  109.7 10.9 %collective-permute-start.6 = (bf16[256,384]{1,0:T(8,128)(2,1)S(1)}, bf16[256,384]{1,0:T(8,128)(2,1)S(1)}, u32[]{:S(2)}, u32[]{:S(2)}) collective-permute-start(bf16[256,384]{1,0:T(8,128)(2,1)S(1)} %get-tuple-element.151), channel_id=1, source_target_pairs={{0,8},{8,0},{16,24},{24,16},{1,9},{9,1},{17,25},{25,17},{2,10},{10... | collective-permute-start | bytes 589832 | tf_op jit(solution)/shard_map/ppermute | solution.py:406
  109.7 21.8 %collective-permute-start.7 = (bf16[256,384]{1,0:T(8,128)(2,1)S(1)}, bf16[256,384]{1,0:T(8,128)(2,1)S(1)}, u32[]{:S(2)}, u32[]{:S(2)}) collective-permute-start(bf16[256,384]{1,0:T(8,128)(2,1)S(1)} %get-tuple-element.152), channel_id=1, source_target_pairs={{0,16},{8,24},{16,0},{24,8},{1,17},{9,25},{17,1},{25,9},{2,18},{10... | collective-permute-start | bytes 589832 | tf_op jit(solution)/shard_map/ppermute | solution.py:406
  113.7 19.1 %collective-permute-start.8 = (bf16[256,384]{1,0:T(8,128)(2,1)S(1)}, bf16[256,384]{1,0:T(8,128)(2,1)S(1)}, u32[]{:S(2)}, u32[]{:S(2)}) collective-permute-start(bf16[256,384]{1,0:T(8,128)(2,1)S(1)} %get-tuple-element.153), channel_id=1, source_target_pairs={{0,24},{8,16},{16,8},{24,0},{1,25},{9,17},{17,9},{25,1},{2,26},{10... | collective-permute-start | bytes 589832 | tf_op jit(solution)/shard_map/ppermute | solution.py:406
  113.8 21.8 %collective-permute-start.9 = (bf16[256,384]{1,0:T(8,128)(2,1)S(1)}, bf16[256,384]{1,0:T(8,128)(2,1)S(1)}, u32[]{:S(2)}, u32[]{:S(2)}) collective-permute-start(bf16[256,384]{1,0:T(8,128)(2,1)S(1)} %get-tuple-element.150.refs_0_), channel_id=1, source_target_pairs={{0,64},{64,0},{1,65},{65,1},{2,66},{66,2},{3,67},{67,3},{4,68},{68... | collective-permute-start | bytes 589832 | tf_op jit(solution)/shard_map/ppermute | solution.py:406
  120.6 15.1 %collective-permute-start.10 = (bf16[256,384]{1,0:T(8,128)(2,1)S(1)}, bf16[256,384]{1,0:T(8,128)(2,1)S(1)}, u32[]{:S(2)}, u32[]{:S(2)}) collective-permute-start(bf16[256,384]{1,0:T(8,128)(2,1)S(1)} %collective-permute-done.6.refs_1_), channel_id=1, source_target_pairs={{0,64},{64,0},{1,65},{65,1},{2,66},{66,2},{3,67},{67,3},{4,68},{68... | collective-permute-start | bytes 589832 | tf_op jit(solution)/shard_map/ppermute | solution.py:406
  155.7 14.0 %collective-permute-start.17 = (bf16[64,2048]{1,0:T(8,128)(2,1)S(1)}, bf16[64,2048]{1,0:T(8,128)(2,1)S(1)}, u32[]{:S(2)}, u32[]{:S(2)}) collective-permute-start(bf16[64,2048]{1,0:T(8,128)(2,1)S(1)} %get-tuple-element.159), channel_id=1, source_target_pairs={{0,2},{1,3},{2,0},{3,1},{4,6},{5,7},{6,4},{7,5},{8,10},{9,11},{10,... | collective-permute-start | bytes 786440 | tf_op jit(solution)/shard_map/ppermute | solution.py:406
  171.1 10.9 %collective-permute-start.21 = (bf16[64,2048]{1,0:T(8,128)(2,1)S(1)}, bf16[64,2048]{1,0:T(8,128)(2,1)S(1)}, u32[]{:S(2)}, u32[]{:S(2)}) collective-permute-start(bf16[64,2048]{1,0:T(8,128)(2,1)S(1)} %fusion.7.p0), channel_id=1, source_target_pairs={{0,2},{1,3},{2,0},{3,1},{4,6},{5,7},{6,4},{7,5},{8,10},{9,11},{10,... | collective-permute-start | bytes 786440 | tf_op jit(solution)/shard_map/ppermute | solution.py:406
  172.9 13.3 %collective-permute-start.22 = (bf16[64,2048]{1,0:T(8,128)(2,1)S(1)}, bf16[64,2048]{1,0:T(8,128)(2,1)S(1)}, u32[]{:S(2)}, u32[]{:S(2)}) collective-permute-start(bf16[64,2048]{1,0:T(8,128)(2,1)S(1)} %fusion.7.p0), channel_id=1, source_target_pairs={{0,3},{1,2},{2,1},{3,0},{4,7},{5,6},{6,5},{7,4},{8,11},{9,10},{10,... | collective-permute-start | bytes 786440 | tf_op jit(solution)/shard_map/ppermute | solution.py:406
  219.3 12.9 %collective-permute-start.25 = (bf16[64,2048]{1,0:T(8,128)(2,1)S(1)}, bf16[64,2048]{1,0:T(8,128)(2,1)S(1)}, u32[]{:S(2)}, u32[]{:S(2)}) collective-permute-start(bf16[64,2048]{1,0:T(8,128)(2,1)S(1)} %get-tuple-element.166), channel_id=1, source_target_pairs={{0,2},{1,3},{2,0},{3,1},{4,6},{5,7},{6,4},{7,5},{8,10},{9,11},{10,... | collective-permute-start | bytes 786440 | tf_op jit(solution)/shard_map/ppermute | solution.py:406
  233.1 14.2 %collective-permute-start.29 = (bf16[64,2048]{1,0:T(8,128)(2,1)S(1)}, bf16[64,2048]{1,0:T(8,128)(2,1)S(1)}, u32[]{:S(2)}, u32[]{:S(2)}) collective-permute-start(bf16[64,2048]{1,0:T(8,128)(2,1)S(1)} %fusion.8.p0), channel_id=1, source_target_pairs={{0,2},{1,3},{2,0},{3,1},{4,6},{5,7},{6,4},{7,5},{8,10},{9,11},{10,... | collective-permute-start | bytes 786440 | tf_op jit(solution)/shard_map/ppermute | solution.py:406
  236.8 13.4 %collective-permute-start.30 = (bf16[64,2048]{1,0:T(8,128)(2,1)S(1)}, bf16[64,2048]{1,0:T(8,128)(2,1)S(1)}, u32[]{:S(2)}, u32[]{:S(2)}) collective-permute-start(bf16[64,2048]{1,0:T(8,128)(2,1)S(1)} %fusion.8.p0), channel_id=1, source_target_pairs={{0,3},{1,2},{2,1},{3,0},{4,7},{5,6},{6,5},{7,4},{8,11},{9,10},{10,... | collective-permute-start | bytes 786440 | tf_op jit(solution)/shard_map/ppermute | solution.py:406
  263.9 11.8 %collective-permute-start.34 = (bf16[256,384]{1,0:T(8,128)(2,1)S(1)}, bf16[256,384]{1,0:T(8,128)(2,1)S(1)}, u32[]{:S(2)}, u32[]{:S(2)}) collective-permute-start(bf16[256,384]{1,0:T(8,128)(2,1)S(1)} %get-tuple-element.169.refs_0_), channel_id=1, source_target_pairs={{0,64},{64,0},{1,65},{65,1},{2,66},{66,2},{3,67},{67,3},{4,68},{68... | collective-permute-start | bytes 589832 | tf_op jit(solution)/shard_map/ppermute | solution.py:406
  291.9 13.6 %collective-permute-start.42 = (bf16[64,2048]{1,0:T(8,128)(2,1)S(1)}, bf16[64,2048]{1,0:T(8,128)(2,1)S(1)}, u32[]{:S(2)}, u32[]{:S(2)}) collective-permute-start(bf16[64,2048]{1,0:T(8,128)(2,1)S(1)} %get-tuple-element.178), channel_id=1, source_target_pairs={{0,2},{1,3},{2,0},{3,1},{4,6},{5,7},{6,4},{7,5},{8,10},{9,11},{10,... | collective-permute-start | bytes 786440 | tf_op jit(solution)/shard_map/ppermute | solution.py:406
  308.2 13.0 %collective-permute-start.47 = (bf16[64,2048]{1,0:T(8,128)(2,1)S(1)}, bf16[64,2048]{1,0:T(8,128)(2,1)S(1)}, u32[]{:S(2)}, u32[]{:S(2)}) collective-permute-start(bf16[64,2048]{1,0:T(8,128)(2,1)S(1)} %fusion.9.p0), channel_id=1, source_target_pairs={{0,3},{1,2},{2,1},{3,0},{4,7},{5,6},{6,5},{7,4},{8,11},{9,10},{10,... | collective-permute-start | bytes 786440 | tf_op jit(solution)/shard_map/ppermute | solution.py:406
  346.9 13.0 %collective-permute-start.52 = (bf16[64,2048]{1,0:T(8,128)(2,1)S(1)}, bf16[64,2048]{1,0:T(8,128)(2,1)S(1)}, u32[]{:S(2)}, u32[]{:S(2)}) collective-permute-start(bf16[64,2048]{1,0:T(8,128)(2,1)S(1)} %get-tuple-element.341.p0), channel_id=1, source_target_pairs={{0,2},{1,3},{2,0},{3,1},{4,6},{5,7},{6,4},{7,5},{8,10},{9,11},{10,... | collective-permute-start | bytes 786440 | tf_op jit(solution)/shard_map/ppermute | solution.py:406
  350.6 13.4 %collective-permute-start.53 = (bf16[64,2048]{1,0:T(8,128)(2,1)S(1)}, bf16[64,2048]{1,0:T(8,128)(2,1)S(1)}, u32[]{:S(2)}, u32[]{:S(2)}) collective-permute-start(bf16[64,2048]{1,0:T(8,128)(2,1)S(1)} %get-tuple-element.341.p0), channel_id=1, source_target_pairs={{0,3},{1,2},{2,1},{3,0},{4,7},{5,6},{6,5},{7,4},{8,11},{9,10},{10,... | collective-permute-start | bytes 786440 | tf_op jit(solution)/shard_map/ppermute | solution.py:406
  372.4 12.9 %collective-permute-start.54 = (bf16[64,2048]{1,0:T(8,128)(2,1)S(1)}, bf16[64,2048]{1,0:T(8,128)(2,1)S(1)}, u32[]{:S(2)}, u32[]{:S(2)}) collective-permute-start(bf16[64,2048]{1,0:T(8,128)(2,1)S(1)} %get-tuple-element.189), channel_id=1, source_target_pairs={{0,2},{1,3},{2,0},{3,1},{4,6},{5,7},{6,4},{7,5},{8,10},{9,11},{10,... | collective-permute-start | bytes 786440 | tf_op jit(solution)/shard_map/ppermute | solution.py:406
  389.4 13.2 %collective-permute-start.59 = (bf16[64,2048]{1,0:T(8,128)(2,1)S(1)}, bf16[64,2048]{1,0:T(8,128)(2,1)S(1)}, u32[]{:S(2)}, u32[]{:S(2)}) collective-permute-start(bf16[64,2048]{1,0:T(8,128)(2,1)S(1)} %get-tuple-element.343.p0), channel_id=1, source_target_pairs={{0,3},{1,2},{2,1},{3,0},{4,7},{5,6},{6,5},{7,4},{8,11},{9,10},{10,... | collective-permute-start | bytes 786440 | tf_op jit(solution)/shard_map/ppermute | solution.py:406
  411.1 17.7 %collective-permute-start.70 = (bf16[64,2048]{1,0:T(8,128)(2,1)S(1)}, bf16[64,2048]{1,0:T(8,128)(2,1)S(1)}, u32[]{:S(2)}, u32[]{:S(2)}) collective-permute-start(bf16[64,2048]{1,0:T(8,128)(2,1)S(1)} %get-tuple-element.362.p0), channel_id=1, source_target_pairs={{0,1},{1,0},{2,3},{3,2},{4,5},{5,4},{6,7},{7,6},{8,9},{9,8},{10,11... | collective-permute-start | bytes 786440 | tf_op jit(solution)/shard_map/ppermute | solution.py:406
  411.1 17.7 %collective-permute-start.71 = (bf16[64,2048]{1,0:T(8,128)(2,1)S(1)}, bf16[64,2048]{1,0:T(8,128)(2,1)S(1)}, u32[]{:S(2)}, u32[]{:S(2)}) collective-permute-start(bf16[64,2048]{1,0:T(8,128)(2,1)S(1)} %get-tuple-element.362.p0), channel_id=1, source_target_pairs={{0,2},{1,3},{2,0},{3,1},{4,6},{5,7},{6,4},{7,5},{8,10},{9,11},{10,... | collective-permute-start | bytes 786440 | tf_op jit(solution)/shard_map/ppermute | solution.py:406
  414.8 15.5 %collective-permute-start.72 = (bf16[64,2048]{1,0:T(8,128)(2,1)S(1)}, bf16[64,2048]{1,0:T(8,128)(2,1)}, u32[]{:S(2)}, u32[]{:S(2)}) collective-permute-start(bf16[64,2048]{1,0:T(8,128)(2,1)S(1)} %get-tuple-element.362.p0), channel_id=1, source_target_pairs={{0,3},{1,2},{2,1},{3,0},{4,7},{5,6},{6,5},{7,4},{8,11},{9,10},{10,... | collective-permute-start | bytes 786440 | tf_op jit(solution)/shard_map/ppermute | solution.py:406
  424.8 20.2 %collective-permute-start.63 = (f32[1024,256]{1,0:T(8,128)}, f32[1024,256]{1,0:T(8,128)}, u32[]{:S(2)}, u32[]{:S(2)}) collective-permute-start(f32[1024,256]{1,0:T(8,128)} %get-tuple-element.202), channel_id=1, source_target_pairs={{0,64},{64,0},{1,65},{65,1},{2,66},{66,2},{3,67},{67,3},{4,68},{68... | collective-permute-start | bytes 3145736 | tf_op jit(solution)/shard_map/ppermute | solution.py:406
  432.5 21.5 %collective-permute-start.73 = (bf16[256,2048]{1,0:T(8,128)(2,1)}, bf16[256,2048]{1,0:T(8,128)(2,1)}, u32[]{:S(2)}, u32[]{:S(2)}) collective-permute-start(bf16[256,2048]{1,0:T(8,128)(2,1)} %settle.2), channel_id=1, source_target_pairs={{0,0},{32,64},{64,32},{96,96},{1,1},{33,65},{65,33},{97,97},{2,2},... | collective-permute-start | bytes 3145736 | tf_op jit(solution)/shard_map/ppermute | solution.py:536
  434.4 27.1 %collective-permute-start.74 = (bf16[256,2048]{1,0:T(8,128)(2,1)}, bf16[256,2048]{1,0:T(8,128)(2,1)}, u32[]{:S(2)}, u32[]{:S(2)}) collective-permute-start(bf16[256,2048]{1,0:T(8,128)(2,1)} %settle.2), channel_id=1, source_target_pairs={{0,4},{4,0},{32,68},{36,64},{64,36},{68,32},{96,100},{100,96},{1,5... | collective-permute-start | bytes 3145736 | tf_op jit(solution)/shard_map/ppermute | solution.py:541
  437.5 86.2 %collective-permute-start.80 = (bf16[256,2048]{1,0:T(8,128)(2,1)S(1)}, bf16[256,2048]{1,0:T(8,128)(2,1)S(1)}, u32[]{:S(2)}, u32[]{:S(2)}) collective-permute-start(bf16[256,2048]{1,0:T(8,128)(2,1)S(1)} %get-tuple-element.163.refs_0_.refs_4_), channel_id=1, source_target_pairs={{0,64},{64,0},{1,65},{65,1},{2,66},{66,2},{3,67},{67,3},{4,68},{68... | collective-permute-start | bytes 3145736 | tf_op jit(solution)/shard_map/ppermute | solution.py:406
  445.0 78.7 %collective-permute-start.81 = (bf16[256,2048]{1,0:T(8,128)(2,1)S(1)}, bf16[256,2048]{1,0:T(8,128)(2,1)S(1)}, u32[]{:S(2)}, u32[]{:S(2)}) collective-permute-start(bf16[256,2048]{1,0:T(8,128)(2,1)S(1)} %get-tuple-element.181.refs_0_.refs_6_), channel_id=1, source_target_pairs={{0,64},{64,0},{1,65},{65,1},{2,66},{66,2},{3,67},{67,3},{4,68},{68... | collective-permute-start | bytes 3145736 | tf_op jit(solution)/shard_map/ppermute | solution.py:406
  447.6 17.2 %collective-permute-start.64 = (bf16[256,384]{1,0:T(8,128)(2,1)S(1)}, bf16[256,384]{1,0:T(8,128)(2,1)S(1)}, u32[]{:S(2)}, u32[]{:S(2)}) collective-permute-start(bf16[256,384]{1,0:T(8,128)(2,1)S(1)} %get-tuple-element.204), channel_id=1, source_target_pairs={{0,8},{8,0},{16,24},{24,16},{1,9},{9,1},{17,25},{25,17},{2,10},{10... | collective-permute-start | bytes 589832 | tf_op jit(solution)/shard_map/ppermute | solution.py:406
  479.1 12.4 %collective-permute-start.67 = (bf16[64,2048]{1,0:T(8,128)(2,1)S(1)}, bf16[64,2048]{1,0:T(8,128)(2,1)S(1)}, u32[]{:S(2)}, u32[]{:S(2)}) collective-permute-start(bf16[64,2048]{1,0:T(8,128)(2,1)S(1)} %get-tuple-element.208), channel_id=1, source_target_pairs={{0,2},{1,3},{2,0},{3,1},{4,6},{5,7},{6,4},{7,5},{8,10},{9,11},{10,... | collective-permute-start | bytes 786440 | tf_op jit(solution)/shard_map/ppermute | solution.py:406
  494.1 13.7 %collective-permute-start.76 = (bf16[64,2048]{1,0:T(8,128)(2,1)S(1)}, bf16[64,2048]{1,0:T(8,128)(2,1)S(1)}, u32[]{:S(2)}, u32[]{:S(2)}) collective-permute-start(bf16[64,2048]{1,0:T(8,128)(2,1)S(1)} %get-tuple-element.346.p0), channel_id=1, source_target_pairs={{0,2},{1,3},{2,0},{3,1},{4,6},{5,7},{6,4},{7,5},{8,10},{9,11},{10,... | collective-permute-start | bytes 786440 | tf_op jit(solution)/shard_map/ppermute | solution.py:406
  497.7 13.4 %collective-permute-start.77 = (bf16[64,2048]{1,0:T(8,128)(2,1)S(1)}, bf16[64,2048]{1,0:T(8,128)(2,1)S(1)}, u32[]{:S(2)}, u32[]{:S(2)}) collective-permute-start(bf16[64,2048]{1,0:T(8,128)(2,1)S(1)} %get-tuple-element.346.p0), channel_id=1, source_target_pairs={{0,3},{1,2},{2,1},{3,0},{4,7},{5,6},{6,5},{7,4},{8,11},{9,10},{10,... | collective-permute-start | bytes 786440 | tf_op jit(solution)/shard_map/ppermute | solution.py:406
  500.0 23.7 %collective-permute-start.79 = (bf16[256,1024]{1,0:T(8,128)(2,1)S(1)}, bf16[256,1024]{1,0:T(8,128)(2,1)S(1)}, u32[]{:S(2)}, u32[]{:S(2)}) collective-permute-start(bf16[256,1024]{1,0:T(8,128)(2,1)S(1)} %copy-done.42), channel_id=1, source_target_pairs={{0,64},{64,0},{1,65},{65,1},{2,66},{66,2},{3,67},{67,3},{4,68},{68... | collective-permute-start | bytes 1572872 | tf_op jit(solution)/shard_map/ppermute | solution.py:406
  532.0 196.6 %reduce-scatter.6.cloned.1.call-start = ((), (), s32[]{:S(2)}) async-start(), calls=%async_computation.7 | async-start | bytes 4718592 | tf_op jit(solution)/shard_map/reduce_scatter | solution.py:496
  533.0 14.9 %collective-permute-start.82 = (bf16[64,2048]{1,0:T(8,128)(2,1)S(1)}, bf16[64,2048]{1,0:T(8,128)(2,1)S(1)}, u32[]{:S(2)}, u32[]{:S(2)}) collective-permute-start(bf16[64,2048]{1,0:T(8,128)(2,1)S(1)} %copy-done.60), channel_id=1, source_target_pairs={{0,2},{1,3},{2,0},{3,1},{4,6},{5,7},{6,4},{7,5},{8,10},{9,11},{10,... | collective-permute-start | bytes 786440 | tf_op jit(solution)/shard_map/ppermute | solution.py:406
  536.2 15.0 %collective-permute-start.85 = (bf16[256,1024]{1,0:T(8,128)(2,1)}, bf16[256,1024]{1,0:T(8,128)(2,1)S(1)}, u32[]{:S(2)}, u32[]{:S(2)}) collective-permute-start(bf16[256,1024]{1,0:T(8,128)(2,1)} %get-tuple-element.225), channel_id=1, source_target_pairs={{0,64},{64,0},{1,65},{65,1},{2,66},{66,2},{3,67},{67,3},{4,68},{68... | collective-permute-start | bytes 1572872 | tf_op jit(solution)/shard_map/ppermute | solution.py:406
  537.1 14.1 %collective-permute-start.86 = (bf16[256,1024]{1,0:T(8,128)(2,1)}, bf16[256,1024]{1,0:T(8,128)(2,1)S(1)}, u32[]{:S(2)}, u32[]{:S(2)}) collective-permute-start(bf16[256,1024]{1,0:T(8,128)(2,1)} %get-tuple-element.227), channel_id=1, source_target_pairs={{0,64},{64,0},{1,65},{65,1},{2,66},{66,2},{3,67},{67,3},{4,68},{68... | collective-permute-start | bytes 1572872 | tf_op jit(solution)/shard_map/ppermute | solution.py:406
  559.6 191.0 %reduce-scatter.4.cloned.1.call-start = ((), (), s32[]{:S(2)}) async-start(), calls=%async_computation.6 | async-start | bytes 4718592 | tf_op jit(solution)/shard_map/reduce_scatter | solution.py:516
  559.7 13.7 %collective-permute-start.90 = (bf16[64,2048]{1,0:T(8,128)(2,1)S(1)}, bf16[64,2048]{1,0:T(8,128)(2,1)S(1)}, u32[]{:S(2)}, u32[]{:S(2)}) collective-permute-start(bf16[64,2048]{1,0:T(8,128)(2,1)S(1)} %get-tuple-element.228.p0), channel_id=1, source_target_pairs={{0,2},{1,3},{2,0},{3,1},{4,6},{5,7},{6,4},{7,5},{8,10},{9,11},{10,... | collective-permute-start | bytes 786440 | tf_op jit(solution)/shard_map/ppermute | solution.py:406
  561.9 13.5 %collective-permute-start.91 = (bf16[64,2048]{1,0:T(8,128)(2,1)S(1)}, bf16[64,2048]{1,0:T(8,128)(2,1)S(1)}, u32[]{:S(2)}, u32[]{:S(2)}) collective-permute-start(bf16[64,2048]{1,0:T(8,128)(2,1)S(1)} %get-tuple-element.228.p0), channel_id=1, source_target_pairs={{0,3},{1,2},{2,1},{3,0},{4,7},{5,6},{6,5},{7,4},{8,11},{9,10},{10,... | collective-permute-start | bytes 786440 | tf_op jit(solution)/shard_map/ppermute | solution.py:406
  607.4 11.3 %collective-permute-start.96 = (bf16[256,384]{1,0:T(8,128)(2,1)S(1)}, bf16[256,384]{1,0:T(8,128)(2,1)S(1)}, u32[]{:S(2)}, u32[]{:S(2)}) collective-permute-start(bf16[256,384]{1,0:T(8,128)(2,1)S(1)} %get-tuple-element.241), channel_id=1, source_target_pairs={{0,8},{8,0},{16,24},{24,16},{1,9},{9,1},{17,25},{25,17},{2,10},{10... | collective-permute-start | bytes 589832 | tf_op jit(solution)/shard_map/ppermute | solution.py:406
  607.5 20.5 %collective-permute-start.97 = (bf16[256,384]{1,0:T(8,128)(2,1)S(1)}, bf16[256,384]{1,0:T(8,128)(2,1)S(1)}, u32[]{:S(2)}, u32[]{:S(2)}) collective-permute-start(bf16[256,384]{1,0:T(8,128)(2,1)S(1)} %get-tuple-element.242), channel_id=1, source_target_pairs={{0,16},{8,24},{16,0},{24,8},{1,17},{9,25},{17,1},{25,9},{2,18},{10... | collective-permute-start | bytes 589832 | tf_op jit(solution)/shard_map/ppermute | solution.py:406
  609.8 19.1 %collective-permute-start.98 = (bf16[256,384]{1,0:T(8,128)(2,1)S(1)}, bf16[256,384]{1,0:T(8,128)(2,1)S(1)}, u32[]{:S(2)}, u32[]{:S(2)}) collective-permute-start(bf16[256,384]{1,0:T(8,128)(2,1)S(1)} %get-tuple-element.243), channel_id=1, source_target_pairs={{0,24},{8,16},{16,8},{24,0},{1,25},{9,17},{17,9},{25,1},{2,26},{10... | collective-permute-start | bytes 589832 | tf_op jit(solution)/shard_map/ppermute | solution.py:406
  611.3 23.6 %collective-permute-start.99 = (bf16[256,1024]{1,0:T(8,128)(2,1)S(1)}, bf16[256,1024]{1,0:T(8,128)(2,1)S(1)}, u32[]{:S(2)}, u32[]{:S(2)}) collective-permute-start(bf16[256,1024]{1,0:T(8,128)(2,1)S(1)} %copy-done.28), channel_id=1, source_target_pairs={{0,64},{64,0},{1,65},{65,1},{2,66},{66,2},{3,67},{67,3},{4,68},{68... | collective-permute-start | bytes 1572872 | tf_op jit(solution)/shard_map/ppermute | solution.py:406
  612.5 23.6 %collective-permute-start.105 = (bf16[256,512]{1,0:T(8,128)(2,1)S(1)}, bf16[256,512]{1,0:T(8,128)(2,1)S(1)}, u32[]{:S(2)}, u32[]{:S(2)}) collective-permute-start(bf16[256,512]{1,0:T(8,128)(2,1)S(1)} %copy-done.50), channel_id=1, source_target_pairs={{0,64},{64,0},{1,65},{65,1},{2,66},{66,2},{3,67},{67,3},{4,68},{68... | collective-permute-start | bytes 786440 | tf_op jit(solution)/shard_map/ppermute | solution.py:406
  618.6 18.5 %collective-permute-start.100 = (bf16[256,1024]{1,0:T(8,128)(2,1)S(1)}, bf16[256,1024]{1,0:T(8,128)(2,1)S(1)}, u32[]{:S(2)}, u32[]{:S(2)}) collective-permute-start(bf16[256,1024]{1,0:T(8,128)(2,1)S(1)} %copy-done.32), channel_id=1, source_target_pairs={{0,64},{64,0},{1,65},{65,1},{2,66},{66,2},{3,67},{67,3},{4,68},{68... | collective-permute-start | bytes 1572872 | tf_op jit(solution)/shard_map/ppermute | solution.py:406
  628.0 12.0 %collective-permute-start.102 = (bf16[256,1536]{1,0:T(8,128)(2,1)S(1)}, bf16[256,1536]{1,0:T(8,128)(2,1)S(1)}, u32[]{:S(2)}, u32[]{:S(2)}) collective-permute-start(bf16[256,1536]{1,0:T(8,128)(2,1)S(1)} %copy-done.24), channel_id=1, source_target_pairs={{0,64},{64,0},{1,65},{65,1},{2,66},{66,2},{3,67},{67,3},{4,68},{68... | collective-permute-start | bytes 2359304 | tf_op jit(solution)/shard_map/ppermute | solution.py:406
  675.6 12.4 %collective-permute-start.107 = (bf16[64,2048]{1,0:T(8,128)(2,1)S(1)}, bf16[64,2048]{1,0:T(8,128)(2,1)S(1)}, u32[]{:S(2)}, u32[]{:S(2)}) collective-permute-start(bf16[64,2048]{1,0:T(8,128)(2,1)S(1)} %copy-done.52), channel_id=1, source_target_pairs={{0,2},{1,3},{2,0},{3,1},{4,6},{5,7},{6,4},{7,5},{8,10},{9,11},{10,... | collective-permute-start | bytes 786440 | tf_op jit(solution)/shard_map/ppermute | solution.py:406
  679.6 33.9 %collective-permute-start.126 = (f32[124,128]{1,0:T(8,128)S(1)}, f32[124,128]{1,0:T(8,128)S(1)}, u32[]{:S(2)}, u32[]{:S(2)}) collective-permute-start(f32[124,128]{1,0:T(8,128)S(1)} %add_add_fusion.8), channel_id=1, source_target_pairs={{0,32},{4,36},{32,0},{36,4},{1,33},{5,37},{33,1},{37,5},{2,34},{6,... | collective-permute-start | bytes 190472 | tf_op jit(solution)/shard_map/ppermute | solution.py:406
  680.2 33.3 %collective-permute-start.127 = (f32[124,128]{1,0:T(8,128)S(1)}, f32[124,128]{1,0:T(8,128)S(1)}, u32[]{:S(2)}, u32[]{:S(2)}) collective-permute-start(f32[124,128]{1,0:T(8,128)S(1)} %add_add_fusion.8), channel_id=1, source_target_pairs={{0,36},{4,32},{32,4},{36,0},{1,37},{5,33},{33,5},{37,1},{2,38},{6,... | collective-permute-start | bytes 190472 | tf_op jit(solution)/shard_map/ppermute | solution.py:406
  681.4 35.0 %collective-permute-start.125 = (f32[124,128]{1,0:T(8,128)S(1)}, f32[124,128]{1,0:T(8,128)S(1)}, u32[]{:S(2)}, u32[]{:S(2)}) collective-permute-start(f32[124,128]{1,0:T(8,128)S(1)} %add_add_fusion.8), channel_id=1, source_target_pairs={{0,4},{4,0},{32,36},{36,32},{1,5},{5,1},{33,37},{37,33},{2,6},{6,2... | collective-permute-start | bytes 190472 | tf_op jit(solution)/shard_map/ppermute | solution.py:406
  688.1 32.5 %collective-permute-start.110 = (bf16[64,2048]{1,0:T(8,128)(2,1)S(1)}, bf16[64,2048]{1,0:T(8,128)(2,1)S(1)}, u32[]{:S(2)}, u32[]{:S(2)}) collective-permute-start(bf16[64,2048]{1,0:T(8,128)(2,1)S(1)} %add_convert_fusion), channel_id=1, source_target_pairs={{0,0},{32,64},{64,32},{96,96},{1,1},{33,65},{65,33},{97,97},{2,2},... | collective-permute-start | bytes 786440 | tf_op jit(solution)/shard_map/ppermute | solution.py:536
  692.7 27.9 %collective-permute-start.111 = (bf16[64,2048]{1,0:T(8,128)(2,1)S(1)}, bf16[64,2048]{1,0:T(8,128)(2,1)S(1)}, u32[]{:S(2)}, u32[]{:S(2)}) collective-permute-start(bf16[64,2048]{1,0:T(8,128)(2,1)S(1)} %add_convert_fusion), channel_id=1, source_target_pairs={{0,4},{4,0},{32,68},{36,64},{64,36},{68,32},{96,100},{100,96},{1,5... | collective-permute-start | bytes 786440 | tf_op jit(solution)/shard_map/ppermute | solution.py:541
  720.7 11.6 %collective-permute-start.112 = (bf16[2,64,2048]{2,1,0:T(8,128)(2,1)S(1)}, bf16[2,64,2048]{2,1,0:T(8,128)(2,1)S(1)}, u32[]{:S(2)}, u32[]{:S(2)}) collective-permute-start(bf16[2,64,2048]{2,1,0:T(8,128)(2,1)S(1)} %pad_maximum_fusion.p0), channel_id=1, source_target_pairs={{0,1},{1,0},{2,3},{3,2},{4,5},{5,4},{6,7},{7,6},{8,9},{9,8},{10,11... | collective-permute-start | bytes 1572872 | tf_op jit(solution)/shard_map/ppermute | solution.py:406
  722.1 23.9 %collective-permute-start.113 = (bf16[2,64,2048]{2,1,0:T(8,128)(2,1)S(1)}, bf16[2,64,2048]{2,1,0:T(8,128)(2,1)S(1)}, u32[]{:S(2)}, u32[]{:S(2)}) collective-permute-start(bf16[2,64,2048]{2,1,0:T(8,128)(2,1)S(1)} %pad_maximum_fusion.p0), channel_id=1, source_target_pairs={{0,2},{1,3},{2,0},{3,1},{4,6},{5,7},{6,4},{7,5},{8,10},{9,11},{10,... | collective-permute-start | bytes 1572872 | tf_op jit(solution)/shard_map/ppermute | solution.py:406
  724.6 21.3 %collective-permute-start.114 = (bf16[2,64,2048]{2,1,0:T(8,128)(2,1)S(1)}, bf16[2,64,2048]{2,1,0:T(8,128)(2,1)S(1)}, u32[]{:S(2)}, u32[]{:S(2)}) collective-permute-start(bf16[2,64,2048]{2,1,0:T(8,128)(2,1)S(1)} %pad_maximum_fusion.p0), channel_id=1, source_target_pairs={{0,3},{1,2},{2,1},{3,0},{4,7},{5,6},{6,5},{7,4},{8,11},{9,10},{10,... | collective-permute-start | bytes 1572872 | tf_op jit(solution)/shard_map/ppermute | solution.py:406
  726.3 27.8 %collective-permute-start.117 = (bf16[128,1024]{1,0:T(8,128)(2,1)S(1)}, bf16[128,1024]{1,0:T(8,128)(2,1)S(1)}, u32[]{:S(2)}, u32[]{:S(2)}) collective-permute-start(bf16[128,1024]{1,0:T(8,128)(2,1)S(1)} %slice.215), channel_id=1, source_target_pairs={{0,4},{4,0},{1,5},{5,1},{2,6},{6,2},{3,7},{7,3},{8,12},{12,8},{9,1... | collective-permute-start | bytes 786440 | tf_op jit(solution)/shard_map/ppermute | solution.py:406
  729.6 25.6 %collective-permute-start.116 = (bf16[128,1024]{1,0:T(8,128)(2,1)S(1)}, bf16[128,1024]{1,0:T(8,128)(2,1)}, u32[]{:S(2)}, u32[]{:S(2)}) collective-permute-start(bf16[128,1024]{1,0:T(8,128)(2,1)S(1)} %slice.213), channel_id=1, source_target_pairs={{0,4},{4,0},{1,5},{5,1},{2,6},{6,2},{3,7},{7,3},{8,12},{12,8},{9,1... | collective-permute-start | bytes 786440 | tf_op jit(solution)/shard_map/ppermute | solution.py:406
  (213 other events, 3121.4 us)
Sparse Core Ops, SparseCore 0:
  21.4 67.1 all-gather.3
  90.9 63.7 all-gather.5
  156.4 53.0 all-gather.7
  532.1 48.4 reduce-scatter.7
  582.9 61.7 reduce-scatter.5
  660.2 52.8 reduce-scatter.3

commit v2 on v1

v2 whole, which is shorter than its diff:
```python
import functools

import jax
import jax.numpy as jnp
from jax import lax
from jax.experimental import pallas as pl
from jax.experimental.pallas import tpu as pltpu
from jax.sharding import Mesh, PartitionSpec as P

AXES = ("core", "ylo", "x", "yhi", "z")
Y = ("ylo", "yhi")
ROWS = ("core", "ylo", "x")
D = 2048
HD = 128
TOK = 256
OWN = 64
REACH = 512
LOW = jnp.bfloat16
F32 = jnp.float32
BLOCKED = -1e30
SCALE = HD ** (-0.5)
LOG2E = 1.4426950408889634
EPSILON = 1e-05
CURVE = 0.7978845608028654
CUBIC = 0.044715


def shape(dims, dtype=LOW):
    return jax.ShapeDtypeStruct(dims, dtype)


def dot_t(a, b, ca=1, cb=0):
    return lax.dot_general(a, b, (((ca,), (cb,)), ((), ())), preferred_element_type=F32)


def call(name, body, outs, *args, spot=None, scratch=(), mib=12, flops=0, size=2**21, exps=0):
    specs = [pl.BlockSpec(memory_space=pltpu.VMEM)] * len(args)
    if spot is not None:
        args = (spot,) + args
        specs = [pl.BlockSpec(memory_space=pltpu.SMEM)] + specs
    return pl.pallas_call(
        body,
        in_specs=specs,
        out_specs=[pl.BlockSpec(memory_space=pltpu.VMEM)] * len(outs),
        out_shape=outs,
        scratch_shapes=scratch,
        compiler_params=pltpu.CompilerParams(vmem_limit_bytes=mib * 2**20),
        cost_estimate=pl.CostEstimate(flops=flops, bytes_accessed=size, transcendentals=exps),
        name=name,
    )(*args)


def at_block(index, size):
    return pl.ds(pl.multiple_of(index * size, size), size)


def pack_heads_body(q, k, v, o, out):
    for j in range(2):
        at = slice(128 * j, 128 * j + 128)
        for t, part in enumerate((q, k, v)):
            out[:, 384 * j + 128 * t : 384 * j + 128 * t + 128] = part[:, at]
    out[:, 768:] = o[...].T


def turn_body(down, out):
    out[...] = down[...].T


def join_heads_columns(own, far, out, rows):
    for j in range(2):
        for h, part in enumerate((own, far)):
            slot = 2 * j + h
            out[rows, 384 * slot : 384 * slot + 384] = part[:, 384 * j : 384 * j + 384]
            out[rows, 1536 + 128 * slot : 1664 + 128 * slot] = part[:, 768 + 128 * j : 896 + 128 * j]


def pair_body(heads, spot, *refs):
    parts, out = refs[:-1], refs[-1]
    for ylo in range(2):
        rows = at_block(ylo ^ spot[2], 128)
        if heads:
            join_heads_columns(parts[ylo], parts[ylo + 2], out, rows)
            continue
        for i, d in enumerate((ylo, ylo + 2, ylo + 4, ylo + 6)):
            out[rows, 1024 * i : 1024 * i + 1024] = parts[d][...]


def pair(heads, spot, parts):
    outs = [shape((256, 2048 if heads else 4096))]
    return call("pair", functools.partial(pair_body, heads), outs, *parts, spot=spot)[0]


def pack(body, width, *parts):
    return call("pack", body, [shape((128, width))], *parts)[0]


def load_body(first, source, kept, sems):
    copies = []
    for core in range(2):
        for ylo in range(2):
            for x in range(4):
                at, to = 256 * (4 * core + x) + 128 * ylo, 1024 * core + 512 * ylo + 128 * x
                part = source.at[pl.ds(at, 128), pl.ds(first, 2048)]
                copies.append(pltpu.make_async_copy(part, kept.at[pl.ds(to, 128)], sems.at[len(copies)]))
    for copy in copies:
        copy.start()
    for copy in copies:
        copy.wait()


def load(matrix, first=0):
    return pl.pallas_call(
        functools.partial(load_body, first),
        in_specs=[pl.BlockSpec(memory_space=pl.ANY)],
        out_specs=pl.BlockSpec(memory_space=pltpu.VMEM),
        out_shape=pltpu.VMEM((D, 2048), LOW),
        scratch_shapes=[pltpu.SemaphoreType.DMA((16,))],
        compiler_params=pltpu.CompilerParams(vmem_limit_bytes=2**22),
        cost_estimate=pl.CostEstimate(flops=0, bytes_accessed=4 * matrix.size, transcendentals=0),
        name="load",
    )(pltpu.with_memory_space_constraint(matrix, pltpu.HBM))


def held(matrix):
    return pltpu.with_memory_space_constraint(matrix, pltpu.VMEM)


def settle_body(spot, p0, p1, p2, p3, out):
    for d, part in enumerate((p0, p1, p2, p3)):
        at = at_block(d ^ spot[3], OWN)
        if len(out.shape) == 2:
            out[at] = part[...]
        else:
            out[:, at] = part[...]


def settle(spot, parts):
    return call("settle", settle_body, [shape(parts[0].shape[:-2] + (TOK, D))], *parts, spot=spot)[0]


def four(refs, at):
    p = [ref[at].astype(F32) for ref in refs]
    return (p[0] + p[2]) + (p[1] + p[3])


def rows_body(kind, first, spot, p0, p1, p2, p3, w, *refs):
    extra = refs[0] if kind != "heads" else None
    keep, send, *outs = refs[1:] if kind != "heads" else refs
    kept, sent = at_block(spot[1], D // 2), at_block(1 - spot[1], D // 2)
    for i, p in enumerate((p0, p1, p2, p3)):
        keep[OWN * i : OWN * i + OWN] = p[:OWN, kept]
        send[OWN * i : OWN * i + OWN] = p[:OWN, sent]
    if p0.shape[0] > OWN:
        *outs, sums = outs
        sums[...] = four((p0, p1, p2, p3), slice(OWN, OWN + 16))

    def product(at):
        return dot_t(keep[...], w[kept, at]) + dot_t(send[...], w[sent, at])

    if kind in ("qkv", "heads"):
        width = outs[0].shape[1]
        for d in range(4):
            slot = d ^ spot[0]
            values = product(pl.ds(pl.multiple_of(first + slot * width, 128), width))
            if kind == "qkv":
                values = values + extra[:, at_block(slot, width)]
            outs[d][...] = values.astype(LOW)
        return
    tile = 512
    for i in range(4):
        at = slice(tile * i, tile * i + tile)
        values = product(at)
        if kind == "up":
            values = values + extra[:, at]
            square = values * values
            bend = jnp.tanh(CURVE * (values + CUBIC * (square * values)))
            outs[0][:, at] = (0.5 * values * (1.0 + bend)).astype(LOW)
            slope = 0.5 * (1.0 + bend) + 0.5 * values * (1.0 - bend * bend) * (CURVE * (1.0 + 3.0 * CUBIC * square))
            outs[1][:, at] = slope.astype(LOW)
        else:
            low = (values * extra[:, at].astype(F32)).astype(LOW)
            outs[0][:, at] = low
            outs[1][:, at] = jnp.sum(low.astype(F32), axis=0, keepdims=True)


def rows_mm(kind, spot, pieces, weight, extra=None):
    half = shape((TOK, D // 2))
    n, first, outs = {
        "qkv": (1536, 0, [shape((TOK, 384))] * 4),
        "heads": (512, 1536, [shape((TOK, HD))] * 4),
        "up": (2048, 0, [shape((TOK, 2048))] * 2),
        "slope": (2048, 0, [shape((TOK, 2048)), shape((1, 2048), F32)]),
    }[kind]
    args = (held(weight),) if extra is None else (held(weight), extra)
    if pieces[0].shape[0] > OWN:
        outs = [*outs, shape((16, D), F32)]
    return call(
        "rows_" + kind,
        functools.partial(rows_body, kind, first),
        [half, half, *outs],
        *pieces,
        *args,
        spot=spot,
        mib=12,
        flops=2 * TOK * D * n,
        size=2 * D * n,
        exps=TOK * n if kind == "up" else 0,
    )


def scatter_body(n_parts, first, k, spot, *refs):
    parts, w, outs = refs[:n_parts], refs[n_parts], refs[n_parts + 1 : n_parts + 5]
    if n_parts == 1:
        rows = parts[0]
    else:
        rows = refs[n_parts + 5]
        for d, part in enumerate(parts):
            rows[:, at_block(d ^ spot[0], k // 4)] = part[...]
    tile = 512
    for i in range(D // tile):
        to = slice(tile * i, tile * i + tile)
        values = dot_t(rows[...], w[to, first : first + k], 1, 1)
        outs[0][:, to] = values[:OWN]
        for d in range(1, 4):
            outs[d][:, to] = values[OWN * d : OWN * d + OWN].astype(LOW)


def scatter_mm(spot, parts, weight, k, first):
    outs = [shape((OWN, D), F32)] + [shape((OWN, D))] * 3
    if len(parts) > 1:
        outs.append(shape((TOK, k)))
    return call(
        "scatter_mm",
        functools.partial(scatter_body, len(parts), first, k),
        outs,
        *parts,
        held(weight),
        spot=spot,
        flops=2 * TOK * D * k,
        size=2 * D * k,
    )


def fetched(refs, olds, buffers, sems, chunks):
    ready, copies, at = [], [], 0
    for ref, old, count in zip(refs, olds, chunks):
        if not old:
            ready.append(ref)
            copies.append([None] * count)
            continue
        n = ref.shape[1] // count
        parts = [(pl.ds(0, ref.shape[0]), pl.ds(n * c, n)) for c in range(count)]
        ready.append(buffers[at])
        copies.append([pltpu.make_async_copy(ref.at[p], buffers[at].at[p], sems.at[at, c]) for c, p in enumerate(parts)])
        at += 1
    for c in range(max(chunks)):
        for mine in copies:
            if c < len(mine) and mine[c] is not None:
                mine[c].start()
    return ready, copies


def arrive(copies):
    for copy in copies:
        if copy is not None:
            copy.wait()


def old_call(name, body, outs, out_specs, operands, olds, chunks, spot, scratch, mib):
    buffers = [pltpu.VMEM(a.shape, a.dtype) for a, old in zip(operands, olds) if old]
    n_in, n_old = len(operands), len(buffers)

    def inner(spot_ref, *refs):
        out_refs = refs[n_in : n_in + len(outs)]
        rest = refs[n_in + len(outs) :]
        ready, copies = fetched(refs[:n_in], olds, rest[:n_old], rest[n_old], chunks)
        body(spot_ref, ready, copies, out_refs, rest[n_old + 1 :])

    args = [pltpu.with_memory_space_constraint(a, pltpu.HBM) if old else a for a, old in zip(operands, olds)]
    return pl.pallas_call(
        inner,
        in_specs=[pl.BlockSpec(memory_space=pltpu.SMEM)]
        + [pl.BlockSpec(memory_space=pl.ANY if old else pltpu.VMEM) for old in olds],
        out_specs=out_specs,
        out_shape=outs,
        scratch_shapes=[*buffers, pltpu.SemaphoreType.DMA((max(n_old, 1), max(chunks))), *scratch],
        compiler_params=pltpu.CompilerParams(vmem_limit_bytes=mib * 2**20),
        cost_estimate=pl.CostEstimate(flops=2**32, bytes_accessed=2**23, transcendentals=0),
        name=name,
    )(spot, *args)


def term_body(spot, operands, copies, outs, scratch):
    turned, parts, sems = scratch
    for i in range(4):
        arrive(copies[i])
        turned[:, TOK * i : TOK * i + TOK] = operands[i][...].T
    sent = []
    for step in range(4):
        at = slice(512 * step, 512 * step + 512)
        arrive([copies[4 + i][step] for i in range(4)])
        total = None
        for i in range(4):
            part = dot_t(turned[:, TOK * i : TOK * i + TOK], operands[4 + i][:, at])
            total = part if total is None else total + part
        if step > 1:
            sent[step - 2].wait()
        parts[step & 1] = total.astype(LOW)
        sent.append(pltpu.make_async_copy(parts.at[step & 1], outs[0].at[:, pl.ds(512 * step, 512)], sems.at[step & 1]))
        sent[-1].start()
    arrive(sent[2:])


def weight_term(spot, lefts, rights, olds):
    return old_call(
        "weight_term",
        term_body,
        [pltpu.HBM((1024, 2048), LOW)],
        [pl.BlockSpec(memory_space=pl.ANY)],
        [*lefts, *rights],
        olds,
        [1] * 4 + [4] * 4,
        spot,
        [pltpu.VMEM((1024, 1024), LOW), pltpu.VMEM((2, 1024, 512), LOW), pltpu.SemaphoreType.DMA((2,))],
        16,
    )[0]


def head_terms_body(spot, operands, copies, outs, turned):
    rights = operands[4:8], operands[12:16]
    for g in range(2):
        for i in range(4):
            arrive(copies[8 * g + i])
            for x in range(4):
                for ylo in range(2):
                    at, to = 512 * ylo + 128 * x, 256 * x + 128 * ylo
                    turned[g][to : to + 128, TOK * i : TOK * i + TOK] = operands[8 * g + i][:, at : at + 128].T
    for i in (*range(4, 8), *range(12, 16)):
        arrive(copies[i])
    for slot in range(4):
        first = 1024 * (slot & 1)
        for g, width in enumerate((384, 128)):
            total = None
            for i in range(4):
                part = dot_t(turned[g][:, TOK * i : TOK * i + TOK], rights[g][i][:, width * slot : width * slot + width])
                total = part if total is None else total + part
            to = first + width * (slot >> 1)
            outs[0][:, to : to + width] = total.astype(LOW)
            first += 2 * width
    line = [jnp.sum(rights[0][i][...].astype(F32), axis=0, keepdims=True) for i in (0, 2)]
    outs[1][...] = line[0] + line[1]


def head_terms(spot, sides, olds):
    return old_call(
        "head_terms",
        head_terms_body,
        [shape((1024, 2048)), shape((1, 1536), F32)],
        [pl.BlockSpec(memory_space=pltpu.VMEM)] * 2,
        [part for side in sides for part in side],
        olds,
        [1] * 16,
        spot,
        [pltpu.VMEM((1024, 1024), LOW)] * 2,
        20,
    )


def cut_body(spot, total, *outs):
    for d in range(4):
        outs[d][...] = total[at_block((d & 1) ^ spot[2], 128), 1024 * (d >> 1) : 1024 * (d >> 1) + 1024]


def cut(spot, total):
    return call("cut", cut_body, [shape((128, 1024))] * 4, total, spot=spot)


def heads_result_body(p0, p1, p2, p3, q, k, v, o):
    total = four((p0, p1, p2, p3), slice(None))
    for j in range(2):
        to = slice(128 * j, 128 * j + 128)
        for t, ref in enumerate((q, k, v)):
            at = 384 * j + 128 * t
            ref[:, to] = total[:, at : at + 128]
        o[to] = total[:, 768 + 128 * j : 896 + 128 * j].T


def heads_result(parts):
    square = shape((128, 256), F32)
    return call("heads_result", heads_result_body, [square, square, square, shape((256, 128), F32)], *parts)


def hidden_result_body(up, up_far, down, down_far, up_out, down_out):
    up_out[...] = up[:, :1024].astype(F32) + up_far[...].astype(F32)
    down_out[...] = (down[:, :1024].astype(F32) + down_far[...].astype(F32)).T


def hidden_result(*parts):
    return call("hidden_result", hidden_result_body, [shape((128, 1024), F32), shape((1024, 128), F32)], *parts)


def norm_body(given, *refs):
    parts, (base, bias, gain, shift, normed, scale, result, low) = refs[:given], refs[given:]
    values = base[...] + bias[...] + ((parts[0][...] + parts[2][...].astype(F32)) + (parts[1][...].astype(F32) + parts[3][...].astype(F32)))
    center = jnp.mean(values, axis=-1, keepdims=True)
    centered = values - center
    spread = jnp.mean(centered * centered, axis=-1, keepdims=True)
    root = lax.rsqrt(spread + EPSILON)
    unit = centered * root
    normed[...] = unit
    scale[...] = root
    values = unit * gain[...] + shift[...]
    result[...] = values
    low[...] = values.astype(LOW)


def norm(parts, base, bias, gain, shift):
    rows = shape((OWN, D), F32)
    outs = [rows, shape((OWN, 1), F32), rows, shape((OWN, D))]
    return call("norm", functools.partial(norm_body, 4), outs, *parts, base, bias, gain, shift, flops=2**21)


def norm_back_body(given, under, *refs):
    parts, (base, normed, scale, gain, *refs) = refs[:given], refs[given:]
    if under:
        ffn_sums, sums_two, *refs = refs
    back, low, sums = refs
    grad = base[...]
    if given:
        grad = grad + ((parts[0][...] + parts[2][...].astype(F32)) + (parts[1][...].astype(F32) + parts[3][...].astype(F32)))
    unit = normed[...]
    tilted = grad * gain[...]
    values = tilted - jnp.mean(tilted, axis=-1, keepdims=True) - unit * jnp.mean(tilted * unit, axis=-1, keepdims=True)
    values = values * scale[...]
    back[...] = values
    cut = values.astype(LOW)
    low[:OWN] = cut
    lines = [jnp.sum(part, axis=0, keepdims=True) for part in (grad * unit, grad, cut.astype(F32))]
    for i, line in enumerate(lines):
        sums[i : i + 1] = line
    if under:
        lines = jnp.concatenate([*lines, ffn_sums[...], jnp.zeros((10, D), F32)], axis=0)
        both = jnp.concatenate([sums_two[...], jnp.zeros((10, D), F32)], axis=0)
        low[OWN:] = (lines + both).astype(LOW)


def norm_back(parts, base, normed, scale, gain, under=()):
    outs = [shape((OWN, D), F32), shape((OWN + 16 * bool(under), D)), shape((3, D), F32)]
    body = functools.partial(norm_back_body, len(parts), bool(under))
    return call("norm_back", body, outs, *parts, base, normed, scale, gain, *under, flops=2**21)


def marks_body(spot, seg, row, column, table):
    lane = lax.broadcasted_iota(jnp.int32, (1, 64), 1)
    for i in range(32):
        block = ((spot[1] ^ (i >> 4)) * 4 + (spot[0] ^ ((i >> 2) & 3))) * 4 + (spot[3] ^ (i & 3))
        line = seg[pl.ds(block, 1)] * 8192.0 + (block * 64 + lane).astype(F32)
        table[i : i + 1] = line
        if i < 16:
            row[:, 64 * i : 64 * i + 64] = line
    turned = table[...].T
    for i in range(32):
        column[64 * i : 64 * i + 64] = turned[:, i : i + 1]


def marks(spot, seg):
    outs = [shape((1, 1024), F32), shape((2048, 1), F32)]
    return call("marks", marks_body, outs, seg.reshape(32, 64), spot=spot, scratch=[pltpu.VMEM((32, 64), F32)])


def near(marks, keys, windowed):
    return jnp.abs(marks - keys) <= (REACH if windowed else 2047.0)


def load_heads(pieces, keys, values):
    for i, piece in enumerate(pieces):
        at = slice(TOK * i, TOK * i + TOK)
        keys[at] = piece[:, HD : 2 * HD]
        values[at] = piece[:, 2 * HD :]


def block_gap(spot, d, e):
    query, key = spot[0] ^ d, spot[0] ^ (e & 3)
    gap = jnp.abs(query - key)
    if e < 4:
        return gap
    return jnp.where(spot[1] == 0, 4 + key - query, 4 + query - key)


def attend_chunk(windowed, query, keys, at, qmark, kmark):
    s = dot_t(keys[at], query, 1, 1)
    return jnp.where(near(qmark, kmark[at], windowed), s, BLOCKED)


def fwd_body(windowed, spot, *refs):
    pieces, qmark, kmark = refs[:8], refs[8], refs[9]
    outs, lse, keys, values, best, total, mixed = refs[10:14], *refs[14:]
    load_heads(pieces, keys, values)
    own = slice(0, 4 * TOK if windowed else 8 * TOK)
    for d in range(4):
        at = slice(TOK * d, TOK * d + TOK)
        query, mark = pieces[d][:, :HD], qmark[:, at]
        s = attend_chunk(windowed, query, keys, own, mark, kmark)
        top = jnp.max(s, axis=0, keepdims=True)
        p = jnp.exp2((s - top) * (SCALE * LOG2E))
        count = jnp.sum(p, axis=0, keepdims=True)
        part = dot_t(values[own], p.astype(LOW), 0, 0)
        if windowed:
            best[...], total[...], mixed[...] = top, count, part
            for e in range(4, 8):

                @pl.when(block_gap(spot, d, e) < 3)
                def _():
                    far = slice(TOK * e, TOK * e + TOK)
                    s = attend_chunk(windowed, query, keys, far, mark, kmark)
                    top = jnp.maximum(best[...], jnp.max(s, axis=0, keepdims=True))
                    p = jnp.exp2((s - top) * (SCALE * LOG2E))
                    less = jnp.exp2((best[...] - top) * (SCALE * LOG2E))
                    total[...] = total[...] * less + jnp.sum(p, axis=0, keepdims=True)
                    mixed[...] = mixed[...] * less + dot_t(values[far], p.astype(LOW), 0, 0)
                    best[...] = top

            top, count, part = best[...], total[...], mixed[...]
        outs[d][...] = (part / count).T.astype(LOW)
        lse[:, at] = top * (SCALE * LOG2E) + jnp.log2(count)


def attend_fwd(spot, pieces, mark, windowed):
    n = 4 * TOK
    *mixed, lse = call(
        "attend_fwd",
        functools.partial(fwd_body, windowed),
        [shape((TOK, HD))] * 4 + [shape((1, n), F32)],
        *pieces,
        *mark,
        spot=spot,
        scratch=[pltpu.VMEM((2 * n, HD), LOW)] * 2
        + [pltpu.VMEM((1, TOK), F32)] * 2
        + [pltpu.VMEM((HD, TOK), F32)],
        mib=12,
        flops=8 * n * n * HD,
        size=2**22,
        exps=2 * n * n,
    )
    return mixed, lse


def bwd_body(windowed, spot, refs, copies, results, scratch):
    pieces, grads, outs, lse, qmark, kmark = refs[:8], refs[8:12], refs[12:16], *refs[16:]
    (*dq, own, far), (keys, values, acc, turned) = results, scratch
    n = 4 * TOK
    for copy in copies:
        arrive(copy)
    load_heads(pieces, keys, values)
    acc[...] = jnp.zeros_like(acc)
    for d in range(4):
        place = slice(TOK * d, TOK * d + TOK)
        query, grad, mark, norm_log = pieces[d][:, :HD], grads[d][...], qmark[:, place], lse[:, place]
        dots = jnp.sum((grad.astype(F32) * outs[d][...].astype(F32)).T, axis=0, keepdims=True)

        def chunk(at):
            s = attend_chunk(windowed, query, keys, at, mark, kmark)
            p = jnp.exp2(s * (SCALE * LOG2E) - norm_log)
            ds = (p * (dot_t(values[at], grad, 1, 1) - dots)).astype(LOW)
            acc[at, :HD] += dot_t(ds, query)
            acc[at, HD:] += dot_t(p.astype(LOW), grad)
            return dot_t(keys[at], ds, 0, 0)

        if not windowed:
            part = chunk(slice(0, 2 * n))
        else:
            turned[...] = chunk(slice(0, n))
            for e in range(4, 8):

                @pl.when(block_gap(spot, d, e) < 3)
                def _():
                    turned[...] += chunk(slice(TOK * e, TOK * e + TOK))

            part = turned[...]
        dq[d][...] = (part * SCALE).T.astype(LOW)
    for ref, start in ((own, 0), (far, n)):
        ref[:, :HD] = acc[start : start + n, :HD] * SCALE
        ref[:, HD:] = acc[start : start + n, HD:]


def attend_bwd(spot, pieces, grads, mixed, lse, mark, windowed):
    n = 4 * TOK
    old = [windowed] * 8
    outs = [shape((TOK, HD))] * 4 + [shape((n, 2 * HD), F32)] * 2
    *dq, own, far = old_call(
        "attend_bwd",
        functools.partial(bwd_body, windowed),
        outs,
        [pl.BlockSpec(memory_space=pltpu.VMEM)] * 6,
        [*pieces, *grads, *mixed, lse, *mark],
        old + [False] * 4 + old[:4] + [False] * 3,
        [1] * 19,
        spot,
        [pltpu.VMEM((2 * n, HD), LOW)] * 2 + [pltpu.VMEM((2 * n, 2 * HD), F32), pltpu.VMEM((HD, TOK), F32)],
        18,
    )
    return dq, own, far


def join_body(*refs):
    dq, own, far, outs = refs[:4], refs[4], refs[5], refs[6:]
    for d in range(4):
        at = slice(TOK * d, TOK * d + TOK)
        outs[d][:, :HD] = dq[d][...]
        outs[d][:, HD:] = (own[at] + far[at]).astype(LOW)


def join_heads(dq, own, far):
    return call("join_heads", join_body, [shape((TOK, 3 * HD))] * 4, *dq, own, far)


def swap(values, axis, bits, size=4):
    if axis == Y:
        bits = (bits & 1) * 2 + (bits >> 1)
    return lax.ppermute(values, axis, [(i, i ^ bits) for i in range(size)])


def sibling(values):
    return swap(values, "core", 1, 2)


def exchange(pieces, axis):
    got = {d: swap(pieces[d], axis, d) for d in (2, 1, 3)}
    return [pieces[0], got[1], got[2], got[3]]


def gather(piece, axis):
    return exchange([piece] * 4, axis)


def four_sum(parts):
    return (parts[0].astype(F32) + parts[2].astype(F32)) + (parts[1].astype(F32) + parts[3].astype(F32))


def line_sum(values, axis):
    return four_sum(gather(values, axis))


def tie(*values):
    return lax.optimization_barrier(values)


def pick(stacked, index):
    return lax.dynamic_index_in_dim(stacked, index, 0, keepdims=False)


def layer_forward(spot, stream, pieces, matrices, vectors, mark, windowed):
    heads_matrix, up_matrix, down_matrix = matrices
    qkv_bias, up_bias, out_bias, down_bias, attn_gain, attn_shift, ffn_gain, ffn_shift = vectors
    keep, send, *heads = rows_mm("qkv", spot, pieces, heads_matrix, qkv_bias)
    rows = (keep, send)
    heads = exchange(heads, "x")
    heads = heads + [sibling(h) for h in heads]
    mixed, lse = attend_fwd(spot, heads, mark, windowed)
    *branch, attended = scatter_mm(spot, exchange(mixed, "x"), heads_matrix, 512, 1536)
    normed, scale, first, low = norm(exchange(branch, "z"), stream, out_bias, attn_gain, attn_shift)
    loaded = load(up_matrix) if windowed else up_matrix
    keep, send, active, slope = rows_mm("up", spot, gather(low, "z"), loaded, up_bias)
    if windowed:
        down_matrix = load(up_matrix, 2048)
    second = scatter_mm(spot, [active], down_matrix, 2048, 0)
    normed_two, scale_two, result, low = norm(exchange(second, "z"), first, down_bias, ffn_gain, ffn_shift)
    saved = (heads, mixed, lse, normed, scale, slope, normed_two, scale_two)
    far = [sibling(part) for part in (rows[1], attended, send, active)]
    low, *far = tie(low, *far)
    sides = (rows[0], far[0]), (attended, far[1]), (keep, far[2]), (active, far[3])
    return result, low, saved, sides, (heads_matrix, loaded, down_matrix)


FRESH_LEFTS = [False] * 2 + [True] * 6
FRESH_RIGHTS = [True] * 4 + [False] * 2 + [True] * 2


def layer_backward(spot, parts, base, saved, sides, matrices, vectors, mark, windowed, earlier=None, before=(), sums_two=None, turn=None):
    heads_matrix, up_matrix, down_matrix = matrices
    attn_gain, ffn_gain = vectors[4], vectors[6]
    heads, mixed, lse, normed, scale, slope, normed_two, scale_two = saved
    rows, attended, first_rows, active = sides
    last = earlier is not None
    grad_summed, low, ffn_sums = norm_back(parts, base, normed_two, scale_two, ffn_gain)
    keep, send, grad_up, up_sums = rows_mm("slope", spot, gather(low, "z"), down_matrix, slope)
    down_pair = (keep, sibling(send)), active
    up_pair = first_rows, (grad_up, sibling(grad_up))
    if last:
        down_term = weight_term(spot, *two_layers(down_pair, earlier[3]), FRESH_LEFTS)
        grad_up, down_term = tie(grad_up, down_term)
    parts = exchange(scatter_mm(spot, [grad_up], up_matrix, 2048, 0), "z")
    if last:
        down_sum = lax.psum_scatter(down_term, ("ylo", "x"), scatter_dimension=0, tiled=True)
        up_term = weight_term(spot, *two_layers(up_pair, earlier[2]), FRESH_RIGHTS)
    under = (ffn_sums, sums_two[0]) if last else ()
    grad_residual, low, attn_sums = norm_back(parts, grad_summed, normed, scale, attn_gain, under)
    if last:
        low, up_term = tie(low, up_term)
        up_sum = lax.psum_scatter(up_term, ("ylo", "x"), scatter_dimension=0, tiled=True)
    sums = (jnp.concatenate([attn_sums, ffn_sums]), up_sums)
    keep, send, *grad_heads = rows_mm("heads", spot, gather(low, "z"), heads_matrix)
    if last:
        *grad_heads, own_sums = grad_heads
        hidden_sums = by_yhi((up_sums + sums_two[1]).reshape(2, 1024), spot[4])
        sums = jnp.concatenate([own_sums[:6].reshape(24, 512), hidden_sums.reshape(4, 512)])
    out_pair = (keep, sibling(send)), attended
    grad_heads = exchange(grad_heads, "x")
    grad_heads[3], *before = tie(grad_heads[3], *before)
    grad_queries, own_terms, far_terms = attend_bwd(spot, heads, grad_heads, mixed, lse, mark, windowed)
    grad_parts = exchange(join_heads(grad_queries, own_terms, sibling(far_terms)), "x")
    *partial, grad_packed = scatter_mm(spot, grad_parts, heads_matrix, 1536, 0)
    qkv_pair = rows, (grad_packed, sibling(grad_packed))
    if not last:
        return exchange(partial, "z"), grad_residual, (qkv_pair, out_pair, up_pair, down_pair), sums, before
    sides = [*two_layers(qkv_pair, earlier[0]), *two_layers(out_pair, earlier[1])]
    rest, line = head_terms(spot, sides, FRESH_RIGHTS + FRESH_LEFTS)
    rest, line, *partial = tie(rest, line, *partial)
    rest = lax.psum_scatter(rest, "x", scatter_dimension=0, tiled=True)
    low = (four_sum(exchange(partial, "z")) + grad_residual).astype(LOW)
    same, other = turn(low)
    heads = line.reshape(2, 2, 3, 128)
    heads = jnp.stack([by_yhi(heads[j], spot[4]) for j in range(2)]).reshape(3, 512)
    sums = jnp.concatenate([sums, heads, jnp.zeros((1, 512), F32)])
    sums = line_sum(line_sum(sums + sibling(sums), "x"), Y).reshape(-1)
    result = gather(by_micro(spot[4], same, other), "z")
    far = [swap(total[:, 1024:], "yhi", 1, 2) for total in (up_sum, down_sum)]
    rest, *far = tie(rest, *far)
    rest = heads_result(exchange(cut(spot, rest), Y))
    return settle(spot, result), (*rest, *hidden_result(up_sum, far[0], down_sum, far[1])), sums


def two_layers(one, two):
    return list(one[0]) + list(two[0]), list(one[1]) + list(two[1])


def turn_same(core, ylo, values):
    got = lax.ppermute(values, ("core", "ylo"), [(1, 2), (2, 1)])
    return jnp.where(core == ylo, values, got)


def turn_other(values):
    perm = [(c * 4 + l * 2 + h, l * 4 + c * 2 + 1 - h) for c in range(2) for l in range(2) for h in range(2)]
    return lax.ppermute(values, ("core", "ylo", "yhi"), perm)


def by_micro(yhi, same, other):
    return jnp.stack([jnp.where(yhi == 0, same, other), jnp.where(yhi == 0, other, same)])


def by_yhi(values, yhi):
    return jnp.where(yhi == 0, values, values[::-1])


def shards(
    inputs,
    cotangent,
    segments,
    query_weight,
    key_weight,
    value_weight,
    out_weight,
    up_weight,
    down_weight,
    query_bias,
    value_bias,
    out_bias,
    up_bias,
    down_bias,
    attn_gain,
    attn_shift,
    ffn_gain,
    ffn_shift,
):
    core, ylo, x, yhi, z = (lax.axis_index(name) for name in AXES)
    spot = jnp.stack([x, core, ylo, z, yhi]).astype(jnp.int32)
    local = pack(pack_heads_body, 1024, query_weight, key_weight, value_weight, out_weight)
    parts = gather(local, Y)
    *parts, inputs, down_weight = tie(*parts, inputs, down_weight)

    def gathered(heads, parts):
        return lax.all_gather(pair(heads, spot, parts), ("core", "x"), axis=0, tiled=True)

    heads_matrix = gathered(True, parts)
    own_rows = turn_same(core, ylo, pick(pick(inputs, yhi)[0].reshape(4, OWN, D), z))
    pieces = gather(own_rows, "z")
    *pieces, up_weight = tie(*pieces, up_weight)
    hidden_matrix = gathered(False, gather(up_weight, Y) + gather(pack(turn_body, 1024, down_weight), Y))
    matrices = (load(heads_matrix), hidden_matrix, None)
    bias_own = jnp.concatenate([query_bias, value_bias, up_bias])
    bias = (bias_own, swap(bias_own, "yhi", 1, 2))
    none = jnp.zeros((128,), F32)
    qkv_bias = jnp.concatenate(
        [
            part
            for j in range(2)
            for h in range(2)
            for part in (bias[h][128 * j : 128 * j + 128], none, bias[h][256 + 128 * j : 384 + 128 * j])
        ]
    )
    up_all = jnp.concatenate([bias[h][512:] for h in range(2)])
    vectors = (qkv_bias, up_all, out_bias, down_bias, attn_gain, attn_shift, ffn_gain, ffn_shift)
    vectors = tuple(v[None] for v in vectors)
    top_grad = turn_same(core, ylo, pick(pick(cotangent, yhi)[0].reshape(4, OWN, D), z)).astype(F32)
    seg_here = pick(segments, yhi)[0].astype(F32)
    mark = marks(spot, jnp.where(core == ylo, seg_here, sibling(seg_here)))
    middle, low, saved_one, sides_one, matrices = layer_forward(
        spot, own_rows.astype(F32), pieces, matrices, vectors, mark, True
    )
    _, low, saved_two, sides_two, _ = layer_forward(spot, middle, gather(low, "z"), matrices, vectors, mark, False)
    parts, base, pairs, sums_two, result = layer_backward(
        spot, [], top_grad, saved_two, sides_two, matrices, vectors, mark, False, None, gather(low, "z")
    )
    result = settle(spot, result)
    same, other = turn_same(core, ylo, result), turn_other(result)
    parts[0], same, other = tie(parts[0], same, other)

    def turn(low):
        return turn_same(core, ylo, low), turn_other(low)

    input_grad, matrix_grads, sums = layer_backward(
        spot, parts, base, saved_one, sides_one, matrices, vectors, mark, True, pairs, (), sums_two, turn
    )
    own = sums[: 6 * D].reshape(6, D)
    heads = sums[7 * D : 7 * D + 1536].reshape(2, 2, 3, 128)
    heads = lax.dynamic_index_in_dim(heads, yhi, 1, keepdims=False)
    return (
        by_micro(yhi, same, other)[:, None],
        input_grad[:, None],
        *matrix_grads,
        heads[:, 0].reshape(-1),
        heads[:, 2].reshape(-1),
        own[2],
        pick(sums[6 * D : 7 * D].reshape(2, 1024), yhi),
        own[5],
        own[0],
        own[1],
        own[3],
        own[4],
    )


def solution(mesh):
    split = Mesh(mesh.devices.reshape(2, 2, 4, 2, 4), AXES)
    token = P(None, "core", ("ylo", "x"), None)
    inner = P(("core", "ylo", "x"), ("yhi", "z"))
    outer = P(("yhi", "z"), ("core", "ylo", "x"))
    unit = P(("yhi", "z"))
    matrix = (inner, inner, inner, outer, inner, outer)
    vector = (unit, unit, P(), unit, P(), P(), P(), P(), P())
    in_specs = (token, token, P(None, "core", None)) + matrix + vector
    out_specs = (token, token) + matrix + vector
    return jax.shard_map(shards, mesh=split, in_specs=in_specs, out_specs=out_specs, check_vma=False)
```

time: 784 us -> 684 us (0.87)
  local copies, waits for them, and re-layouts: 79.9 us -> 37.1 us
  waiting for transfers between devices: 308 us -> 291 us
  between operations: 32 us -> 15.8 us
  other arithmetic: 21.2 us -> 5.62 us
  Pallas kernels: 132 us -> 124 us
    unnamed x299 -> x220, local copies, waits for them, and re-layouts: 67.3 us -> 31.3 us
    ppermute x122 -> x127, waiting for transfers between devices: 274 us -> 253 us  [swap(): return lax.ppermute(values, axis, [(i, i ^ bits) for i in range(size)])]
    all_gather x3 -> x2, waiting for transfers between devices: 12.6 us -> 24.6 us  [gathered(): lax.all_gather(pair(heads, spot, parts), ('core', 'x'), axis=0, tiled=True)]
    reduce_sum x16 -> x0, other arithmetic: 10.3 us -> none  [the longest x4 4.51 us: norm_back(): terms = (jnp.sum(grad * normed, axis=0), jnp.sum(grad, axis=0))]
    ppermute x122 -> x127, starting transfers between devices: 175 us -> 185 us  [swap(): return lax.ppermute(values, axis, [(i, i ^ bits) for i in range(size)])]
    ppermute x4, waiting for transfers between devices: 16.1 us -> 7.19 us  [turn_same(): got = lax.ppermute(values, ('core', 'ylo'), [(1, 2), (2, 1)])]
    pallas_call x32 -> x46, Pallas kernels: 132 us -> 124 us  [the longest x38 70.6 us: call(): pl.pallas_call(body, in_specs=specs, out_specs=[pl.BlockSpec(memory_space...]
  transfers between devices with their start and end apart: 134 -> 138, of which waited for: 75 -> 79; matrix products, arithmetic and copies ran while one was open for 4% -> 2% of each run, Pallas kernels for 11% -> 13%
where the time goes in v2:
time: 684 us; the launch traced here: 675 us
  waiting for transfers between devices  291 us (43%)
  starting transfers between devices  201 us (29%)
  Pallas kernels  124 us (18%)
  local copies, waits for them, and re-layouts  37.1 us (5%)
  between operations  15.8 us (2%)
    ppermute x127, waiting for transfers between devices, swap(): return lax.ppermute(values, axis, [(i, i ^ bits) for i in range(size)])  253 us
    ppermute x127, starting transfers between devices, swap(): return lax.ppermute(values, axis, [(i, i ^ bits) for i in range(size)])  185 us
    pallas_call x38, Pallas kernels, call(): pl.pallas_call(body, in_specs=specs, out_specs=[pl.BlockSpec(memory_space...  70.6 us
    pallas_call x5, Pallas kernels, old_call(): pl.pallas_call(inner, in_specs=[pl.BlockSpec(memory_space=pltpu.SMEM)] +...  42.3 us
    unnamed x220, local copies, waits for them, and re-layouts  31.3 us
    all_gather x2, waiting for transfers between devices, gathered(): lax.all_gather(pair(heads, spot, parts), ('core', 'x'), axis=0, tiled=True)  24.6 us
  transfers between devices with their start and end apart: 138, of which 79 were waited for; matrix products, arithmetic and copies ran while one was open for 2% of the time, Pallas kernels for 13%

profile of v2, /device:TPU:1, one launch (start us, length us, event | category | flops | bytes accessed | tf_op | source)
XLA Modules:
  0.0 675.0 jit_solution(11696741631319429027)
XLA Ops:
  18.7 8.4 %collective-permute-done.1.refs_2_ = bf16[128,1024]{1,0:T(8,128)(2,1)S(1)} collective-permute-done((bf16[128,1024]{1,0:T(8,128)(2,1)S(1)}, bf16[128,1024]{1,0:T(8,128)(2,1)S(1)}, u32[]{:S(2)}, u32[]{:S(2)}) %collective-permute-start.1) | collective-permute-done | bytes 262176 | tf_op jit(solution)/shard_map/ppermute | solution.py:620
  35.4 5.4 collective-permute-done.3
  43.6 3.3 collective-permute-start.5
  50.9 3.5 collective-permute-done.5.p2
  58.0 3.4 collective-permute-start.27
  62.5 4.3 collective-permute-done.25.refs_1_
  66.8 3.8 collective-permute-done.26.refs_2_
  70.6 3.6 collective-permute-done.27.refs_3_
  77.5 3.5 collective-permute-done.7
  82.2 3.5 load.3.w.refs_4_
  98.4 5.2 collective-permute-start.13
  103.6 4.2 collective-permute-start.14
  109.0 5.4 attend_fwd.2
  120.4 3.6 collective-permute-done.17.refs_2_
  125.4 3.4 copy-done.3
  137.7 7.8 %collective-permute-done.20.refs_2_ = bf16[64,2048]{1,0:T(8,128)(2,1)S(1)} collective-permute-done((bf16[64,2048]{1,0:T(8,128)(2,1)S(1)}, bf16[64,2048]{1,0:T(8,128)(2,1)S(1)}, u32[]{:S(2)}, u32[]{:S(2)}) %collective-permute-start.20) | collective-permute-done | bytes 262176 | tf_op jit(solution)/shard_map/ppermute | solution.py:620
  152.5 23.5 %all-gather.5.cloned.1.call-done.source = bf16[2048,4096]{1,0:T(8,128)(2,1)} async-done(((bf16[256,4096]{1,0:T(8,128)(2,1)}), bf16[2048,4096]{1,0:T(8,128)(2,1)}) %all-gather.5.cloned.1.call-update) | async-done | bytes 16777232 | tf_op jit(solution)/shard_map/all_gather | solution.py:782
  175.9 3.5 load.4.w.refs_1_
  179.5 4.1 rows_up.2
  184.2 4.3 load.5.refs_1_.w
  196.4 3.8 collective-permute-done.31.refs_1_
  202.1 5.4 collective-permute-done.32.refs_2_
  208.6 5.0 collective-permute-done.33.refs_3_
  218.0 3.5 collective-permute-done.38.p1
  221.6 5.9 collective-permute-done.39.p2
  248.0 6.2 attend_fwd.3
  254.3 3.2 collective-permute-start.50
  263.4 3.4 collective-permute-start.53
  269.3 7.5 %collective-permute-done.53.refs_2_ = bf16[64,2048]{1,0:T(8,128)(2,1)S(1)} collective-permute-done((bf16[64,2048]{1,0:T(8,128)(2,1)S(1)}, bf16[64,2048]{1,0:T(8,128)(2,1)S(1)}, u32[]{:S(2)}, u32[]{:S(2)}) %collective-permute-start.53) | collective-permute-done | bytes 262176 | tf_op jit(solution)/shard_map/ppermute | solution.py:620
  276.8 3.4 collective-permute-done.54.refs_3_
  284.6 5.8 collective-permute-start.48
  292.1 3.6 collective-permute-done.57.p3
  295.7 4.1 rows_up.3
  302.8 3.3 collective-permute-start.59
  308.5 7.5 %collective-permute-done.59.refs_2_ = bf16[64,2048]{1,0:T(8,128)(2,1)S(1)} collective-permute-done((bf16[64,2048]{1,0:T(8,128)(2,1)S(1)}, bf16[64,2048]{1,0:T(8,128)(2,1)S(1)}, u32[]{:S(2)}, u32[]{:S(2)}) %collective-permute-start.59) | collective-permute-done | bytes 262176 | tf_op jit(solution)/shard_map/ppermute | solution.py:620
  316.0 3.6 collective-permute-done.60.refs_3_
  328.7 4.6 collective-permute-done.62.p2
  333.2 3.6 collective-permute-done.63.p3
  345.6 3.6 collective-permute-start.65
  349.7 3.6 collective-permute-start.75
  359.3 3.4 collective-permute-done.66.refs_3_
  371.5 5.4 collective-permute-done.68.p2
  381.6 3.7 collective-permute-done.72.refs_11_
  390.2 6.5 attend_bwd.2
  396.8 6.9 %collective-permute-start.80 = (f32[1024,256]{1,0:T(8,128)S(1)}, f32[1024,256]{1,0:T(8,128)S(1)}, u32[]{:S(2)}, u32[]{:S(2)}) collective-permute-start(f32[1024,256]{1,0:T(8,128)S(1)} %get-tuple-element.292), channel_id=1, source_target_pairs={{0,64},{64,0},{1,65},{65,1},{2,66},{66,2},{3,67},{67,3},{4,68},{68... | collective-permute-start | bytes 3145736 | tf_op jit(solution)/shard_map/ppermute | solution.py:620
  416.7 4.5 collective-permute-done.82.refs_2_
  434.6 7.2 %collective-permute-done.87.refs_2_ = bf16[64,2048]{1,0:T(8,128)(2,1)S(1)} collective-permute-done((bf16[64,2048]{1,0:T(8,128)(2,1)S(1)}, bf16[64,2048]{1,0:T(8,128)(2,1)S(1)}, u32[]{:S(2)}, u32[]{:S(2)}) %collective-permute-start.87) | collective-permute-done | bytes 262176 | tf_op jit(solution)/shard_map/ppermute | solution.py:620
  450.8 6.0 collective-permute-done.90.p2
  467.3 8.5 %weight_term.2 = bf16[1024,2048]{1,0:T(8,128)(2,1)} custom-call(s32[5]{0:T(128)S(1)} %stack.50.spot.spot_ref, bf16[256,1024]{1,0:T(8,128)(2,1)S(1)} %get-tuple-element.318.refs_0_, bf16[256,1024]{1,0:T(8,128)(2,1)S(1)} %collective-permute-done.92.refs_1_, bf16[256,1024]{1,0:T(8,128)(2,1)} %copy-done.55, bf16[256,1024]{1,0:T(8,128)(2,1)} %copy-done.93, ...), custom_call_target="tpu_custom_call" | custom-call | flops 4294967296 | bytes 8388608 | tf_op jit(solution)/shard_map/weight_term/pallas_call | solution.py:280
  476.7 3.4 copy-done.6
  486.9 3.7 collective-permute-done.94.refs_1_
  490.6 7.3 %collective-permute-done.95.refs_2_ = bf16[64,2048]{1,0:T(8,128)(2,1)S(1)} collective-permute-done((bf16[64,2048]{1,0:T(8,128)(2,1)S(1)}, bf16[64,2048]{1,0:T(8,128)(2,1)S(1)}, u32[]{:S(2)}, u32[]{:S(2)}) %collective-permute-start.95) | collective-permute-done | bytes 262176 | tf_op jit(solution)/shard_map/ppermute | solution.py:620
  502.9 8.8 %weight_term.3 = bf16[1024,2048]{1,0:T(8,128)(2,1)} custom-call(s32[5]{0:T(128)S(1)} %stack.50.spot.spot_ref, bf16[256,1024]{1,0:T(8,128)(2,1)} %copy-done.50, bf16[256,1024]{1,0:T(8,128)(2,1)} %copy-done.90, bf16[256,1024]{1,0:T(8,128)(2,1)} %copy-done.51, bf16[256,1024]{1,0:T(8,128)(2,1)} %copy-done.92, ...), custom_call_target="tpu_custom_call" | custom-call | flops 4294967296 | bytes 8388608 | tf_op jit(solution)/shard_map/weight_term/pallas_call | solution.py:280
  514.6 6.5 collective-permute-done.100.p2
  521.1 8.6 %collective-permute-done.101.p3 = bf16[80,2048]{1,0:T(8,128)(2,1)S(1)} collective-permute-done((bf16[80,2048]{1,0:T(8,128)(2,1)S(1)}, bf16[80,2048]{1,0:T(8,128)(2,1)S(1)}, u32[]{:S(2)}, u32[]{:S(2)}) %collective-permute-start.101) | collective-permute-done | bytes 327712 | tf_op jit(solution)/shard_map/ppermute | solution.py:620
  529.7 3.4 copy-done.4
  541.4 3.9 collective-permute-done.103.refs_10_
  545.3 8.3 %attend_bwd.3 = (bf16[256,128]{1,0:T(8,128)(2,1)S(1)}, bf16[256,128]{1,0:T(8,128)(2,1)S(1)}, bf16[256,128]{1,0:T(8,128)(2,1)S(1)}, bf16[256,128]{1,0:T(8,128)(2,...) custom-call(s32[5]{0:T(128)S(1)} %stack.50.spot.spot_ref, bf16[256,384]{1,0:T(8,128)(2,1)} %copy-done.65, ...), custom_call_target="tpu_custom_call" | custom-call | flops 4294967296 | bytes 8388608 | tf_op jit(solution)/shard_map/attend_bwd/pallas_call | solution.py:280
  563.2 6.1 collective-permute-done.106.refs_1_
  569.3 9.4 %collective-permute-done.107.refs_2_ = bf16[256,384]{1,0:T(8,128)(2,1)S(1)} collective-permute-done((bf16[256,384]{1,0:T(8,128)(2,1)S(1)}, bf16[256,384]{1,0:T(8,128)(2,1)S(1)}, u32[]{:S(2)}, u32[]{:S(2)}) %collective-permute-start.107) | collective-permute-done | bytes 196640 | tf_op jit(solution)/shard_map/ppermute | solution.py:620
  586.5 10.2 %head_terms.1 = (bf16[1024,2048]{1,0:T(8,128)(2,1)S(1)}, f32[1,1536]{1,0:T(1,128)S(1)}) custom-call(s32[5]{0:T(128)S(1)} %stack.50.spot.spot_ref, bf16[256,1024]{1,0:T(8,128)(2,1)} %copy-done.48, bf16[256,1024]{1,0:T(8,128)(2,1)} %copy-done.89, bf16[256,1024]{1,0:T(8,128)(2,1)} %copy-done.49, bf16[256,1024]{1,0:T(8,128)(2,1)} %copy-done.91, ...), custom_call_target="tpu_custom_call" | custom-call | flops 4294967296 | bytes 8388608 | tf_op jit(solution)/shard_map/head_terms/pallas_call | solution.py:280
  624.1 5.7 collective-permute-done.117
  639.9 5.2 collective-permute-done.122.down_far
  645.0 4.0 collective-permute-done.121.up_far
  (534 shorter events, 314.4 us)
Async XLA Ops:
  7.2 75.0 %all-gather.3.cloned.1.call-start = ((), (), s32[]{:S(2)}) async-start(), calls=%async_computation.3 | async-start | bytes 9437184 | tf_op jit(solution)/shard_map/all_gather | solution.py:782
  13.0 14.0 %collective-permute-start.1 = (bf16[128,1024]{1,0:T(8,128)(2,1)S(1)}, bf16[128,1024]{1,0:T(8,128)(2,1)S(1)}, u32[]{:S(2)}, u32[]{:S(2)}) collective-permute-start(bf16[128,1024]{1,0:T(8,128)(2,1)S(1)} %pack.2.refs_0_), channel_id=1, source_target_pairs={{0,4},{4,0},{32,36},{36,32},{1,5},{5,1},{33,37},{37,33},{2,6},{6,2... | collective-permute-start | bytes 786440 | tf_op jit(solution)/shard_map/ppermute | solution.py:620
  15.7 13.4 %collective-permute-start.2 = (bf16[128,1024]{1,0:T(8,128)(2,1)S(1)}, bf16[128,1024]{1,0:T(8,128)(2,1)S(1)}, u32[]{:S(2)}, u32[]{:S(2)}) collective-permute-start(bf16[128,1024]{1,0:T(8,128)(2,1)S(1)} %pack.2.refs_0_), channel_id=1, source_target_pairs={{0,36},{4,32},{32,4},{36,0},{1,37},{5,33},{33,5},{37,1},{2,38},{6,... | collective-permute-start | bytes 786440 | tf_op jit(solution)/shard_map/ppermute | solution.py:620
  30.7 145.2 %all-gather.5.cloned.1.call-start = ((), (), s32[]{:S(2)}) async-start(), calls=%async_computation.4 | async-start | bytes 18874368 | tf_op jit(solution)/shard_map/all_gather | solution.py:782
  47.1 14.4 %collective-permute-start.29 = (bf16[128,1024]{1,0:T(8,128)(2,1)S(1)}, bf16[128,1024]{1,0:T(8,128)(2,1)S(1)}, u32[]{:S(2)}, u32[]{:S(2)}) collective-permute-start(bf16[128,1024]{1,0:T(8,128)(2,1)S(1)} %pack.3.refs_4_), channel_id=1, source_target_pairs={{0,4},{4,0},{32,36},{36,32},{1,5},{5,1},{33,37},{37,33},{2,6},{6,2... | collective-permute-start | bytes 786440 | tf_op jit(solution)/shard_map/ppermute | solution.py:620
  48.9 13.5 %collective-permute-start.30 = (bf16[128,1024]{1,0:T(8,128)(2,1)S(1)}, bf16[128,1024]{1,0:T(8,128)(2,1)S(1)}, u32[]{:S(2)}, u32[]{:S(2)}) collective-permute-start(bf16[128,1024]{1,0:T(8,128)(2,1)S(1)} %pack.3.refs_4_), channel_id=1, source_target_pairs={{0,36},{4,32},{32,4},{36,0},{1,37},{5,33},{33,5},{37,1},{2,38},{6,... | collective-permute-start | bytes 786440 | tf_op jit(solution)/shard_map/ppermute | solution.py:620
  58.0 16.2 %collective-permute-start.27 = (bf16[128,1024]{1,0:T(8,128)(2,1)S(1)}, bf16[128,1024]{1,0:T(8,128)(2,1)S(1)}, u32[]{:S(2)}, u32[]{:S(2)}) collective-permute-start(bf16[128,1024]{1,0:T(8,128)(2,1)S(1)} %copy-done.20), channel_id=1, source_target_pairs={{0,36},{4,32},{32,4},{36,0},{1,37},{5,33},{33,5},{37,1},{2,38},{6,... | collective-permute-start | bytes 786440 | tf_op jit(solution)/shard_map/ppermute | solution.py:620
  76.2 557.9 %reduce-scatter.8.cloned.1.call-start = ((), (), s32[]{:S(2)}) async-start(), calls=%async_computation.7 | async-start | bytes 4718592 | tf_op jit(solution)/shard_map/reduce_scatter | solution.py:694
  92.9 14.9 %collective-permute-start.15 = (f32[2048]{0:T(1024)S(1)}, f32[2048]{0:T(1024)S(1)}, u32[]{:S(2)}, u32[]{:S(2)}) collective-permute-start(f32[2048]{0:T(1024)S(1)} %bitcast.91), channel_id=1, source_target_pairs={{0,64},{64,0},{1,65},{65,1},{2,66},{66,2},{3,67},{67,3},{4,68},{68... | collective-permute-start | bytes 24584 | tf_op jit(solution)/shard_map/ppermute | solution.py:620
  95.4 13.5 %collective-permute-start.11 = (bf16[256,384]{1,0:T(8,128)(2,1)S(1)}, bf16[256,384]{1,0:T(8,128)(2,1)S(1)}, u32[]{:S(2)}, u32[]{:S(2)}) collective-permute-start(bf16[256,384]{1,0:T(8,128)(2,1)S(1)} %get-tuple-element.215.refs_0_), channel_id=1, source_target_pairs={{0,64},{64,0},{1,65},{65,1},{2,66},{66,2},{3,67},{67,3},{4,68},{68... | collective-permute-start | bytes 589832 | tf_op jit(solution)/shard_map/ppermute | solution.py:620
  95.5 13.5 %collective-permute-start.12 = (bf16[256,384]{1,0:T(8,128)(2,1)S(1)}, bf16[256,384]{1,0:T(8,128)(2,1)S(1)}, u32[]{:S(2)}, u32[]{:S(2)}) collective-permute-start(bf16[256,384]{1,0:T(8,128)(2,1)S(1)} %collective-permute-done.8.refs_1_), channel_id=1, source_target_pairs={{0,64},{64,0},{1,65},{65,1},{2,66},{66,2},{3,67},{67,3},{4,68},{68... | collective-permute-start | bytes 589832 | tf_op jit(solution)/shard_map/ppermute | solution.py:620
  132.4 13.1 %collective-permute-start.20 = (bf16[64,2048]{1,0:T(8,128)(2,1)S(1)}, bf16[64,2048]{1,0:T(8,128)(2,1)S(1)}, u32[]{:S(2)}, u32[]{:S(2)}) collective-permute-start(bf16[64,2048]{1,0:T(8,128)(2,1)S(1)} %get-tuple-element.227), channel_id=1, source_target_pairs={{0,2},{1,3},{2,0},{3,1},{4,6},{5,7},{6,4},{7,5},{8,10},{9,11},{10,... | collective-permute-start | bytes 786440 | tf_op jit(solution)/shard_map/ppermute | solution.py:620
  134.6 13.5 %collective-permute-start.21 = (bf16[64,2048]{1,0:T(8,128)(2,1)S(1)}, bf16[64,2048]{1,0:T(8,128)(2,1)S(1)}, u32[]{:S(2)}, u32[]{:S(2)}) collective-permute-start(bf16[64,2048]{1,0:T(8,128)(2,1)S(1)} %get-tuple-element.228), channel_id=1, source_target_pairs={{0,3},{1,2},{2,1},{3,0},{4,7},{5,6},{6,5},{7,4},{8,11},{9,10},{10,... | collective-permute-start | bytes 786440 | tf_op jit(solution)/shard_map/ppermute | solution.py:620
  148.5 30.9 %collective-permute-start.22 = (bf16[64,2048]{1,0:T(8,128)(2,1)S(1)}, bf16[64,2048]{1,0:T(8,128)(2,1)S(1)}, u32[]{:S(2)}, u32[]{:S(2)}) collective-permute-start(bf16[64,2048]{1,0:T(8,128)(2,1)S(1)} %get-tuple-element.229.p0), channel_id=1, source_target_pairs={{0,1},{1,0},{2,3},{3,2},{4,5},{5,4},{6,7},{7,6},{8,9},{9,8},{10,11... | collective-permute-start | bytes 786440 | tf_op jit(solution)/shard_map/ppermute | solution.py:620
  148.6 30.9 %collective-permute-start.23 = (bf16[64,2048]{1,0:T(8,128)(2,1)S(1)}, bf16[64,2048]{1,0:T(8,128)(2,1)S(1)}, u32[]{:S(2)}, u32[]{:S(2)}) collective-permute-start(bf16[64,2048]{1,0:T(8,128)(2,1)S(1)} %get-tuple-element.229.p0), channel_id=1, source_target_pairs={{0,2},{1,3},{2,0},{3,1},{4,6},{5,7},{6,4},{7,5},{8,10},{9,11},{10,... | collective-permute-start | bytes 786440 | tf_op jit(solution)/shard_map/ppermute | solution.py:620
  149.9 29.6 %collective-permute-start.24 = (bf16[64,2048]{1,0:T(8,128)(2,1)S(1)}, bf16[64,2048]{1,0:T(8,128)(2,1)S(1)}, u32[]{:S(2)}, u32[]{:S(2)}) collective-permute-start(bf16[64,2048]{1,0:T(8,128)(2,1)S(1)} %get-tuple-element.229.p0), channel_id=1, source_target_pairs={{0,3},{1,2},{2,1},{3,0},{4,7},{5,6},{6,5},{7,4},{8,11},{9,10},{10,... | collective-permute-start | bytes 786440 | tf_op jit(solution)/shard_map/ppermute | solution.py:620
  183.7 30.4 %collective-permute-start.37 = (bf16[256,2048]{1,0:T(8,128)(2,1)S(1)}, bf16[256,2048]{1,0:T(8,128)(2,1)S(1)}, u32[]{:S(2)}, u32[]{:S(2)}) collective-permute-start(bf16[256,2048]{1,0:T(8,128)(2,1)S(1)} %get-tuple-element.232.refs_0_.refs_4_), channel_id=1, source_target_pairs={{0,64},{64,0},{1,65},{65,1},{2,66},{66,2},{3,67},{67,3},{4,68},{68... | collective-permute-start | bytes 3145736 | tf_op jit(solution)/shard_map/ppermute | solution.py:620
  193.7 13.7 %collective-permute-start.32 = (bf16[64,2048]{1,0:T(8,128)(2,1)S(1)}, bf16[64,2048]{1,0:T(8,128)(2,1)S(1)}, u32[]{:S(2)}, u32[]{:S(2)}) collective-permute-start(bf16[64,2048]{1,0:T(8,128)(2,1)S(1)} %get-tuple-element.235), channel_id=1, source_target_pairs={{0,2},{1,3},{2,0},{3,1},{4,6},{5,7},{6,4},{7,5},{8,10},{9,11},{10,... | collective-permute-start | bytes 786440 | tf_op jit(solution)/shard_map/ppermute | solution.py:620
  195.6 18.4 %collective-permute-start.34 = (bf16[256,1024]{1,0:T(8,128)(2,1)S(1)}, bf16[256,1024]{1,0:T(8,128)(2,1)S(1)}, u32[]{:S(2)}, u32[]{:S(2)}) collective-permute-start(bf16[256,1024]{1,0:T(8,128)(2,1)S(1)} %copy-done.57), channel_id=1, source_target_pairs={{0,64},{64,0},{1,65},{65,1},{2,66},{66,2},{3,67},{67,3},{4,68},{68... | collective-permute-start | bytes 1572872 | tf_op jit(solution)/shard_map/ppermute | solution.py:620
  196.4 17.6 %collective-permute-start.36 = (bf16[256,1024]{1,0:T(8,128)(2,1)S(1)}, bf16[256,1024]{1,0:T(8,128)(2,1)S(1)}, u32[]{:S(2)}, u32[]{:S(2)}) collective-permute-start(bf16[256,1024]{1,0:T(8,128)(2,1)S(1)} %get-tuple-element.241), channel_id=1, source_target_pairs={{0,64},{64,0},{1,65},{65,1},{2,66},{66,2},{3,67},{67,3},{4,68},{68... | collective-permute-start | bytes 1572872 | tf_op jit(solution)/shard_map/ppermute | solution.py:620
  200.2 13.4 %collective-permute-start.33 = (bf16[64,2048]{1,0:T(8,128)(2,1)S(1)}, bf16[64,2048]{1,0:T(8,128)(2,1)S(1)}, u32[]{:S(2)}, u32[]{:S(2)}) collective-permute-start(bf16[64,2048]{1,0:T(8,128)(2,1)S(1)} %get-tuple-element.236), channel_id=1, source_target_pairs={{0,3},{1,2},{2,1},{3,0},{4,7},{5,6},{6,5},{7,4},{8,11},{9,10},{10,... | collective-permute-start | bytes 786440 | tf_op jit(solution)/shard_map/ppermute | solution.py:620
  214.2 13.2 %collective-permute-start.39 = (bf16[64,2048]{1,0:T(8,128)(2,1)S(1)}, bf16[64,2048]{1,0:T(8,128)(2,1)S(1)}, u32[]{:S(2)}, u32[]{:S(2)}) collective-permute-start(bf16[64,2048]{1,0:T(8,128)(2,1)S(1)} %get-tuple-element.242.p0), channel_id=1, source_target_pairs={{0,2},{1,3},{2,0},{3,1},{4,6},{5,7},{6,4},{7,5},{8,10},{9,11},{10,... | collective-permute-start | bytes 786440 | tf_op jit(solution)/shard_map/ppermute | solution.py:620
  215.9 13.6 %collective-permute-start.40 = (bf16[64,2048]{1,0:T(8,128)(2,1)S(1)}, bf16[64,2048]{1,0:T(8,128)(2,1)S(1)}, u32[]{:S(2)}, u32[]{:S(2)}) collective-permute-start(bf16[64,2048]{1,0:T(8,128)(2,1)S(1)} %get-tuple-element.242.p0), channel_id=1, source_target_pairs={{0,3},{1,2},{2,1},{3,0},{4,7},{5,6},{6,5},{7,4},{8,11},{9,10},{10,... | collective-permute-start | bytes 786440 | tf_op jit(solution)/shard_map/ppermute | solution.py:620
  263.4 13.3 %collective-permute-start.53 = (bf16[64,2048]{1,0:T(8,128)(2,1)S(1)}, bf16[64,2048]{1,0:T(8,128)(2,1)S(1)}, u32[]{:S(2)}, u32[]{:S(2)}) collective-permute-start(bf16[64,2048]{1,0:T(8,128)(2,1)S(1)} %get-tuple-element.253), channel_id=1, source_target_pairs={{0,2},{1,3},{2,0},{3,1},{4,6},{5,7},{6,4},{7,5},{8,10},{9,11},{10,... | collective-permute-start | bytes 786440 | tf_op jit(solution)/shard_map/ppermute | solution.py:620
  266.8 13.4 %collective-permute-start.54 = (bf16[64,2048]{1,0:T(8,128)(2,1)S(1)}, bf16[64,2048]{1,0:T(8,128)(2,1)S(1)}, u32[]{:S(2)}, u32[]{:S(2)}) collective-permute-start(bf16[64,2048]{1,0:T(8,128)(2,1)S(1)} %get-tuple-element.254), channel_id=1, source_target_pairs={{0,3},{1,2},{2,1},{3,0},{4,7},{5,6},{6,5},{7,4},{8,11},{9,10},{10,... | collective-permute-start | bytes 786440 | tf_op jit(solution)/shard_map/ppermute | solution.py:620
  282.3 13.4 %collective-permute-start.57 = (bf16[64,2048]{1,0:T(8,128)(2,1)S(1)}, bf16[64,2048]{1,0:T(8,128)(2,1)S(1)}, u32[]{:S(2)}, u32[]{:S(2)}) collective-permute-start(bf16[64,2048]{1,0:T(8,128)(2,1)S(1)} %get-tuple-element.256.p0), channel_id=1, source_target_pairs={{0,3},{1,2},{2,1},{3,0},{4,7},{5,6},{6,5},{7,4},{8,11},{9,10},{10,... | collective-permute-start | bytes 786440 | tf_op jit(solution)/shard_map/ppermute | solution.py:620
  284.6 22.1 %collective-permute-start.48 = (bf16[64,2048]{1,0:T(8,128)(2,1)S(1)}, bf16[64,2048]{1,0:T(8,128)(2,1)S(1)}, u32[]{:S(2)}, u32[]{:S(2)}) collective-permute-start(bf16[64,2048]{1,0:T(8,128)(2,1)S(1)} %dynamic-slice_bitcast_fusion), channel_id=1, source_target_pairs={{32,64},{64,32},{33,65},{65,33},{34,66},{66,34},{35,67},{67,35},{3... | collective-permute-start | bytes 786440 | tf_op jit(solution)/shard_map/ppermute | solution.py:738
  306.2 13.4 %collective-permute-start.60 = (bf16[64,2048]{1,0:T(8,128)(2,1)S(1)}, bf16[64,2048]{1,0:T(8,128)(2,1)S(1)}, u32[]{:S(2)}, u32[]{:S(2)}) collective-permute-start(bf16[64,2048]{1,0:T(8,128)(2,1)S(1)} %get-tuple-element.261), channel_id=1, source_target_pairs={{0,3},{1,2},{2,1},{3,0},{4,7},{5,6},{6,5},{7,4},{8,11},{9,10},{10,... | collective-permute-start | bytes 786440 | tf_op jit(solution)/shard_map/ppermute | solution.py:620
  323.5 13.4 %collective-permute-start.63 = (bf16[64,2048]{1,0:T(8,128)(2,1)S(1)}, bf16[64,2048]{1,0:T(8,128)(2,1)S(1)}, u32[]{:S(2)}, u32[]{:S(2)}) collective-permute-start(bf16[64,2048]{1,0:T(8,128)(2,1)S(1)} %get-tuple-element.265.p0), channel_id=1, source_target_pairs={{0,3},{1,2},{2,1},{3,0},{4,7},{5,6},{6,5},{7,4},{8,11},{9,10},{10,... | collective-permute-start | bytes 786440 | tf_op jit(solution)/shard_map/ppermute | solution.py:620
  325.7 41.6 %collective-permute-start.76 = (bf16[256,2048]{1,0:T(8,128)(2,1)S(1)}, bf16[256,2048]{1,0:T(8,128)(2,1)S(1)}, u32[]{:S(2)}, u32[]{:S(2)}) collective-permute-start(bf16[256,2048]{1,0:T(8,128)(2,1)S(1)} %get-tuple-element.257.refs_0_.refs_6_), channel_id=1, source_target_pairs={{0,64},{64,0},{1,65},{65,1},{2,66},{66,2},{3,67},{67,3},{4,68},{68... | collective-permute-start | bytes 3145736 | tf_op jit(solution)/shard_map/ppermute | solution.py:620
  343.0 20.5 %collective-permute-start.73 = (bf16[256,1024]{1,0:T(8,128)(2,1)S(1)}, bf16[256,1024]{1,0:T(8,128)(2,1)S(1)}, u32[]{:S(2)}, u32[]{:S(2)}) collective-permute-start(bf16[256,1024]{1,0:T(8,128)(2,1)S(1)} %get-tuple-element.281), channel_id=1, source_target_pairs={{0,64},{64,0},{1,65},{65,1},{2,66},{66,2},{3,67},{67,3},{4,68},{68... | collective-permute-start | bytes 1572872 | tf_op jit(solution)/shard_map/ppermute | solution.py:620
  349.2 13.4 %collective-permute-start.66 = (bf16[64,2048]{1,0:T(8,128)(2,1)S(1)}, bf16[64,2048]{1,0:T(8,128)(2,1)S(1)}, u32[]{:S(2)}, u32[]{:S(2)}) collective-permute-start(bf16[64,2048]{1,0:T(8,128)(2,1)S(1)} %get-tuple-element.271), channel_id=1, source_target_pairs={{0,3},{1,2},{2,1},{3,0},{4,7},{5,6},{6,5},{7,4},{8,11},{9,10},{10,... | collective-permute-start | bytes 786440 | tf_op jit(solution)/shard_map/ppermute | solution.py:620
  349.7 17.6 %collective-permute-start.75 = (bf16[256,1024]{1,0:T(8,128)(2,1)S(1)}, bf16[256,1024]{1,0:T(8,128)(2,1)S(1)}, u32[]{:S(2)}, u32[]{:S(2)}) collective-permute-start(bf16[256,1024]{1,0:T(8,128)(2,1)S(1)} %get-tuple-element.283), channel_id=1, source_target_pairs={{0,64},{64,0},{1,65},{65,1},{2,66},{66,2},{3,67},{67,3},{4,68},{68... | collective-permute-start | bytes 1572872 | tf_op jit(solution)/shard_map/ppermute | solution.py:620
  363.4 13.4 %collective-permute-start.68 = (bf16[64,2048]{1,0:T(8,128)(2,1)S(1)}, bf16[64,2048]{1,0:T(8,128)(2,1)S(1)}, u32[]{:S(2)}, u32[]{:S(2)}) collective-permute-start(bf16[64,2048]{1,0:T(8,128)(2,1)S(1)} %get-tuple-element.275.p0), channel_id=1, source_target_pairs={{0,2},{1,3},{2,0},{3,1},{4,6},{5,7},{6,4},{7,5},{8,10},{9,11},{10,... | collective-permute-start | bytes 786440 | tf_op jit(solution)/shard_map/ppermute | solution.py:620
  367.3 18.0 %collective-permute-start.77 = (bf16[64,2048]{1,0:T(8,128)(2,1)S(1)}, bf16[64,2048]{1,0:T(8,128)(2,1)S(1)}, u32[]{:S(2)}, u32[]{:S(2)}) collective-permute-start(bf16[64,2048]{1,0:T(8,128)(2,1)S(1)} %get-tuple-element.298.p0), channel_id=1, source_target_pairs={{0,1},{1,0},{2,3},{3,2},{4,5},{5,4},{6,7},{7,6},{8,9},{9,8},{10,11... | collective-permute-start | bytes 786440 | tf_op jit(solution)/shard_map/ppermute | solution.py:620
  367.4 20.7 %collective-permute-start.78 = (bf16[64,2048]{1,0:T(8,128)(2,1)S(1)}, bf16[64,2048]{1,0:T(8,128)(2,1)S(1)}, u32[]{:S(2)}, u32[]{:S(2)}) collective-permute-start(bf16[64,2048]{1,0:T(8,128)(2,1)S(1)} %get-tuple-element.298.p0), channel_id=1, source_target_pairs={{0,2},{1,3},{2,0},{3,1},{4,6},{5,7},{6,4},{7,5},{8,10},{9,11},{10,... | collective-permute-start | bytes 786440 | tf_op jit(solution)/shard_map/ppermute | solution.py:620
  370.5 19.8 %collective-permute-start.79 = (bf16[64,2048]{1,0:T(8,128)(2,1)S(1)}, bf16[64,2048]{1,0:T(8,128)(2,1)S(1)}, u32[]{:S(2)}, u32[]{:S(2)}) collective-permute-start(bf16[64,2048]{1,0:T(8,128)(2,1)S(1)} %get-tuple-element.298.p0), channel_id=1, source_target_pairs={{0,3},{1,2},{2,1},{3,0},{4,7},{5,6},{6,5},{7,4},{8,11},{9,10},{10,... | collective-permute-start | bytes 786440 | tf_op jit(solution)/shard_map/ppermute | solution.py:620
  404.3 27.6 %collective-permute-start.84 = (bf16[256,2048]{1,0:T(8,128)(2,1)S(1)}, bf16[256,2048]{1,0:T(8,128)(2,1)S(1)}, u32[]{:S(2)}, u32[]{:S(2)}) collective-permute-start(bf16[256,2048]{1,0:T(8,128)(2,1)S(1)} %settle.2), channel_id=1, source_target_pairs={{32,64},{64,32},{33,65},{65,33},{34,66},{66,34},{35,67},{67,35},{3... | collective-permute-start | bytes 3145736 | tf_op jit(solution)/shard_map/ppermute | solution.py:738
  407.0 26.1 %collective-permute-start.85 = (bf16[256,2048]{1,0:T(8,128)(2,1)S(1)}, bf16[256,2048]{1,0:T(8,128)(2,1)S(1)}, u32[]{:S(2)}, u32[]{:S(2)}) collective-permute-start(bf16[256,2048]{1,0:T(8,128)(2,1)S(1)} %settle.2), channel_id=1, source_target_pairs={{0,4},{4,0},{32,68},{36,64},{64,36},{68,32},{96,100},{100,96},{1,5... | collective-permute-start | bytes 3145736 | tf_op jit(solution)/shard_map/ppermute | solution.py:744
  426.9 14.9 %collective-permute-start.87 = (bf16[64,2048]{1,0:T(8,128)(2,1)S(1)}, bf16[64,2048]{1,0:T(8,128)(2,1)S(1)}, u32[]{:S(2)}, u32[]{:S(2)}) collective-permute-start(bf16[64,2048]{1,0:T(8,128)(2,1)S(1)} %get-tuple-element.310), channel_id=1, source_target_pairs={{0,2},{1,3},{2,0},{3,1},{4,6},{5,7},{6,4},{7,5},{8,10},{9,11},{10,... | collective-permute-start | bytes 786440 | tf_op jit(solution)/shard_map/ppermute | solution.py:620
  429.9 13.9 %collective-permute-start.88 = (bf16[64,2048]{1,0:T(8,128)(2,1)S(1)}, bf16[64,2048]{1,0:T(8,128)(2,1)S(1)}, u32[]{:S(2)}, u32[]{:S(2)}) collective-permute-start(bf16[64,2048]{1,0:T(8,128)(2,1)S(1)} %get-tuple-element.311), channel_id=1, source_target_pairs={{0,3},{1,2},{2,1},{3,0},{4,7},{5,6},{6,5},{7,4},{8,11},{9,10},{10,... | collective-permute-start | bytes 786440 | tf_op jit(solution)/shard_map/ppermute | solution.py:620
  446.5 13.4 %collective-permute-start.91 = (bf16[64,2048]{1,0:T(8,128)(2,1)S(1)}, bf16[64,2048]{1,0:T(8,128)(2,1)S(1)}, u32[]{:S(2)}, u32[]{:S(2)}) collective-permute-start(bf16[64,2048]{1,0:T(8,128)(2,1)S(1)} %get-tuple-element.315.p0), channel_id=1, source_target_pairs={{0,3},{1,2},{2,1},{3,0},{4,7},{5,6},{6,5},{7,4},{8,11},{9,10},{10,... | collective-permute-start | bytes 786440 | tf_op jit(solution)/shard_map/ppermute | solution.py:620
  448.4 17.4 %collective-permute-start.93 = (bf16[256,1024]{1,0:T(8,128)(2,1)S(1)}, bf16[256,1024]{1,0:T(8,128)(2,1)S(1)}, u32[]{:S(2)}, u32[]{:S(2)}) collective-permute-start(bf16[256,1024]{1,0:T(8,128)(2,1)S(1)} %get-tuple-element.321), channel_id=1, source_target_pairs={{0,64},{64,0},{1,65},{65,1},{2,66},{66,2},{3,67},{67,3},{4,68},{68... | collective-permute-start | bytes 1572872 | tf_op jit(solution)/shard_map/ppermute | solution.py:620
  475.8 159.4 %reduce-scatter.6.cloned.1.call-start = ((), (), s32[]{:S(2)}) async-start(), calls=%async_computation.6 | async-start | bytes 4718592 | tf_op jit(solution)/shard_map/reduce_scatter | solution.py:700
  475.9 26.1 %collective-permute-start.98 = (bf16[256,2048]{1,0:T(8,128)(2,1)S(1)}, bf16[256,2048]{1,0:T(8,128)(2,1)S(1)}, u32[]{:S(2)}, u32[]{:S(2)}) collective-permute-start(bf16[256,2048]{1,0:T(8,128)(2,1)S(1)} %get-tuple-element.267.refs_0_.refs_6_), channel_id=1, source_target_pairs={{0,64},{64,0},{1,65},{65,1},{2,66},{66,2},{3,67},{67,3},{4,68},{68... | collective-permute-start | bytes 3145736 | tf_op jit(solution)/shard_map/ppermute | solution.py:620
  476.3 25.6 %collective-permute-start.97 = (bf16[256,2048]{1,0:T(8,128)(2,1)S(1)}, bf16[256,2048]{1,0:T(8,128)(2,1)S(1)}, u32[]{:S(2)}, u32[]{:S(2)}) collective-permute-start(bf16[256,2048]{1,0:T(8,128)(2,1)S(1)} %get-tuple-element.324.refs_0_.refs_4_), channel_id=1, source_target_pairs={{0,64},{64,0},{1,65},{65,1},{2,66},{66,2},{3,67},{67,3},{4,68},{68... | collective-permute-start | bytes 3145736 | tf_op jit(solution)/shard_map/ppermute | solution.py:620
  483.0 14.9 %collective-permute-start.95 = (bf16[64,2048]{1,0:T(8,128)(2,1)S(1)}, bf16[64,2048]{1,0:T(8,128)(2,1)S(1)}, u32[]{:S(2)}, u32[]{:S(2)}) collective-permute-start(bf16[64,2048]{1,0:T(8,128)(2,1)S(1)} %get-tuple-element.327), channel_id=1, source_target_pairs={{0,2},{1,3},{2,0},{3,1},{4,6},{5,7},{6,4},{7,5},{8,10},{9,11},{10,... | collective-permute-start | bytes 786440 | tf_op jit(solution)/shard_map/ppermute | solution.py:620
  486.1 13.8 %collective-permute-start.96 = (bf16[64,2048]{1,0:T(8,128)(2,1)S(1)}, bf16[64,2048]{1,0:T(8,128)(2,1)S(1)}, u32[]{:S(2)}, u32[]{:S(2)}) collective-permute-start(bf16[64,2048]{1,0:T(8,128)(2,1)S(1)} %get-tuple-element.328), channel_id=1, source_target_pairs={{0,3},{1,2},{2,1},{3,0},{4,7},{5,6},{6,5},{7,4},{8,11},{9,10},{10,... | collective-permute-start | bytes 786440 | tf_op jit(solution)/shard_map/ppermute | solution.py:620
  511.8 137.3 %reduce-scatter.4.cloned.1.call-start = ((), (), s32[]{:S(2)}) async-start(), calls=%async_computation.5 | async-start | bytes 5242880 | tf_op jit(solution)/shard_map/reduce_scatter | solution.py:719
  511.9 17.7 %collective-permute-start.101 = (bf16[80,2048]{1,0:T(8,128)(2,1)S(1)}, bf16[80,2048]{1,0:T(8,128)(2,1)S(1)}, u32[]{:S(2)}, u32[]{:S(2)}) collective-permute-start(bf16[80,2048]{1,0:T(8,128)(2,1)S(1)} %get-tuple-element.340.p0), channel_id=1, source_target_pairs={{0,3},{1,2},{2,1},{3,0},{4,7},{5,6},{6,5},{7,4},{8,11},{9,10},{10,... | collective-permute-start | bytes 983048 | tf_op jit(solution)/shard_map/ppermute | solution.py:620
  512.9 16.8 %collective-permute-start.99 = (bf16[80,2048]{1,0:T(8,128)(2,1)S(1)}, bf16[80,2048]{1,0:T(8,128)(2,1)S(1)}, u32[]{:S(2)}, u32[]{:S(2)}) collective-permute-start(bf16[80,2048]{1,0:T(8,128)(2,1)S(1)} %get-tuple-element.340.p0), channel_id=1, source_target_pairs={{0,1},{1,0},{2,3},{3,2},{4,5},{5,4},{6,7},{7,6},{8,9},{9,8},{10,11... | collective-permute-start | bytes 983048 | tf_op jit(solution)/shard_map/ppermute | solution.py:620
  558.2 20.5 %collective-permute-start.107 = (bf16[256,384]{1,0:T(8,128)(2,1)S(1)}, bf16[256,384]{1,0:T(8,128)(2,1)S(1)}, u32[]{:S(2)}, u32[]{:S(2)}) collective-permute-start(bf16[256,384]{1,0:T(8,128)(2,1)S(1)} %get-tuple-element.354), channel_id=1, source_target_pairs={{0,16},{8,24},{16,0},{24,8},{1,17},{9,25},{17,1},{25,9},{2,18},{10... | collective-permute-start | bytes 589832 | tf_op jit(solution)/shard_map/ppermute | solution.py:620
  560.5 18.2 %collective-permute-start.108 = (bf16[256,384]{1,0:T(8,128)(2,1)S(1)}, bf16[256,384]{1,0:T(8,128)(2,1)S(1)}, u32[]{:S(2)}, u32[]{:S(2)}) collective-permute-start(bf16[256,384]{1,0:T(8,128)(2,1)S(1)} %get-tuple-element.355), channel_id=1, source_target_pairs={{0,24},{8,16},{16,8},{24,0},{1,25},{9,17},{17,9},{25,1},{2,26},{10... | collective-permute-start | bytes 589832 | tf_op jit(solution)/shard_map/ppermute | solution.py:620
  562.0 23.5 %collective-permute-start.110 = (bf16[256,1536]{1,0:T(8,128)(2,1)S(1)}, bf16[256,1536]{1,0:T(8,128)(2,1)S(1)}, u32[]{:S(2)}, u32[]{:S(2)}) collective-permute-start(bf16[256,1536]{1,0:T(8,128)(2,1)S(1)} %copy-done.47), channel_id=1, source_target_pairs={{0,64},{64,0},{1,65},{65,1},{2,66},{66,2},{3,67},{67,3},{4,68},{68... | collective-permute-start | bytes 2359304 | tf_op jit(solution)/shard_map/ppermute | solution.py:620
  600.4 13.4 %collective-permute-start.114 = (bf16[64,2048]{1,0:T(8,128)(2,1)S(1)}, bf16[64,2048]{1,0:T(8,128)(2,1)S(1)}, u32[]{:S(2)}, u32[]{:S(2)}) collective-permute-start(bf16[64,2048]{1,0:T(8,128)(2,1)S(1)} %copy-done.62), channel_id=1, source_target_pairs={{0,1},{1,0},{2,3},{3,2},{4,5},{5,4},{6,7},{7,6},{8,9},{9,8},{10,11... | collective-permute-start | bytes 786440 | tf_op jit(solution)/shard_map/ppermute | solution.py:620
  601.7 14.2 %collective-permute-start.115 = (bf16[64,2048]{1,0:T(8,128)(2,1)S(1)}, bf16[64,2048]{1,0:T(8,128)(2,1)S(1)}, u32[]{:S(2)}, u32[]{:S(2)}) collective-permute-start(bf16[64,2048]{1,0:T(8,128)(2,1)S(1)} %get-tuple-element.373), channel_id=1, source_target_pairs={{0,3},{1,2},{2,1},{3,0},{4,7},{5,6},{6,5},{7,4},{8,11},{9,10},{10,... | collective-permute-start | bytes 786440 | tf_op jit(solution)/shard_map/ppermute | solution.py:620
  605.1 14.9 %collective-permute-start.127 = (f32[32,512]{1,0:T(8,128)S(1)}, f32[32,512]{1,0:T(8,128)S(1)}, u32[]{:S(2)}, u32[]{:S(2)}) collective-permute-start(f32[32,512]{1,0:T(8,128)S(1)} %fusion.4), channel_id=1, source_target_pairs={{0,16},{8,24},{16,0},{24,8},{1,17},{9,25},{17,1},{25,9},{2,18},{10... | collective-permute-start | bytes 196616 | tf_op jit(solution)/shard_map/ppermute | solution.py:620
  605.4 14.7 %collective-permute-start.128 = (f32[32,512]{1,0:T(8,128)S(1)}, f32[32,512]{1,0:T(8,128)S(1)}, u32[]{:S(2)}, u32[]{:S(2)}) collective-permute-start(f32[32,512]{1,0:T(8,128)S(1)} %fusion.4), channel_id=1, source_target_pairs={{0,8},{8,0},{16,24},{24,16},{1,9},{9,1},{17,25},{25,17},{2,10},{10... | collective-permute-start | bytes 196616 | tf_op jit(solution)/shard_map/ppermute | solution.py:620
  629.9 22.1 %collective-permute-start.118 = (bf16[2,64,2048]{2,1,0:T(8,128)(2,1)S(1)}, bf16[2,64,2048]{2,1,0:T(8,128)(2,1)S(1)}, u32[]{:S(2)}, u32[]{:S(2)}) collective-permute-start(bf16[2,64,2048]{2,1,0:T(8,128)(2,1)S(1)} %pad_maximum_fusion.p0), channel_id=1, source_target_pairs={{0,1},{1,0},{2,3},{3,2},{4,5},{5,4},{6,7},{7,6},{8,9},{9,8},{10,11... | collective-permute-start | bytes 1572872 | tf_op jit(solution)/shard_map/ppermute | solution.py:620
  630.0 29.1 %collective-permute-start.119 = (bf16[2,64,2048]{2,1,0:T(8,128)(2,1)S(1)}, bf16[2,64,2048]{2,1,0:T(8,128)(2,1)S(1)}, u32[]{:S(2)}, u32[]{:S(2)}) collective-permute-start(bf16[2,64,2048]{2,1,0:T(8,128)(2,1)S(1)} %pad_maximum_fusion.p0), channel_id=1, source_target_pairs={{0,2},{1,3},{2,0},{3,1},{4,6},{5,7},{6,4},{7,5},{8,10},{9,11},{10,... | collective-permute-start | bytes 1572872 | tf_op jit(solution)/shard_map/ppermute | solution.py:620
  631.9 28.1 %collective-permute-start.120 = (bf16[2,64,2048]{2,1,0:T(8,128)(2,1)S(1)}, bf16[2,64,2048]{2,1,0:T(8,128)(2,1)S(1)}, u32[]{:S(2)}, u32[]{:S(2)}) collective-permute-start(bf16[2,64,2048]{2,1,0:T(8,128)(2,1)S(1)} %pad_maximum_fusion.p0), channel_id=1, source_target_pairs={{0,3},{1,2},{2,1},{3,0},{4,7},{5,6},{6,5},{7,4},{8,11},{9,10},{10,... | collective-permute-start | bytes 1572872 | tf_op jit(solution)/shard_map/ppermute | solution.py:620
  651.0 15.0 %collective-permute-start.123 = (bf16[128,1024]{1,0:T(8,128)(2,1)S(1)}, bf16[128,1024]{1,0:T(8,128)(2,1)S(1)}, u32[]{:S(2)}, u32[]{:S(2)}) collective-permute-start(bf16[128,1024]{1,0:T(8,128)(2,1)S(1)} %get-tuple-element.380), channel_id=1, source_target_pairs={{0,32},{4,36},{32,0},{36,4},{1,33},{5,37},{33,1},{37,5},{2,34},{6,... | collective-permute-start | bytes 786440 | tf_op jit(solution)/shard_map/ppermute | solution.py:620
  651.1 14.9 %collective-permute-start.124 = (bf16[128,1024]{1,0:T(8,128)(2,1)S(1)}, bf16[128,1024]{1,0:T(8,128)(2,1)S(1)}, u32[]{:S(2)}, u32[]{:S(2)}) collective-permute-start(bf16[128,1024]{1,0:T(8,128)(2,1)S(1)} %get-tuple-element.381), channel_id=1, source_target_pairs={{0,4},{4,0},{32,36},{36,32},{1,5},{5,1},{33,37},{37,33},{2,6},{6,2... | collective-permute-start | bytes 786440 | tf_op jit(solution)/shard_map/ppermute | solution.py:620
  652.0 15.4 %collective-permute-start.125 = (bf16[128,1024]{1,0:T(8,128)(2,1)S(1)}, bf16[128,1024]{1,0:T(8,128)(2,1)S(1)}, u32[]{:S(2)}, u32[]{:S(2)}) collective-permute-start(bf16[128,1024]{1,0:T(8,128)(2,1)S(1)} %get-tuple-element.382), channel_id=1, source_target_pairs={{0,36},{4,32},{32,4},{36,0},{1,37},{5,33},{33,5},{37,1},{2,38},{6,... | collective-permute-start | bytes 786440 | tf_op jit(solution)/shard_map/ppermute | solution.py:620
  (175 other events, 2297.6 us)
Sparse Core Ops, SparseCore 0:
  30.8 51.3 all-gather.2
  84.5 91.3 all-gather.4
  475.9 49.2 reduce-scatter.7
  527.5 60.9 reduce-scatter.5
  598.8 44.8 reduce-scatter.3

commit v3 on v2

--- a/solution.py
+++ b/solution.py
@@ -54,12 +54,33 @@
     return pl.ds(pl.multiple_of(index * size, size), size)
 
 
-def pack_heads_body(q, k, v, o, out):
+def pack_heads_body(q_far, k_far, v_far, o_far, out, q, k, v, o, sems):
+    copies = [
+        pltpu.make_async_copy(far, part, sems.at[i])
+        for i, (far, part) in enumerate(((q_far, q), (k_far, k), (v_far, v), (o_far, o)))
+    ]
+    for copy in copies:
+        copy.start()
+    for copy in copies:
+        copy.wait()
     for j in range(2):
         at = slice(128 * j, 128 * j + 128)
         for t, part in enumerate((q, k, v)):
             out[:, 384 * j + 128 * t : 384 * j + 128 * t + 128] = part[:, at]
     out[:, 768:] = o[...].T
+
+
+def pack_heads(*parts):
+    return pl.pallas_call(
+        pack_heads_body,
+        in_specs=[pl.BlockSpec(memory_space=pl.ANY)] * 4,
+        out_specs=pl.BlockSpec(memory_space=pltpu.VMEM),
+        out_shape=shape((128, 1024)),
+        scratch_shapes=[pltpu.VMEM(part.shape, part.dtype) for part in parts] + [pltpu.SemaphoreType.DMA((4,))],
+        compiler_params=pltpu.CompilerParams(vmem_limit_bytes=2**22),
+        cost_estimate=pl.CostEstimate(flops=0, bytes_accessed=2**19, transcendentals=0),
+        name="pack_heads",
+    )(*[pltpu.with_memory_space_constraint(part, pltpu.HBM) for part in parts])
 
 
 def turn_body(down, out):
@@ -94,31 +115,16 @@
     return call("pack", body, [shape((128, width))], *parts)[0]
 
 
-def load_body(first, source, kept, sems):
+def turned_rows(source, kept, columns, to, sems):
     copies = []
     for core in range(2):
         for ylo in range(2):
             for x in range(4):
-                at, to = 256 * (4 * core + x) + 128 * ylo, 1024 * core + 512 * ylo + 128 * x
-                part = source.at[pl.ds(at, 128), pl.ds(first, 2048)]
-                copies.append(pltpu.make_async_copy(part, kept.at[pl.ds(to, 128)], sems.at[len(copies)]))
-    for copy in copies:
-        copy.start()
-    for copy in copies:
-        copy.wait()
-
-
-def load(matrix, first=0):
-    return pl.pallas_call(
-        functools.partial(load_body, first),
-        in_specs=[pl.BlockSpec(memory_space=pl.ANY)],
-        out_specs=pl.BlockSpec(memory_space=pltpu.VMEM),
-        out_shape=pltpu.VMEM((D, 2048), LOW),
-        scratch_shapes=[pltpu.SemaphoreType.DMA((16,))],
-        compiler_params=pltpu.CompilerParams(vmem_limit_bytes=2**22),
-        cost_estimate=pl.CostEstimate(flops=0, bytes_accessed=4 * matrix.size, transcendentals=0),
-        name="load",
-    )(pltpu.with_memory_space_constraint(matrix, pltpu.HBM))
+                at, row = 256 * (4 * core + x) + 128 * ylo, 1024 * core + 512 * ylo + 128 * x
+                part = source.at[pl.ds(at, 128), pl.ds(columns[0], columns[1])]
+                place = kept.at[pl.ds(row, 128), pl.ds(to, columns[1])]
+                copies.append(pltpu.make_async_copy(part, place, sems.at[len(copies)]))
+    return copies
 
 
 def held(matrix):
@@ -143,9 +149,26 @@
     return (p[0] + p[2]) + (p[1] + p[3])
 
 
-def rows_body(kind, first, spot, p0, p1, p2, p3, w, *refs):
+def rows_body(kind, first, loads, spot, p0, p1, p2, p3, w, *refs):
     extra = refs[0] if kind != "heads" else None
     keep, send, *outs = refs[1:] if kind != "heads" else refs
+    chunks, later = [], []
+    if loads:
+        source = w
+        *outs, sems = outs
+        w, *more = outs[-loads:]
+        outs = outs[:-loads]
+        chunks = [turned_rows(source, w, (512 * c, 512), 512 * c, sems.at[c]) for c in range(4)]
+        later = [turned_rows(source, ref, (2048, 2048), 0, sems.at[4]) for ref in more]
+        for chunk in chunks + later:
+            for copy in chunk:
+                copy.start()
+
+    def loaded(count):
+        while chunks and 4 - len(chunks) < count:
+            for copy in chunks.pop(0):
+                copy.wait()
+
     kept, sent = at_block(spot[1], D // 2), at_block(1 - spot[1], D // 2)
     for i, p in enumerate((p0, p1, p2, p3)):
         keep[OWN * i : OWN * i + OWN] = p[:OWN, kept]
@@ -157,6 +180,18 @@
     def product(at):
         return dot_t(keep[...], w[kept, at]) + dot_t(send[...], w[sent, at])
 
+    if kind == "qkv" and loads:
+        for slot in range(4):
+            loaded(slot if slot else 1)
+            low = (product(slice(384 * slot, 384 * slot + 384)) + extra[:, 384 * slot : 384 * slot + 384]).astype(LOW)
+            for d in range(4):
+
+                @pl.when((slot ^ spot[0]) == d)
+                def _():
+                    outs[d][...] = low
+
+        loaded(4)
+        return
     if kind in ("qkv", "heads"):
         width = outs[0].shape[1]
         for d in range(4):
@@ -169,6 +204,7 @@
     tile = 512
     for i in range(4):
         at = slice(tile * i, tile * i + tile)
+        loaded(i + 1)
         values = product(at)
         if kind == "up":
             values = values + extra[:, at]
@@ -181,9 +217,12 @@
             low = (values * extra[:, at].astype(F32)).astype(LOW)
             outs[0][:, at] = low
             outs[1][:, at] = jnp.sum(low.astype(F32), axis=0, keepdims=True)
-
-
-def rows_mm(kind, spot, pieces, weight, extra=None):
+    for chunk in later:
+        for copy in chunk:
+            copy.wait()
+
+
+def rows_mm(kind, spot, pieces, weight, extra=None, loads=0):
     half = shape((TOK, D // 2))
     n, first, outs = {
         "qkv": (1536, 0, [shape((TOK, 384))] * 4),
@@ -191,21 +230,27 @@
         "up": (2048, 0, [shape((TOK, 2048))] * 2),
         "slope": (2048, 0, [shape((TOK, 2048)), shape((1, 2048), F32)]),
     }[kind]
-    args = (held(weight),) if extra is None else (held(weight), extra)
+    args = [weight if loads else held(weight)] + ([] if extra is None else [extra])
     if pieces[0].shape[0] > OWN:
         outs = [*outs, shape((16, D), F32)]
-    return call(
-        "rows_" + kind,
-        functools.partial(rows_body, kind, first),
-        [half, half, *outs],
-        *pieces,
-        *args,
-        spot=spot,
-        mib=12,
-        flops=2 * TOK * D * n,
-        size=2 * D * n,
-        exps=TOK * n if kind == "up" else 0,
-    )
+    body = functools.partial(rows_body, kind, first, loads)
+    cost = pl.CostEstimate(flops=2 * TOK * D * n, bytes_accessed=2 * D * n, transcendentals=TOK * n if kind == "up" else 0)
+    vmem = pl.BlockSpec(memory_space=pltpu.VMEM)
+    if loads:
+        args[0] = pltpu.with_memory_space_constraint(weight, pltpu.HBM)
+    return pl.pallas_call(
+        body,
+        in_specs=[pl.BlockSpec(memory_space=pltpu.SMEM)]
+        + [vmem] * 4
+        + [pl.BlockSpec(memory_space=pl.ANY) if loads else vmem]
+        + [vmem] * (len(args) - 1),
+        out_specs=[vmem] * (2 + len(outs) + loads),
+        out_shape=[half, half, *outs] + [pltpu.VMEM((D, 2048), LOW)] * loads,
+        scratch_shapes=[pltpu.SemaphoreType.DMA((5, 16))] if loads else [],
+        compiler_params=pltpu.CompilerParams(vmem_limit_bytes=12 * 2**20),
+        cost_estimate=cost,
+        name="rows_" + kind,
+    )(spot, *pieces, *args)
 
 
 def scatter_body(n_parts, first, k, spot, *refs):
@@ -326,7 +371,8 @@
     )[0]
 
 
-def head_terms_body(spot, operands, copies, outs, turned):
+def head_terms_body(spot, operands, copies, outs, scratch):
+    *turned, parts, sems = scratch
     rights = operands[4:8], operands[12:16]
     for g in range(2):
         for i in range(4):
@@ -337,31 +383,40 @@
                     turned[g][to : to + 128, TOK * i : TOK * i + TOK] = operands[8 * g + i][:, at : at + 128].T
     for i in (*range(4, 8), *range(12, 16)):
         arrive(copies[i])
+    sent = []
     for slot in range(4):
+        if slot > 1:
+            arrive(sent[2 * slot - 4 : 2 * slot - 2])
         first = 1024 * (slot & 1)
+        at = 0
         for g, width in enumerate((384, 128)):
             total = None
             for i in range(4):
                 part = dot_t(turned[g][:, TOK * i : TOK * i + TOK], rights[g][i][:, width * slot : width * slot + width])
                 total = part if total is None else total + part
+            held_part = parts.at[slot & 1, :, pl.ds(at, width)]
+            held_part[...] = total.astype(LOW)
             to = first + width * (slot >> 1)
-            outs[0][:, to : to + width] = total.astype(LOW)
+            sent.append(pltpu.make_async_copy(held_part, outs[0].at[:, pl.ds(to, width)], sems.at[slot & 1, g]))
+            sent[-1].start()
             first += 2 * width
+            at += width
     line = [jnp.sum(rights[0][i][...].astype(F32), axis=0, keepdims=True) for i in (0, 2)]
     outs[1][...] = line[0] + line[1]
+    arrive(sent[4:])
 
 
 def head_terms(spot, sides, olds):
     return old_call(
         "head_terms",
         head_terms_body,
-        [shape((1024, 2048)), shape((1, 1536), F32)],
-        [pl.BlockSpec(memory_space=pltpu.VMEM)] * 2,
+        [pltpu.HBM((1024, 2048), LOW), shape((1, 1536), F32)],
+        [pl.BlockSpec(memory_space=pl.ANY), pl.BlockSpec(memory_space=pltpu.VMEM)],
         [part for side in sides for part in side],
         olds,
         [1] * 16,
         spot,
-        [pltpu.VMEM((1024, 1024), LOW)] * 2,
+        [pltpu.VMEM((1024, 1024), LOW)] * 2 + [pltpu.VMEM((2, 1024, 512), LOW), pltpu.SemaphoreType.DMA((2, 2))],
         20,
     )
 
@@ -652,24 +707,25 @@
 def layer_forward(spot, stream, pieces, matrices, vectors, mark, windowed):
     heads_matrix, up_matrix, down_matrix = matrices
     qkv_bias, up_bias, out_bias, down_bias, attn_gain, attn_shift, ffn_gain, ffn_shift = vectors
-    keep, send, *heads = rows_mm("qkv", spot, pieces, heads_matrix, qkv_bias)
+    keep, send, *heads = rows_mm("qkv", spot, pieces, heads_matrix, qkv_bias, int(windowed))
+    if windowed:
+        *heads, heads_matrix = heads
     rows = (keep, send)
     heads = exchange(heads, "x")
     heads = heads + [sibling(h) for h in heads]
     mixed, lse = attend_fwd(spot, heads, mark, windowed)
     *branch, attended = scatter_mm(spot, exchange(mixed, "x"), heads_matrix, 512, 1536)
     normed, scale, first, low = norm(exchange(branch, "z"), stream, out_bias, attn_gain, attn_shift)
-    loaded = load(up_matrix) if windowed else up_matrix
-    keep, send, active, slope = rows_mm("up", spot, gather(low, "z"), loaded, up_bias)
+    keep, send, active, slope, *loaded = rows_mm("up", spot, gather(low, "z"), up_matrix, up_bias, 2 * windowed)
     if windowed:
-        down_matrix = load(up_matrix, 2048)
+        up_matrix, down_matrix = loaded
     second = scatter_mm(spot, [active], down_matrix, 2048, 0)
     normed_two, scale_two, result, low = norm(exchange(second, "z"), first, down_bias, ffn_gain, ffn_shift)
     saved = (heads, mixed, lse, normed, scale, slope, normed_two, scale_two)
     far = [sibling(part) for part in (rows[1], attended, send, active)]
     low, *far = tie(low, *far)
     sides = (rows[0], far[0]), (attended, far[1]), (keep, far[2]), (active, far[3])
-    return result, low, saved, sides, (heads_matrix, loaded, down_matrix)
+    return result, low, saved, sides, (heads_matrix, up_matrix, down_matrix)
 
 
 FRESH_LEFTS = [False] * 2 + [True] * 6
@@ -774,7 +830,7 @@
 ):
     core, ylo, x, yhi, z = (lax.axis_index(name) for name in AXES)
     spot = jnp.stack([x, core, ylo, z, yhi]).astype(jnp.int32)
-    local = pack(pack_heads_body, 1024, query_weight, key_weight, value_weight, out_weight)
+    local = pack_heads(query_weight, key_weight, value_weight, out_weight)
     parts = gather(local, Y)
     *parts, inputs, down_weight = tie(*parts, inputs, down_weight)
 
@@ -786,7 +842,7 @@
     pieces = gather(own_rows, "z")
     *pieces, up_weight = tie(*pieces, up_weight)
     hidden_matrix = gathered(False, gather(up_weight, Y) + gather(pack(turn_body, 1024, down_weight), Y))
-    matrices = (load(heads_matrix), hidden_matrix, None)
+    matrices = (heads_matrix, hidden_matrix, None)
     bias_own = jnp.concatenate([query_bias, value_bias, up_bias])
     bias = (bias_own, swap(bias_own, "yhi", 1, 2))
     none = jnp.zeros((128,), F32)
@@ -804,6 +860,8 @@
     top_grad = turn_same(core, ylo, pick(pick(cotangent, yhi)[0].reshape(4, OWN, D), z)).astype(F32)
     seg_here = pick(segments, yhi)[0].astype(F32)
     mark = marks(spot, jnp.where(core == ylo, seg_here, sibling(seg_here)))
+    *pieces, mark_row, mark_column = tie(*pieces, *mark)
+    mark = (mark_row, mark_column)
     middle, low, saved_one, sides_one, matrices = layer_forward(
         spot, own_rows.astype(F32), pieces, matrices, vectors, mark, True
     )

time: 684 us -> 681 us (level)
    pallas_call x38 -> x29, Pallas kernels: 70.6 us -> 46.3 us  [call(): pl.pallas_call(body, in_specs=specs, out_specs=[pl.BlockSpec(memory_space...]
    pallas_call x3 -> x9, Pallas kernels: 11.4 us -> 31.7 us  [the longest x8 30.5 us: rows_mm(): pl.pallas_call(body, in_specs=[pl.BlockSpec(memory_space=pltpu.SMEM)] + [...]
    ppermute x127, waiting for transfers between devices: 253 us -> 269 us  [swap(): return lax.ppermute(values, axis, [(i, i ^ bits) for i in range(size)])]
    all_gather x2, waiting for transfers between devices: 24.6 us -> 12.8 us  [gathered(): lax.all_gather(pair(heads, spot, parts), ('core', 'x'), axis=0, tiled=True)]
    unnamed x220 -> x208, local copies, waits for them, and re-layouts: 31.3 us -> 28.8 us
  transfers between devices with their start and end apart: 138 -> 138, of which waited for: 79 -> 84; matrix products, arithmetic and copies ran while one was open for 2% -> 2% of each run, Pallas kernels for 13% -> 12%
where the time goes in v3:
time: 681 us; the launch traced here: 672 us
  waiting for transfers between devices  296 us (43%)
  starting transfers between devices  197 us (29%)
  Pallas kernels  123 us (18%)
  local copies, waits for them, and re-layouts  34.6 us (5%)
  between operations  15.6 us (2%)
    ppermute x127, waiting for transfers between devices, swap(): return lax.ppermute(values, axis, [(i, i ^ bits) for i in range(size)])  269 us
    ppermute x127, starting transfers between devices, swap(): return lax.ppermute(values, axis, [(i, i ^ bits) for i in range(size)])  182 us
    pallas_call x29, Pallas kernels, call(): pl.pallas_call(body, in_specs=specs, out_specs=[pl.BlockSpec(memory_space...  46.3 us
    pallas_call x5, Pallas kernels, old_call(): pl.pallas_call(inner, in_specs=[pl.BlockSpec(memory_space=pltpu.SMEM)] +...  44.8 us
    pallas_call x8, Pallas kernels, rows_mm(): pl.pallas_call(body, in_specs=[pl.BlockSpec(memory_space=pltpu.SMEM)] + [...  30.5 us
    unnamed x208, local copies, waits for them, and re-layouts  28.8 us
  transfers between devices with their start and end apart: 138, of which 84 were waited for; matrix products, arithmetic and copies ran while one was open for 2% of the time, Pallas kernels for 12%

profile of v3, /device:TPU:1, one launch (start us, length us, event | category | flops | bytes accessed | tf_op | source)
XLA Modules:
  0.0 672.0 jit_solution(9140360886039235816)
XLA Ops:
  16.3 8.4 %collective-permute-done.1.refs_2_ = bf16[128,1024]{1,0:T(8,128)(2,1)S(1)} collective-permute-done((bf16[128,1024]{1,0:T(8,128)(2,1)S(1)}, bf16[128,1024]{1,0:T(8,128)(2,1)S(1)}, u32[]{:S(2)}, u32[]{:S(2)}) %collective-permute-start.1) | collective-permute-done | bytes 262176 | tf_op jit(solution)/shard_map/ppermute | solution.py:675
  33.1 5.4 collective-permute-done.3
  41.2 3.3 collective-permute-start.5
  48.6 3.5 collective-permute-done.5.p2
  55.7 3.4 collective-permute-start.27
  60.1 4.3 collective-permute-done.25.refs_1_
  64.4 3.8 collective-permute-done.26.refs_2_
  68.3 3.6 collective-permute-done.27.refs_3_
  76.2 3.9 collective-permute-done.8
  81.4 6.0 rows_qkv.2
  94.1 3.7 collective-permute-start.13
  97.8 3.9 collective-permute-done.10.refs_2_
  101.7 5.5 collective-permute-start.14
  109.8 5.3 attend_fwd.2
  137.9 8.1 %collective-permute-done.20.refs_2_ = bf16[64,2048]{1,0:T(8,128)(2,1)S(1)} collective-permute-done((bf16[64,2048]{1,0:T(8,128)(2,1)S(1)}, bf16[64,2048]{1,0:T(8,128)(2,1)S(1)}, u32[]{:S(2)}, u32[]{:S(2)}) %collective-permute-start.20) | collective-permute-done | bytes 262176 | tf_op jit(solution)/shard_map/ppermute | solution.py:675
  155.0 5.6 collective-permute-done.23.p2
  160.6 3.4 collective-permute-done.24.p3
  164.0 12.7 %all-gather.5.cloned.1.call-done.w = bf16[2048,4096]{1,0:T(8,128)(2,1)} async-done(((bf16[256,4096]{1,0:T(8,128)(2,1)}), bf16[2048,4096]{1,0:T(8,128)(2,1)}) %all-gather.5.cloned.1.call-update) | async-done | bytes 16777232 | tf_op jit(solution)/shard_map/all_gather | solution.py:838
  176.7 7.4 %rows_up.2 = (bf16[256,1024]{1,0:T(8,128)(2,1)S(1)}, bf16[256,1024]{1,0:T(8,128)(2,1)S(1)}, bf16[256,2048]{1,0:T(8,128)(2,1)S(1)}, bf16[256,2048]{1,0:T(8,128)(2...) custom-call(s32[5]{0:T(128)S(1)} %stack.50.spot.spot_ref, ...), custom_call_target="tpu_custom_call" | custom-call | flops 2147483648 | bytes 8388608 | tf_op jit(solution)/shard_map/rows_up/pallas_call | solution.py:241
  198.9 5.4 collective-permute-done.32.refs_2_
  205.4 5.0 collective-permute-done.33.refs_3_
  214.9 3.5 collective-permute-done.38.p1
  218.4 4.8 collective-permute-done.39.p2
  244.0 6.2 attend_fwd.3
  250.3 3.9 collective-permute-start.50
  260.1 3.6 collective-permute-start.53
  265.9 7.7 %collective-permute-done.53.refs_2_ = bf16[64,2048]{1,0:T(8,128)(2,1)S(1)} collective-permute-done((bf16[64,2048]{1,0:T(8,128)(2,1)S(1)}, bf16[64,2048]{1,0:T(8,128)(2,1)S(1)}, u32[]{:S(2)}, u32[]{:S(2)}) %collective-permute-start.53) | collective-permute-done | bytes 262176 | tf_op jit(solution)/shard_map/ppermute | solution.py:675
  273.6 3.4 collective-permute-done.54.refs_3_
  281.5 4.5 collective-permute-start.48
  288.7 3.6 collective-permute-done.57.p3
  292.3 4.1 rows_up.3
  300.2 3.6 collective-permute-start.59
  305.9 7.7 %collective-permute-done.59.refs_2_ = bf16[64,2048]{1,0:T(8,128)(2,1)S(1)} collective-permute-done((bf16[64,2048]{1,0:T(8,128)(2,1)S(1)}, bf16[64,2048]{1,0:T(8,128)(2,1)S(1)}, u32[]{:S(2)}, u32[]{:S(2)}) %collective-permute-start.59) | collective-permute-done | bytes 262176 | tf_op jit(solution)/shard_map/ppermute | solution.py:675
  313.6 3.6 collective-permute-done.60.refs_3_
  326.3 4.4 collective-permute-done.62.p2
  330.6 3.6 collective-permute-done.63.p3
  343.0 3.8 collective-permute-start.65
  347.1 3.4 collective-permute-start.75
  350.5 3.3 collective-permute-done.65.refs_2_
  353.7 3.2 collective-permute-start.74
  356.9 3.4 collective-permute-done.66.refs_3_
  369.0 5.4 collective-permute-done.68.p2
  379.8 3.7 collective-permute-done.72.refs_11_
  388.2 6.5 attend_bwd.2
  394.8 7.2 %collective-permute-start.80 = (f32[1024,256]{1,0:T(8,128)S(1)}, f32[1024,256]{1,0:T(8,128)S(1)}, u32[]{:S(2)}, u32[]{:S(2)}) collective-permute-start(f32[1024,256]{1,0:T(8,128)S(1)} %get-tuple-element.310), channel_id=1, source_target_pairs={{0,64},{64,0},{1,65},{65,1},{2,66},{66,2},{3,67},{67,3},{4,68},{68... | collective-permute-start | bytes 3145736 | tf_op jit(solution)/shard_map/ppermute | solution.py:675
  413.7 3.5 collective-permute-done.82.refs_2_
  431.0 6.7 collective-permute-done.87.refs_2_
  446.8 6.2 collective-permute-done.90.p2
  463.3 8.5 %weight_term.2 = bf16[1024,2048]{1,0:T(8,128)(2,1)} custom-call(s32[5]{0:T(128)S(1)} %stack.50.spot.spot_ref, bf16[256,1024]{1,0:T(8,128)(2,1)S(1)} %get-tuple-element.336.refs_0_, bf16[256,1024]{1,0:T(8,128)(2,1)S(1)} %collective-permute-done.92.refs_1_, bf16[256,1024]{1,0:T(8,128)(2,1)} %copy-done.49, bf16[256,1024]{1,0:T(8,128)(2,1)} %copy-done.87, ...), custom_call_target="tpu_custom_call" | custom-call | flops 4294967296 | bytes 8388608 | tf_op jit(solution)/shard_map/weight_term/pallas_call | solution.py:325
  472.7 3.4 copy-done.5
  482.9 3.7 collective-permute-done.94.refs_1_
  486.6 7.2 %collective-permute-done.95.refs_2_ = bf16[64,2048]{1,0:T(8,128)(2,1)S(1)} collective-permute-done((bf16[64,2048]{1,0:T(8,128)(2,1)S(1)}, bf16[64,2048]{1,0:T(8,128)(2,1)S(1)}, u32[]{:S(2)}, u32[]{:S(2)}) %collective-permute-start.95) | collective-permute-done | bytes 262176 | tf_op jit(solution)/shard_map/ppermute | solution.py:675
  498.8 8.8 %weight_term.3 = bf16[1024,2048]{1,0:T(8,128)(2,1)} custom-call(s32[5]{0:T(128)S(1)} %stack.50.spot.spot_ref, bf16[256,1024]{1,0:T(8,128)(2,1)} %copy-done.44, bf16[256,1024]{1,0:T(8,128)(2,1)} %copy-done.84, bf16[256,1024]{1,0:T(8,128)(2,1)} %copy-done.45, bf16[256,1024]{1,0:T(8,128)(2,1)} %copy-done.86, ...), custom_call_target="tpu_custom_call" | custom-call | flops 4294967296 | bytes 8388608 | tf_op jit(solution)/shard_map/weight_term/pallas_call | solution.py:325
  510.5 6.5 collective-permute-done.100.p2
  517.0 8.6 %collective-permute-done.101.p3 = bf16[80,2048]{1,0:T(8,128)(2,1)S(1)} collective-permute-done((bf16[80,2048]{1,0:T(8,128)(2,1)S(1)}, bf16[80,2048]{1,0:T(8,128)(2,1)S(1)}, u32[]{:S(2)}, u32[]{:S(2)}) %collective-permute-start.101) | collective-permute-done | bytes 327712 | tf_op jit(solution)/shard_map/ppermute | solution.py:675
  525.6 3.4 copy-done.3
  540.6 8.3 %attend_bwd.3 = (bf16[256,128]{1,0:T(8,128)(2,1)S(1)}, bf16[256,128]{1,0:T(8,128)(2,1)S(1)}, bf16[256,128]{1,0:T(8,128)(2,1)S(1)}, bf16[256,128]{1,0:T(8,128)(2,...) custom-call(s32[5]{0:T(128)S(1)} %stack.50.spot.spot_ref, bf16[256,384]{1,0:T(8,128)(2,1)} %copy-done.59, ...), custom_call_target="tpu_custom_call" | custom-call | flops 4294967296 | bytes 8388608 | tf_op jit(solution)/shard_map/attend_bwd/pallas_call | solution.py:325
  558.7 6.1 collective-permute-done.106.refs_1_
  564.8 10.2 %collective-permute-done.107.refs_2_ = bf16[256,384]{1,0:T(8,128)(2,1)S(1)} collective-permute-done((bf16[256,384]{1,0:T(8,128)(2,1)S(1)}, bf16[256,384]{1,0:T(8,128)(2,1)S(1)}, u32[]{:S(2)}, u32[]{:S(2)}) %collective-permute-start.107) | collective-permute-done | bytes 196640 | tf_op jit(solution)/shard_map/ppermute | solution.py:675
  582.3 12.7 %head_terms.1 = (bf16[1024,2048]{1,0:T(8,128)(2,1)}, f32[1,1536]{1,0:T(1,128)S(1)}) custom-call(s32[5]{0:T(128)S(1)} %stack.50.spot.spot_ref, bf16[256,1024]{1,0:T(8,128)(2,1)} %copy-done.42, bf16[256,1024]{1,0:T(8,128)(2,1)} %copy-done.83, bf16[256,1024]{1,0:T(8,128)(2,1)} %copy-done.43, bf16[256,1024]{1,0:T(8,128)(2,1)} %copy-done.85, ...), custom_call_target="tpu_custom_call" | custom-call | flops 4294967296 | bytes 8388608 | tf_op jit(solution)/shard_map/head_terms/pallas_call | solution.py:325
  602.6 3.4 collective-permute-done.113
  621.4 4.9 collective-permute-done.117
  636.4 5.2 collective-permute-done.122.down_far
  641.6 4.4 collective-permute-done.121.up_far
  (519 shorter events, 314.9 us)
Async XLA Ops:
  7.2 74.2 %all-gather.3.cloned.1.call-start = ((), (), s32[]{:S(2)}) async-start(), calls=%async_computation.3 | async-start | bytes 9437184 | tf_op jit(solution)/shard_map/all_gather | solution.py:838
  10.7 14.0 %collective-permute-start.1 = (bf16[128,1024]{1,0:T(8,128)(2,1)S(1)}, bf16[128,1024]{1,0:T(8,128)(2,1)S(1)}, u32[]{:S(2)}, u32[]{:S(2)}) collective-permute-start(bf16[128,1024]{1,0:T(8,128)(2,1)S(1)} %pack_heads.1.refs_0_), channel_id=1, source_target_pairs={{0,4},{4,0},{32,36},{36,32},{1,5},{5,1},{33,37},{37,33},{2,6},{6,2... | collective-permute-start | bytes 786440 | tf_op jit(solution)/shard_map/ppermute | solution.py:675
  13.3 13.4 %collective-permute-start.2 = (bf16[128,1024]{1,0:T(8,128)(2,1)S(1)}, bf16[128,1024]{1,0:T(8,128)(2,1)S(1)}, u32[]{:S(2)}, u32[]{:S(2)}) collective-permute-start(bf16[128,1024]{1,0:T(8,128)(2,1)S(1)} %pack_heads.1.refs_0_), channel_id=1, source_target_pairs={{0,36},{4,32},{32,4},{36,0},{1,37},{5,33},{33,5},{37,1},{2,38},{6,... | collective-permute-start | bytes 786440 | tf_op jit(solution)/shard_map/ppermute | solution.py:675
  28.4 148.3 %all-gather.5.cloned.1.call-start = ((), (), s32[]{:S(2)}) async-start(), calls=%async_computation.4 | async-start | bytes 18874368 | tf_op jit(solution)/shard_map/all_gather | solution.py:838
  44.7 14.4 %collective-permute-start.29 = (bf16[128,1024]{1,0:T(8,128)(2,1)S(1)}, bf16[128,1024]{1,0:T(8,128)(2,1)S(1)}, u32[]{:S(2)}, u32[]{:S(2)}) collective-permute-start(bf16[128,1024]{1,0:T(8,128)(2,1)S(1)} %pack.1.refs_4_), channel_id=1, source_target_pairs={{0,4},{4,0},{32,36},{36,32},{1,5},{5,1},{33,37},{37,33},{2,6},{6,2... | collective-permute-start | bytes 786440 | tf_op jit(solution)/shard_map/ppermute | solution.py:675
  46.6 13.5 %collective-permute-start.30 = (bf16[128,1024]{1,0:T(8,128)(2,1)S(1)}, bf16[128,1024]{1,0:T(8,128)(2,1)S(1)}, u32[]{:S(2)}, u32[]{:S(2)}) collective-permute-start(bf16[128,1024]{1,0:T(8,128)(2,1)S(1)} %pack.1.refs_4_), channel_id=1, source_target_pairs={{0,36},{4,32},{32,4},{36,0},{1,37},{5,33},{33,5},{37,1},{2,38},{6,... | collective-permute-start | bytes 786440 | tf_op jit(solution)/shard_map/ppermute | solution.py:675
  55.2 13.0 %collective-permute-start.26 = (bf16[128,1024]{1,0:T(8,128)(2,1)S(1)}, bf16[128,1024]{1,0:T(8,128)(2,1)S(1)}, u32[]{:S(2)}, u32[]{:S(2)}) collective-permute-start(bf16[128,1024]{1,0:T(8,128)(2,1)S(1)} %copy-done.18), channel_id=1, source_target_pairs={{0,4},{4,0},{32,36},{36,32},{1,5},{5,1},{33,37},{37,33},{2,6},{6,2... | collective-permute-start | bytes 786440 | tf_op jit(solution)/shard_map/ppermute | solution.py:675
  55.7 16.2 %collective-permute-start.27 = (bf16[128,1024]{1,0:T(8,128)(2,1)S(1)}, bf16[128,1024]{1,0:T(8,128)(2,1)S(1)}, u32[]{:S(2)}, u32[]{:S(2)}) collective-permute-start(bf16[128,1024]{1,0:T(8,128)(2,1)S(1)} %copy-done.18), channel_id=1, source_target_pairs={{0,36},{4,32},{32,4},{36,0},{1,37},{5,33},{33,5},{37,1},{2,38},{6,... | collective-permute-start | bytes 786440 | tf_op jit(solution)/shard_map/ppermute | solution.py:675
  73.9 556.8 %reduce-scatter.8.cloned.1.call-start = ((), (), s32[]{:S(2)}) async-start(), calls=%async_computation.7 | async-start | bytes 4718592 | tf_op jit(solution)/shard_map/reduce_scatter | solution.py:750
  91.9 15.4 %collective-permute-start.11 = (bf16[256,384]{1,0:T(8,128)(2,1)S(1)}, bf16[256,384]{1,0:T(8,128)(2,1)S(1)}, u32[]{:S(2)}, u32[]{:S(2)}) collective-permute-start(bf16[256,384]{1,0:T(8,128)(2,1)S(1)} %get-tuple-element.233), channel_id=1, source_target_pairs={{0,24},{8,16},{16,8},{24,0},{1,25},{9,17},{17,9},{25,1},{2,26},{10... | collective-permute-start | bytes 589832 | tf_op jit(solution)/shard_map/ppermute | solution.py:675
  92.1 16.7 %collective-permute-start.12 = (bf16[256,384]{1,0:T(8,128)(2,1)S(1)}, bf16[256,384]{1,0:T(8,128)(2,1)S(1)}, u32[]{:S(2)}, u32[]{:S(2)}) collective-permute-start(bf16[256,384]{1,0:T(8,128)(2,1)S(1)} %get-tuple-element.230.refs_0_), channel_id=1, source_target_pairs={{0,64},{64,0},{1,65},{65,1},{2,66},{66,2},{3,67},{67,3},{4,68},{68... | collective-permute-start | bytes 589832 | tf_op jit(solution)/shard_map/ppermute | solution.py:675
  94.1 14.6 %collective-permute-start.13 = (bf16[256,384]{1,0:T(8,128)(2,1)S(1)}, bf16[256,384]{1,0:T(8,128)(2,1)S(1)}, u32[]{:S(2)}, u32[]{:S(2)}) collective-permute-start(bf16[256,384]{1,0:T(8,128)(2,1)S(1)} %collective-permute-done.9.refs_1_), channel_id=1, source_target_pairs={{0,64},{64,0},{1,65},{65,1},{2,66},{66,2},{3,67},{67,3},{4,68},{68... | collective-permute-start | bytes 589832 | tf_op jit(solution)/shard_map/ppermute | solution.py:675
  132.0 14.0 %collective-permute-start.20 = (bf16[64,2048]{1,0:T(8,128)(2,1)S(1)}, bf16[64,2048]{1,0:T(8,128)(2,1)S(1)}, u32[]{:S(2)}, u32[]{:S(2)}) collective-permute-start(bf16[64,2048]{1,0:T(8,128)(2,1)S(1)} %get-tuple-element.243), channel_id=1, source_target_pairs={{0,2},{1,3},{2,0},{3,1},{4,6},{5,7},{6,4},{7,5},{8,10},{9,11},{10,... | collective-permute-start | bytes 786440 | tf_op jit(solution)/shard_map/ppermute | solution.py:675
  135.2 13.5 %collective-permute-start.21 = (bf16[64,2048]{1,0:T(8,128)(2,1)S(1)}, bf16[64,2048]{1,0:T(8,128)(2,1)S(1)}, u32[]{:S(2)}, u32[]{:S(2)}) collective-permute-start(bf16[64,2048]{1,0:T(8,128)(2,1)S(1)} %get-tuple-element.244), channel_id=1, source_target_pairs={{0,3},{1,2},{2,1},{3,0},{4,7},{5,6},{6,5},{7,4},{8,11},{9,10},{10,... | collective-permute-start | bytes 786440 | tf_op jit(solution)/shard_map/ppermute | solution.py:675
  150.5 13.5 %collective-permute-start.24 = (bf16[64,2048]{1,0:T(8,128)(2,1)S(1)}, bf16[64,2048]{1,0:T(8,128)(2,1)S(1)}, u32[]{:S(2)}, u32[]{:S(2)}) collective-permute-start(bf16[64,2048]{1,0:T(8,128)(2,1)S(1)} %get-tuple-element.245.p0), channel_id=1, source_target_pairs={{0,3},{1,2},{2,1},{3,0},{4,7},{5,6},{6,5},{7,4},{8,11},{9,10},{10,... | collective-permute-start | bytes 786440 | tf_op jit(solution)/shard_map/ppermute | solution.py:675
  185.0 26.0 %collective-permute-start.37 = (bf16[256,2048]{1,0:T(8,128)(2,1)S(1)}, bf16[256,2048]{1,0:T(8,128)(2,1)S(1)}, u32[]{:S(2)}, u32[]{:S(2)}) collective-permute-start(bf16[256,2048]{1,0:T(8,128)(2,1)S(1)} %get-tuple-element.248.refs_0_.refs_4_), channel_id=1, source_target_pairs={{0,64},{64,0},{1,65},{65,1},{2,66},{66,2},{3,67},{67,3},{4,68},{68... | collective-permute-start | bytes 3145736 | tf_op jit(solution)/shard_map/ppermute | solution.py:675
  189.3 15.0 %collective-permute-start.32 = (bf16[64,2048]{1,0:T(8,128)(2,1)S(1)}, bf16[64,2048]{1,0:T(8,128)(2,1)S(1)}, u32[]{:S(2)}, u32[]{:S(2)}) collective-permute-start(bf16[64,2048]{1,0:T(8,128)(2,1)S(1)} %get-tuple-element.252), channel_id=1, source_target_pairs={{0,2},{1,3},{2,0},{3,1},{4,6},{5,7},{6,4},{7,5},{8,10},{9,11},{10,... | collective-permute-start | bytes 786440 | tf_op jit(solution)/shard_map/ppermute | solution.py:675
  192.5 18.4 %collective-permute-start.34 = (bf16[256,1024]{1,0:T(8,128)(2,1)S(1)}, bf16[256,1024]{1,0:T(8,128)(2,1)S(1)}, u32[]{:S(2)}, u32[]{:S(2)}) collective-permute-start(bf16[256,1024]{1,0:T(8,128)(2,1)S(1)} %copy-done.51), channel_id=1, source_target_pairs={{0,64},{64,0},{1,65},{65,1},{2,66},{66,2},{3,67},{67,3},{4,68},{68... | collective-permute-start | bytes 1572872 | tf_op jit(solution)/shard_map/ppermute | solution.py:675
  193.3 17.6 %collective-permute-start.36 = (bf16[256,1024]{1,0:T(8,128)(2,1)S(1)}, bf16[256,1024]{1,0:T(8,128)(2,1)S(1)}, u32[]{:S(2)}, u32[]{:S(2)}) collective-permute-start(bf16[256,1024]{1,0:T(8,128)(2,1)S(1)} %get-tuple-element.258), channel_id=1, source_target_pairs={{0,64},{64,0},{1,65},{65,1},{2,66},{66,2},{3,67},{67,3},{4,68},{68... | collective-permute-start | bytes 1572872 | tf_op jit(solution)/shard_map/ppermute | solution.py:675
  196.1 14.4 %collective-permute-start.33 = (bf16[64,2048]{1,0:T(8,128)(2,1)S(1)}, bf16[64,2048]{1,0:T(8,128)(2,1)S(1)}, u32[]{:S(2)}, u32[]{:S(2)}) collective-permute-start(bf16[64,2048]{1,0:T(8,128)(2,1)S(1)} %get-tuple-element.253), channel_id=1, source_target_pairs={{0,3},{1,2},{2,1},{3,0},{4,7},{5,6},{6,5},{7,4},{8,11},{9,10},{10,... | collective-permute-start | bytes 786440 | tf_op jit(solution)/shard_map/ppermute | solution.py:675
  211.9 14.1 %collective-permute-start.40 = (bf16[64,2048]{1,0:T(8,128)(2,1)S(1)}, bf16[64,2048]{1,0:T(8,128)(2,1)S(1)}, u32[]{:S(2)}, u32[]{:S(2)}) collective-permute-start(bf16[64,2048]{1,0:T(8,128)(2,1)S(1)} %get-tuple-element.259.p0), channel_id=1, source_target_pairs={{0,3},{1,2},{2,1},{3,0},{4,7},{5,6},{6,5},{7,4},{8,11},{9,10},{10,... | collective-permute-start | bytes 786440 | tf_op jit(solution)/shard_map/ppermute | solution.py:675
  260.1 13.6 %collective-permute-start.53 = (bf16[64,2048]{1,0:T(8,128)(2,1)S(1)}, bf16[64,2048]{1,0:T(8,128)(2,1)S(1)}, u32[]{:S(2)}, u32[]{:S(2)}) collective-permute-start(bf16[64,2048]{1,0:T(8,128)(2,1)S(1)} %get-tuple-element.270), channel_id=1, source_target_pairs={{0,2},{1,3},{2,0},{3,1},{4,6},{5,7},{6,4},{7,5},{8,10},{9,11},{10,... | collective-permute-start | bytes 786440 | tf_op jit(solution)/shard_map/ppermute | solution.py:675
  263.6 13.4 %collective-permute-start.54 = (bf16[64,2048]{1,0:T(8,128)(2,1)S(1)}, bf16[64,2048]{1,0:T(8,128)(2,1)S(1)}, u32[]{:S(2)}, u32[]{:S(2)}) collective-permute-start(bf16[64,2048]{1,0:T(8,128)(2,1)S(1)} %get-tuple-element.271), channel_id=1, source_target_pairs={{0,3},{1,2},{2,1},{3,0},{4,7},{5,6},{6,5},{7,4},{8,11},{9,10},{10,... | collective-permute-start | bytes 786440 | tf_op jit(solution)/shard_map/ppermute | solution.py:675
  279.0 13.4 %collective-permute-start.57 = (bf16[64,2048]{1,0:T(8,128)(2,1)S(1)}, bf16[64,2048]{1,0:T(8,128)(2,1)S(1)}, u32[]{:S(2)}, u32[]{:S(2)}) collective-permute-start(bf16[64,2048]{1,0:T(8,128)(2,1)S(1)} %get-tuple-element.273.p0), channel_id=1, source_target_pairs={{0,3},{1,2},{2,1},{3,0},{4,7},{5,6},{6,5},{7,4},{8,11},{9,10},{10,... | collective-permute-start | bytes 786440 | tf_op jit(solution)/shard_map/ppermute | solution.py:675
  281.5 22.6 %collective-permute-start.48 = (bf16[64,2048]{1,0:T(8,128)(2,1)S(1)}, bf16[64,2048]{1,0:T(8,128)(2,1)S(1)}, u32[]{:S(2)}, u32[]{:S(2)}) collective-permute-start(bf16[64,2048]{1,0:T(8,128)(2,1)S(1)} %dynamic-slice_bitcast_fusion), channel_id=1, source_target_pairs={{32,64},{64,32},{33,65},{65,33},{34,66},{66,34},{35,67},{67,35},{3... | collective-permute-start | bytes 786440 | tf_op jit(solution)/shard_map/ppermute | solution.py:794
  300.2 13.3 %collective-permute-start.59 = (bf16[64,2048]{1,0:T(8,128)(2,1)S(1)}, bf16[64,2048]{1,0:T(8,128)(2,1)S(1)}, u32[]{:S(2)}, u32[]{:S(2)}) collective-permute-start(bf16[64,2048]{1,0:T(8,128)(2,1)S(1)} %get-tuple-element.278), channel_id=1, source_target_pairs={{0,2},{1,3},{2,0},{3,1},{4,6},{5,7},{6,4},{7,5},{8,10},{9,11},{10,... | collective-permute-start | bytes 786440 | tf_op jit(solution)/shard_map/ppermute | solution.py:675
  303.8 13.4 %collective-permute-start.60 = (bf16[64,2048]{1,0:T(8,128)(2,1)S(1)}, bf16[64,2048]{1,0:T(8,128)(2,1)S(1)}, u32[]{:S(2)}, u32[]{:S(2)}) collective-permute-start(bf16[64,2048]{1,0:T(8,128)(2,1)S(1)} %get-tuple-element.279), channel_id=1, source_target_pairs={{0,3},{1,2},{2,1},{3,0},{4,7},{5,6},{6,5},{7,4},{8,11},{9,10},{10,... | collective-permute-start | bytes 786440 | tf_op jit(solution)/shard_map/ppermute | solution.py:675
  320.9 13.4 %collective-permute-start.63 = (bf16[64,2048]{1,0:T(8,128)(2,1)S(1)}, bf16[64,2048]{1,0:T(8,128)(2,1)S(1)}, u32[]{:S(2)}, u32[]{:S(2)}) collective-permute-start(bf16[64,2048]{1,0:T(8,128)(2,1)S(1)} %get-tuple-element.283.p0), channel_id=1, source_target_pairs={{0,3},{1,2},{2,1},{3,0},{4,7},{5,6},{6,5},{7,4},{8,11},{9,10},{10,... | collective-permute-start | bytes 786440 | tf_op jit(solution)/shard_map/ppermute | solution.py:675
  323.3 41.7 %collective-permute-start.76 = (bf16[256,2048]{1,0:T(8,128)(2,1)S(1)}, bf16[256,2048]{1,0:T(8,128)(2,1)S(1)}, u32[]{:S(2)}, u32[]{:S(2)}) collective-permute-start(bf16[256,2048]{1,0:T(8,128)(2,1)S(1)} %get-tuple-element.275.refs_0_.refs_6_), channel_id=1, source_target_pairs={{0,64},{64,0},{1,65},{65,1},{2,66},{66,2},{3,67},{67,3},{4,68},{68... | collective-permute-start | bytes 3145736 | tf_op jit(solution)/shard_map/ppermute | solution.py:675
  340.4 20.7 %collective-permute-start.73 = (bf16[256,1024]{1,0:T(8,128)(2,1)S(1)}, bf16[256,1024]{1,0:T(8,128)(2,1)S(1)}, u32[]{:S(2)}, u32[]{:S(2)}) collective-permute-start(bf16[256,1024]{1,0:T(8,128)(2,1)S(1)} %get-tuple-element.299), channel_id=1, source_target_pairs={{0,64},{64,0},{1,65},{65,1},{2,66},{66,2},{3,67},{67,3},{4,68},{68... | collective-permute-start | bytes 1572872 | tf_op jit(solution)/shard_map/ppermute | solution.py:675
  346.9 13.4 %collective-permute-start.66 = (bf16[64,2048]{1,0:T(8,128)(2,1)S(1)}, bf16[64,2048]{1,0:T(8,128)(2,1)S(1)}, u32[]{:S(2)}, u32[]{:S(2)}) collective-permute-start(bf16[64,2048]{1,0:T(8,128)(2,1)S(1)} %get-tuple-element.289), channel_id=1, source_target_pairs={{0,3},{1,2},{2,1},{3,0},{4,7},{5,6},{6,5},{7,4},{8,11},{9,10},{10,... | collective-permute-start | bytes 786440 | tf_op jit(solution)/shard_map/ppermute | solution.py:675
  347.1 17.8 %collective-permute-start.75 = (bf16[256,1024]{1,0:T(8,128)(2,1)S(1)}, bf16[256,1024]{1,0:T(8,128)(2,1)S(1)}, u32[]{:S(2)}, u32[]{:S(2)}) collective-permute-start(bf16[256,1024]{1,0:T(8,128)(2,1)S(1)} %get-tuple-element.301), channel_id=1, source_target_pairs={{0,64},{64,0},{1,65},{65,1},{2,66},{66,2},{3,67},{67,3},{4,68},{68... | collective-permute-start | bytes 1572872 | tf_op jit(solution)/shard_map/ppermute | solution.py:675
  361.1 13.3 %collective-permute-start.68 = (bf16[64,2048]{1,0:T(8,128)(2,1)S(1)}, bf16[64,2048]{1,0:T(8,128)(2,1)S(1)}, u32[]{:S(2)}, u32[]{:S(2)}) collective-permute-start(bf16[64,2048]{1,0:T(8,128)(2,1)S(1)} %get-tuple-element.293.p0), channel_id=1, source_target_pairs={{0,2},{1,3},{2,0},{3,1},{4,6},{5,7},{6,4},{7,5},{8,10},{9,11},{10,... | collective-permute-start | bytes 786440 | tf_op jit(solution)/shard_map/ppermute | solution.py:675
  363.2 12.9 %collective-permute-start.69 = (bf16[64,2048]{1,0:T(8,128)(2,1)S(1)}, bf16[64,2048]{1,0:T(8,128)(2,1)S(1)}, u32[]{:S(2)}, u32[]{:S(2)}) collective-permute-start(bf16[64,2048]{1,0:T(8,128)(2,1)S(1)} %get-tuple-element.293.p0), channel_id=1, source_target_pairs={{0,3},{1,2},{2,1},{3,0},{4,7},{5,6},{6,5},{7,4},{8,11},{9,10},{10,... | collective-permute-start | bytes 786440 | tf_op jit(solution)/shard_map/ppermute | solution.py:675
  364.9 18.6 %collective-permute-start.77 = (bf16[64,2048]{1,0:T(8,128)(2,1)S(1)}, bf16[64,2048]{1,0:T(8,128)(2,1)S(1)}, u32[]{:S(2)}, u32[]{:S(2)}) collective-permute-start(bf16[64,2048]{1,0:T(8,128)(2,1)S(1)} %get-tuple-element.316.p0), channel_id=1, source_target_pairs={{0,1},{1,0},{2,3},{3,2},{4,5},{5,4},{6,7},{7,6},{8,9},{9,8},{10,11... | collective-permute-start | bytes 786440 | tf_op jit(solution)/shard_map/ppermute | solution.py:675
  365.0 20.6 %collective-permute-start.78 = (bf16[64,2048]{1,0:T(8,128)(2,1)S(1)}, bf16[64,2048]{1,0:T(8,128)(2,1)S(1)}, u32[]{:S(2)}, u32[]{:S(2)}) collective-permute-start(bf16[64,2048]{1,0:T(8,128)(2,1)S(1)} %get-tuple-element.316.p0), channel_id=1, source_target_pairs={{0,2},{1,3},{2,0},{3,1},{4,6},{5,7},{6,4},{7,5},{8,10},{9,11},{10,... | collective-permute-start | bytes 786440 | tf_op jit(solution)/shard_map/ppermute | solution.py:675
  368.1 19.7 %collective-permute-start.79 = (bf16[64,2048]{1,0:T(8,128)(2,1)S(1)}, bf16[64,2048]{1,0:T(8,128)(2,1)S(1)}, u32[]{:S(2)}, u32[]{:S(2)}) collective-permute-start(bf16[64,2048]{1,0:T(8,128)(2,1)S(1)} %get-tuple-element.316.p0), channel_id=1, source_target_pairs={{0,3},{1,2},{2,1},{3,0},{4,7},{5,6},{6,5},{7,4},{8,11},{9,10},{10,... | collective-permute-start | bytes 786440 | tf_op jit(solution)/shard_map/ppermute | solution.py:675
  402.5 27.1 %collective-permute-start.84 = (bf16[256,2048]{1,0:T(8,128)(2,1)S(1)}, bf16[256,2048]{1,0:T(8,128)(2,1)S(1)}, u32[]{:S(2)}, u32[]{:S(2)}) collective-permute-start(bf16[256,2048]{1,0:T(8,128)(2,1)S(1)} %settle.2), channel_id=1, source_target_pairs={{32,64},{64,32},{33,65},{65,33},{34,66},{66,34},{35,67},{67,35},{3... | collective-permute-start | bytes 3145736 | tf_op jit(solution)/shard_map/ppermute | solution.py:794
  404.6 26.4 %collective-permute-start.85 = (bf16[256,2048]{1,0:T(8,128)(2,1)S(1)}, bf16[256,2048]{1,0:T(8,128)(2,1)S(1)}, u32[]{:S(2)}, u32[]{:S(2)}) collective-permute-start(bf16[256,2048]{1,0:T(8,128)(2,1)S(1)} %settle.2), channel_id=1, source_target_pairs={{0,4},{4,0},{32,68},{36,64},{64,36},{68,32},{96,100},{100,96},{1,5... | collective-permute-start | bytes 3145736 | tf_op jit(solution)/shard_map/ppermute | solution.py:800
  422.7 15.1 %collective-permute-start.87 = (bf16[64,2048]{1,0:T(8,128)(2,1)S(1)}, bf16[64,2048]{1,0:T(8,128)(2,1)S(1)}, u32[]{:S(2)}, u32[]{:S(2)}) collective-permute-start(bf16[64,2048]{1,0:T(8,128)(2,1)S(1)} %get-tuple-element.328), channel_id=1, source_target_pairs={{0,2},{1,3},{2,0},{3,1},{4,6},{5,7},{6,4},{7,5},{8,10},{9,11},{10,... | collective-permute-start | bytes 786440 | tf_op jit(solution)/shard_map/ppermute | solution.py:675
  425.5 14.2 %collective-permute-start.88 = (bf16[64,2048]{1,0:T(8,128)(2,1)S(1)}, bf16[64,2048]{1,0:T(8,128)(2,1)S(1)}, u32[]{:S(2)}, u32[]{:S(2)}) collective-permute-start(bf16[64,2048]{1,0:T(8,128)(2,1)S(1)} %get-tuple-element.329), channel_id=1, source_target_pairs={{0,3},{1,2},{2,1},{3,0},{4,7},{5,6},{6,5},{7,4},{8,11},{9,10},{10,... | collective-permute-start | bytes 786440 | tf_op jit(solution)/shard_map/ppermute | solution.py:675
  442.5 13.4 %collective-permute-start.91 = (bf16[64,2048]{1,0:T(8,128)(2,1)S(1)}, bf16[64,2048]{1,0:T(8,128)(2,1)S(1)}, u32[]{:S(2)}, u32[]{:S(2)}) collective-permute-start(bf16[64,2048]{1,0:T(8,128)(2,1)S(1)} %get-tuple-element.333.p0), channel_id=1, source_target_pairs={{0,3},{1,2},{2,1},{3,0},{4,7},{5,6},{6,5},{7,4},{8,11},{9,10},{10,... | collective-permute-start | bytes 786440 | tf_op jit(solution)/shard_map/ppermute | solution.py:675
  444.3 17.5 %collective-permute-start.93 = (bf16[256,1024]{1,0:T(8,128)(2,1)S(1)}, bf16[256,1024]{1,0:T(8,128)(2,1)S(1)}, u32[]{:S(2)}, u32[]{:S(2)}) collective-permute-start(bf16[256,1024]{1,0:T(8,128)(2,1)S(1)} %get-tuple-element.339), channel_id=1, source_target_pairs={{0,64},{64,0},{1,65},{65,1},{2,66},{66,2},{3,67},{67,3},{4,68},{68... | collective-permute-start | bytes 1572872 | tf_op jit(solution)/shard_map/ppermute | solution.py:675
  471.8 160.8 %reduce-scatter.6.cloned.1.call-start = ((), (), s32[]{:S(2)}) async-start(), calls=%async_computation.6 | async-start | bytes 4718592 | tf_op jit(solution)/shard_map/reduce_scatter | solution.py:756
  471.9 26.0 %collective-permute-start.98 = (bf16[256,2048]{1,0:T(8,128)(2,1)S(1)}, bf16[256,2048]{1,0:T(8,128)(2,1)S(1)}, u32[]{:S(2)}, u32[]{:S(2)}) collective-permute-start(bf16[256,2048]{1,0:T(8,128)(2,1)S(1)} %get-tuple-element.285.refs_0_.refs_6_), channel_id=1, source_target_pairs={{0,64},{64,0},{1,65},{65,1},{2,66},{66,2},{3,67},{67,3},{4,68},{68... | collective-permute-start | bytes 3145736 | tf_op jit(solution)/shard_map/ppermute | solution.py:675
  472.3 25.5 %collective-permute-start.97 = (bf16[256,2048]{1,0:T(8,128)(2,1)S(1)}, bf16[256,2048]{1,0:T(8,128)(2,1)S(1)}, u32[]{:S(2)}, u32[]{:S(2)}) collective-permute-start(bf16[256,2048]{1,0:T(8,128)(2,1)S(1)} %get-tuple-element.342.refs_0_.refs_4_), channel_id=1, source_target_pairs={{0,64},{64,0},{1,65},{65,1},{2,66},{66,2},{3,67},{67,3},{4,68},{68... | collective-permute-start | bytes 3145736 | tf_op jit(solution)/shard_map/ppermute | solution.py:675
  479.0 14.8 %collective-permute-start.95 = (bf16[64,2048]{1,0:T(8,128)(2,1)S(1)}, bf16[64,2048]{1,0:T(8,128)(2,1)S(1)}, u32[]{:S(2)}, u32[]{:S(2)}) collective-permute-start(bf16[64,2048]{1,0:T(8,128)(2,1)S(1)} %get-tuple-element.345), channel_id=1, source_target_pairs={{0,2},{1,3},{2,0},{3,1},{4,6},{5,7},{6,4},{7,5},{8,10},{9,11},{10,... | collective-permute-start | bytes 786440 | tf_op jit(solution)/shard_map/ppermute | solution.py:675
  482.0 13.8 %collective-permute-start.96 = (bf16[64,2048]{1,0:T(8,128)(2,1)S(1)}, bf16[64,2048]{1,0:T(8,128)(2,1)S(1)}, u32[]{:S(2)}, u32[]{:S(2)}) collective-permute-start(bf16[64,2048]{1,0:T(8,128)(2,1)S(1)} %get-tuple-element.346), channel_id=1, source_target_pairs={{0,3},{1,2},{2,1},{3,0},{4,7},{5,6},{6,5},{7,4},{8,11},{9,10},{10,... | collective-permute-start | bytes 786440 | tf_op jit(solution)/shard_map/ppermute | solution.py:675
  507.7 138.3 %reduce-scatter.4.cloned.1.call-start = ((), (), s32[]{:S(2)}) async-start(), calls=%async_computation.5 | async-start | bytes 5242880 | tf_op jit(solution)/shard_map/reduce_scatter | solution.py:775
  507.8 17.7 %collective-permute-start.101 = (bf16[80,2048]{1,0:T(8,128)(2,1)S(1)}, bf16[80,2048]{1,0:T(8,128)(2,1)S(1)}, u32[]{:S(2)}, u32[]{:S(2)}) collective-permute-start(bf16[80,2048]{1,0:T(8,128)(2,1)S(1)} %get-tuple-element.358.p0), channel_id=1, source_target_pairs={{0,3},{1,2},{2,1},{3,0},{4,7},{5,6},{6,5},{7,4},{8,11},{9,10},{10,... | collective-permute-start | bytes 983048 | tf_op jit(solution)/shard_map/ppermute | solution.py:675
  508.8 16.8 %collective-permute-start.99 = (bf16[80,2048]{1,0:T(8,128)(2,1)S(1)}, bf16[80,2048]{1,0:T(8,128)(2,1)S(1)}, u32[]{:S(2)}, u32[]{:S(2)}) collective-permute-start(bf16[80,2048]{1,0:T(8,128)(2,1)S(1)} %get-tuple-element.358.p0), channel_id=1, source_target_pairs={{0,1},{1,0},{2,3},{3,2},{4,5},{5,4},{6,7},{7,6},{8,9},{9,8},{10,11... | collective-permute-start | bytes 983048 | tf_op jit(solution)/shard_map/ppermute | solution.py:675
  553.7 21.3 %collective-permute-start.107 = (bf16[256,384]{1,0:T(8,128)(2,1)S(1)}, bf16[256,384]{1,0:T(8,128)(2,1)S(1)}, u32[]{:S(2)}, u32[]{:S(2)}) collective-permute-start(bf16[256,384]{1,0:T(8,128)(2,1)S(1)} %get-tuple-element.372), channel_id=1, source_target_pairs={{0,16},{8,24},{16,0},{24,8},{1,17},{9,25},{17,1},{25,9},{2,18},{10... | collective-permute-start | bytes 589832 | tf_op jit(solution)/shard_map/ppermute | solution.py:675
  556.9 18.2 %collective-permute-start.108 = (bf16[256,384]{1,0:T(8,128)(2,1)S(1)}, bf16[256,384]{1,0:T(8,128)(2,1)S(1)}, u32[]{:S(2)}, u32[]{:S(2)}) collective-permute-start(bf16[256,384]{1,0:T(8,128)(2,1)S(1)} %get-tuple-element.373), channel_id=1, source_target_pairs={{0,24},{8,16},{16,8},{24,0},{1,25},{9,17},{17,9},{25,1},{2,26},{10... | collective-permute-start | bytes 589832 | tf_op jit(solution)/shard_map/ppermute | solution.py:675
  557.4 23.8 %collective-permute-start.110 = (bf16[256,1536]{1,0:T(8,128)(2,1)S(1)}, bf16[256,1536]{1,0:T(8,128)(2,1)S(1)}, u32[]{:S(2)}, u32[]{:S(2)}) collective-permute-start(bf16[256,1536]{1,0:T(8,128)(2,1)S(1)} %copy-done.41), channel_id=1, source_target_pairs={{0,64},{64,0},{1,65},{65,1},{2,66},{66,2},{3,67},{67,3},{4,68},{68... | collective-permute-start | bytes 2359304 | tf_op jit(solution)/shard_map/ppermute | solution.py:675
  596.7 12.8 %collective-permute-start.114 = (bf16[64,2048]{1,0:T(8,128)(2,1)S(1)}, bf16[64,2048]{1,0:T(8,128)(2,1)S(1)}, u32[]{:S(2)}, u32[]{:S(2)}) collective-permute-start(bf16[64,2048]{1,0:T(8,128)(2,1)S(1)} %copy-done.56), channel_id=1, source_target_pairs={{0,1},{1,0},{2,3},{3,2},{4,5},{5,4},{6,7},{7,6},{8,9},{9,8},{10,11... | collective-permute-start | bytes 786440 | tf_op jit(solution)/shard_map/ppermute | solution.py:675
  597.4 14.7 %collective-permute-start.115 = (bf16[64,2048]{1,0:T(8,128)(2,1)S(1)}, bf16[64,2048]{1,0:T(8,128)(2,1)S(1)}, u32[]{:S(2)}, u32[]{:S(2)}) collective-permute-start(bf16[64,2048]{1,0:T(8,128)(2,1)S(1)} %get-tuple-element.391), channel_id=1, source_target_pairs={{0,3},{1,2},{2,1},{3,0},{4,7},{5,6},{6,5},{7,4},{8,11},{9,10},{10,... | collective-permute-start | bytes 786440 | tf_op jit(solution)/shard_map/ppermute | solution.py:675
  601.4 16.5 %collective-permute-start.127 = (f32[32,512]{1,0:T(8,128)S(1)}, f32[32,512]{1,0:T(8,128)S(1)}, u32[]{:S(2)}, u32[]{:S(2)}) collective-permute-start(f32[32,512]{1,0:T(8,128)S(1)} %fusion.4), channel_id=1, source_target_pairs={{0,16},{8,24},{16,0},{24,8},{1,17},{9,25},{17,1},{25,9},{2,18},{10... | collective-permute-start | bytes 196616 | tf_op jit(solution)/shard_map/ppermute | solution.py:675
  601.5 16.5 %collective-permute-start.128 = (f32[32,512]{1,0:T(8,128)S(1)}, f32[32,512]{1,0:T(8,128)S(1)}, u32[]{:S(2)}, u32[]{:S(2)}) collective-permute-start(f32[32,512]{1,0:T(8,128)S(1)} %fusion.4), channel_id=1, source_target_pairs={{0,8},{8,0},{16,24},{24,16},{1,9},{9,1},{17,25},{25,17},{2,10},{10... | collective-permute-start | bytes 196616 | tf_op jit(solution)/shard_map/ppermute | solution.py:675
  626.4 22.7 %collective-permute-start.118 = (bf16[2,64,2048]{2,1,0:T(8,128)(2,1)S(1)}, bf16[2,64,2048]{2,1,0:T(8,128)(2,1)S(1)}, u32[]{:S(2)}, u32[]{:S(2)}) collective-permute-start(bf16[2,64,2048]{2,1,0:T(8,128)(2,1)S(1)} %pad_maximum_fusion.p0), channel_id=1, source_target_pairs={{0,1},{1,0},{2,3},{3,2},{4,5},{5,4},{6,7},{7,6},{8,9},{9,8},{10,11... | collective-permute-start | bytes 1572872 | tf_op jit(solution)/shard_map/ppermute | solution.py:675
  626.6 29.5 %collective-permute-start.119 = (bf16[2,64,2048]{2,1,0:T(8,128)(2,1)S(1)}, bf16[2,64,2048]{2,1,0:T(8,128)(2,1)S(1)}, u32[]{:S(2)}, u32[]{:S(2)}) collective-permute-start(bf16[2,64,2048]{2,1,0:T(8,128)(2,1)S(1)} %pad_maximum_fusion.p0), channel_id=1, source_target_pairs={{0,2},{1,3},{2,0},{3,1},{4,6},{5,7},{6,4},{7,5},{8,10},{9,11},{10,... | collective-permute-start | bytes 1572872 | tf_op jit(solution)/shard_map/ppermute | solution.py:675
  628.3 28.6 %collective-permute-start.120 = (bf16[2,64,2048]{2,1,0:T(8,128)(2,1)S(1)}, bf16[2,64,2048]{2,1,0:T(8,128)(2,1)S(1)}, u32[]{:S(2)}, u32[]{:S(2)}) collective-permute-start(bf16[2,64,2048]{2,1,0:T(8,128)(2,1)S(1)} %pad_maximum_fusion.p0), channel_id=1, source_target_pairs={{0,3},{1,2},{2,1},{3,0},{4,7},{5,6},{6,5},{7,4},{8,11},{9,10},{10,... | collective-permute-start | bytes 1572872 | tf_op jit(solution)/shard_map/ppermute | solution.py:675
  647.9 15.0 %collective-permute-start.123 = (bf16[128,1024]{1,0:T(8,128)(2,1)S(1)}, bf16[128,1024]{1,0:T(8,128)(2,1)S(1)}, u32[]{:S(2)}, u32[]{:S(2)}) collective-permute-start(bf16[128,1024]{1,0:T(8,128)(2,1)S(1)} %get-tuple-element.398), channel_id=1, source_target_pairs={{0,32},{4,36},{32,0},{36,4},{1,33},{5,37},{33,1},{37,5},{2,34},{6,... | collective-permute-start | bytes 786440 | tf_op jit(solution)/shard_map/ppermute | solution.py:675
  648.0 14.9 %collective-permute-start.124 = (bf16[128,1024]{1,0:T(8,128)(2,1)S(1)}, bf16[128,1024]{1,0:T(8,128)(2,1)S(1)}, u32[]{:S(2)}, u32[]{:S(2)}) collective-permute-start(bf16[128,1024]{1,0:T(8,128)(2,1)S(1)} %get-tuple-element.399), channel_id=1, source_target_pairs={{0,4},{4,0},{32,36},{36,32},{1,5},{5,1},{33,37},{37,33},{2,6},{6,2... | collective-permute-start | bytes 786440 | tf_op jit(solution)/shard_map/ppermute | solution.py:675
  649.2 15.2 %collective-permute-start.125 = (bf16[128,1024]{1,0:T(8,128)(2,1)S(1)}, bf16[128,1024]{1,0:T(8,128)(2,1)S(1)}, u32[]{:S(2)}, u32[]{:S(2)}) collective-permute-start(bf16[128,1024]{1,0:T(8,128)(2,1)S(1)} %get-tuple-element.400), channel_id=1, source_target_pairs={{0,36},{4,32},{32,4},{36,0},{1,37},{5,33},{33,5},{37,1},{2,38},{6,... | collective-permute-start | bytes 786440 | tf_op jit(solution)/shard_map/ppermute | solution.py:675
  (169 other events, 2106.4 us)
Sparse Core Ops, SparseCore 0:
  28.5 51.3 all-gather.2
  82.2 94.5 all-gather.4
  471.9 51.1 reduce-scatter.7
  525.4 60.9 reduce-scatter.5
  595.3 44.6 reduce-scatter.3

commit v4 on v3

--- a/solution.py
+++ b/solution.py
@@ -445,9 +445,18 @@
     return call("heads_result", heads_result_body, [square, square, square, shape((256, 128), F32)], *parts)
 
 
-def hidden_result_body(up, up_far, down, down_far, up_out, down_out):
-    up_out[...] = up[:, :1024].astype(F32) + up_far[...].astype(F32)
-    down_out[...] = (down[:, :1024].astype(F32) + down_far[...].astype(F32)).T
+def far_body(up, down, out):
+    out[:128] = up[:, 1024:]
+    out[128:] = down[:, 1024:]
+
+
+def far_halves(up, down):
+    return call("far_halves", far_body, [shape((256, 1024))], up, down)[0]
+
+
+def hidden_result_body(up, down, far, up_out, down_out):
+    up_out[...] = up[:, :1024].astype(F32) + far[:128].astype(F32)
+    down_out[...] = (down[:, :1024].astype(F32) + far[128:].astype(F32)).T
 
 
 def hidden_result(*parts):
@@ -780,10 +789,10 @@
     sums = jnp.concatenate([sums, heads, jnp.zeros((1, 512), F32)])
     sums = line_sum(line_sum(sums + sibling(sums), "x"), Y).reshape(-1)
     result = gather(by_micro(spot[4], same, other), "z")
-    far = [swap(total[:, 1024:], "yhi", 1, 2) for total in (up_sum, down_sum)]
-    rest, *far = tie(rest, *far)
+    far = swap(far_halves(up_sum, down_sum), "yhi", 1, 2)
+    rest, far = tie(rest, far)
     rest = heads_result(exchange(cut(spot, rest), Y))
-    return settle(spot, result), (*rest, *hidden_result(up_sum, far[0], down_sum, far[1])), sums
+    return settle(spot, result), (*rest, *hidden_result(up_sum, down_sum, far)), sums
 
 
 def two_layers(one, two):

time: 681 us -> 679 us (level)
    unnamed x208 -> x212, local copies, waits for them, and re-layouts: 28.8 us -> 31.1 us
    ppermute x127 -> x126, starting transfers between devices: 182 us -> 180 us  [swap(): return lax.ppermute(values, axis, [(i, i ^ bits) for i in range(size)])]
    pallas_call x29 -> x30, Pallas kernels: 46.3 us -> 46.3 us  [call(): pl.pallas_call(body, in_specs=specs, out_specs=[pl.BlockSpec(memory_space...]
    ppermute x127 -> x126, waiting for transfers between devices: 269 us -> 269 us  [swap(): return lax.ppermute(values, axis, [(i, i ^ bits) for i in range(size)])]
  transfers between devices with their start and end apart: 138 -> 137, of which waited for: 84 -> 83; matrix products, arithmetic and copies ran while one was open for 2% -> 2% of each run, Pallas kernels for 12% -> 12%
where the time goes in v4:
time: 679 us; the launch traced here: 670 us
  waiting for transfers between devices  296 us (44%)
  starting transfers between devices  195 us (29%)
  Pallas kernels  123 us (18%)
  local copies, waits for them, and re-layouts  35 us (5%)
  between operations  15.6 us (2%)
    ppermute x126, waiting for transfers between devices, swap(): return lax.ppermute(values, axis, [(i, i ^ bits) for i in range(size)])  269 us
    ppermute x126, starting transfers between devices, swap(): return lax.ppermute(values, axis, [(i, i ^ bits) for i in range(size)])  180 us
    pallas_call x30, Pallas kernels, call(): pl.pallas_call(body, in_specs=specs, out_specs=[pl.BlockSpec(memory_space...  46.3 us
    pallas_call x5, Pallas kernels, old_call(): pl.pallas_call(inner, in_specs=[pl.BlockSpec(memory_space=pltpu.SMEM)] +...  44.7 us
    unnamed x212, local copies, waits for them, and re-layouts  31.1 us
    pallas_call x8, Pallas kernels, rows_mm(): pl.pallas_call(body, in_specs=[pl.BlockSpec(memory_space=pltpu.SMEM)] + [...  30.5 us
  transfers between devices with their start and end apart: 137, of which 83 were waited for; matrix products, arithmetic and copies ran while one was open for 2% of the time, Pallas kernels for 12%

profile of v4, /device:TPU:1, one launch (start us, length us, event | category | flops | bytes accessed | tf_op | source)
XLA Modules:
  0.0 670.3 jit_solution(12476398179107690714)
XLA Ops:
  16.3 8.4 %collective-permute-done.1.refs_2_ = bf16[128,1024]{1,0:T(8,128)(2,1)S(1)} collective-permute-done((bf16[128,1024]{1,0:T(8,128)(2,1)S(1)}, bf16[128,1024]{1,0:T(8,128)(2,1)S(1)}, u32[]{:S(2)}, u32[]{:S(2)}) %collective-permute-start.1) | collective-permute-done | bytes 262176 | tf_op jit(solution)/shard_map/ppermute | solution.py:684
  33.1 5.4 collective-permute-done.3
  41.2 3.3 collective-permute-start.5
  48.6 3.5 collective-permute-done.5.p2
  55.7 3.4 collective-permute-start.27
  60.1 4.3 collective-permute-done.25.refs_1_
  64.4 3.8 collective-permute-done.26.refs_2_
  68.3 3.6 collective-permute-done.27.refs_3_
  76.2 3.9 collective-permute-done.8
  81.4 6.0 rows_qkv.2
  94.1 3.7 collective-permute-start.13
  97.8 3.9 collective-permute-done.10.refs_2_
  101.7 5.5 collective-permute-start.14
  109.8 5.3 attend_fwd.2
  138.0 8.1 %collective-permute-done.20.refs_2_ = bf16[64,2048]{1,0:T(8,128)(2,1)S(1)} collective-permute-done((bf16[64,2048]{1,0:T(8,128)(2,1)S(1)}, bf16[64,2048]{1,0:T(8,128)(2,1)S(1)}, u32[]{:S(2)}, u32[]{:S(2)}) %collective-permute-start.20) | collective-permute-done | bytes 262176 | tf_op jit(solution)/shard_map/ppermute | solution.py:684
  155.1 5.5 collective-permute-done.23.p2
  160.6 3.4 collective-permute-done.24.p3
  164.1 12.7 %all-gather.5.cloned.1.call-done.w = bf16[2048,4096]{1,0:T(8,128)(2,1)} async-done(((bf16[256,4096]{1,0:T(8,128)(2,1)}), bf16[2048,4096]{1,0:T(8,128)(2,1)}) %all-gather.5.cloned.1.call-update) | async-done | bytes 16777232 | tf_op jit(solution)/shard_map/all_gather | solution.py:847
  176.7 7.4 %rows_up.2 = (bf16[256,1024]{1,0:T(8,128)(2,1)S(1)}, bf16[256,1024]{1,0:T(8,128)(2,1)S(1)}, bf16[256,2048]{1,0:T(8,128)(2,1)S(1)}, bf16[256,2048]{1,0:T(8,128)(2...) custom-call(s32[5]{0:T(128)S(1)} %stack.50.spot.spot_ref, ...), custom_call_target="tpu_custom_call" | custom-call | flops 2147483648 | bytes 8388608 | tf_op jit(solution)/shard_map/rows_up/pallas_call | solution.py:241
  198.9 5.4 collective-permute-done.32.refs_2_
  205.4 5.0 collective-permute-done.33.refs_3_
  214.9 3.5 collective-permute-done.38.p1
  218.4 4.8 collective-permute-done.39.p2
  244.0 6.2 attend_fwd.3
  250.3 3.9 collective-permute-start.50
  260.1 3.6 collective-permute-start.53
  265.9 7.7 %collective-permute-done.53.refs_2_ = bf16[64,2048]{1,0:T(8,128)(2,1)S(1)} collective-permute-done((bf16[64,2048]{1,0:T(8,128)(2,1)S(1)}, bf16[64,2048]{1,0:T(8,128)(2,1)S(1)}, u32[]{:S(2)}, u32[]{:S(2)}) %collective-permute-start.53) | collective-permute-done | bytes 262176 | tf_op jit(solution)/shard_map/ppermute | solution.py:684
  273.6 3.4 collective-permute-done.54.refs_3_
  281.5 4.5 collective-permute-start.48
  288.7 3.6 collective-permute-done.57.p3
  292.3 4.1 rows_up.3
  300.3 3.6 collective-permute-start.59
  305.9 7.7 %collective-permute-done.59.refs_2_ = bf16[64,2048]{1,0:T(8,128)(2,1)S(1)} collective-permute-done((bf16[64,2048]{1,0:T(8,128)(2,1)S(1)}, bf16[64,2048]{1,0:T(8,128)(2,1)S(1)}, u32[]{:S(2)}, u32[]{:S(2)}) %collective-permute-start.59) | collective-permute-done | bytes 262176 | tf_op jit(solution)/shard_map/ppermute | solution.py:684
  313.6 3.6 collective-permute-done.60.refs_3_
  326.3 4.4 collective-permute-done.62.p2
  330.7 3.6 collective-permute-done.63.p3
  343.1 3.8 collective-permute-start.65
  347.1 3.4 collective-permute-start.75
  350.5 3.2 collective-permute-done.65.refs_2_
  353.7 3.2 collective-permute-start.74
  356.9 3.4 collective-permute-done.66.refs_3_
  369.0 5.4 collective-permute-done.68.p2
  379.9 3.7 collective-permute-done.72.refs_11_
  388.2 6.5 attend_bwd.2
  394.8 7.2 %collective-permute-start.80 = (f32[1024,256]{1,0:T(8,128)S(1)}, f32[1024,256]{1,0:T(8,128)S(1)}, u32[]{:S(2)}, u32[]{:S(2)}) collective-permute-start(f32[1024,256]{1,0:T(8,128)S(1)} %get-tuple-element.309), channel_id=1, source_target_pairs={{0,64},{64,0},{1,65},{65,1},{2,66},{66,2},{3,67},{67,3},{4,68},{68... | collective-permute-start | bytes 3145736 | tf_op jit(solution)/shard_map/ppermute | solution.py:684
  413.7 3.5 collective-permute-done.82.refs_2_
  431.1 6.7 collective-permute-done.87.refs_2_
  446.8 6.3 collective-permute-done.90.p2
  463.3 8.5 %weight_term.2 = bf16[1024,2048]{1,0:T(8,128)(2,1)} custom-call(s32[5]{0:T(128)S(1)} %stack.50.spot.spot_ref, bf16[256,1024]{1,0:T(8,128)(2,1)S(1)} %get-tuple-element.335.refs_0_, bf16[256,1024]{1,0:T(8,128)(2,1)S(1)} %collective-permute-done.92.refs_1_, bf16[256,1024]{1,0:T(8,128)(2,1)} %copy-done.51, bf16[256,1024]{1,0:T(8,128)(2,1)} %copy-done.89, ...), custom_call_target="tpu_custom_call" | custom-call | flops 4294967296 | bytes 8388608 | tf_op jit(solution)/shard_map/weight_term/pallas_call | solution.py:325
  472.7 3.4 copy-done.5
  483.0 3.7 collective-permute-done.94.refs_1_
  486.7 7.2 %collective-permute-done.95.refs_2_ = bf16[64,2048]{1,0:T(8,128)(2,1)S(1)} collective-permute-done((bf16[64,2048]{1,0:T(8,128)(2,1)S(1)}, bf16[64,2048]{1,0:T(8,128)(2,1)S(1)}, u32[]{:S(2)}, u32[]{:S(2)}) %collective-permute-start.95) | collective-permute-done | bytes 262176 | tf_op jit(solution)/shard_map/ppermute | solution.py:684
  498.9 8.8 %weight_term.3 = bf16[1024,2048]{1,0:T(8,128)(2,1)} custom-call(s32[5]{0:T(128)S(1)} %stack.50.spot.spot_ref, bf16[256,1024]{1,0:T(8,128)(2,1)} %copy-done.46, bf16[256,1024]{1,0:T(8,128)(2,1)} %copy-done.86, bf16[256,1024]{1,0:T(8,128)(2,1)} %copy-done.47, bf16[256,1024]{1,0:T(8,128)(2,1)} %copy-done.88, ...), custom_call_target="tpu_custom_call" | custom-call | flops 4294967296 | bytes 8388608 | tf_op jit(solution)/shard_map/weight_term/pallas_call | solution.py:325
  510.5 6.5 collective-permute-done.100.p2
  517.0 8.6 %collective-permute-done.101.p3 = bf16[80,2048]{1,0:T(8,128)(2,1)S(1)} collective-permute-done((bf16[80,2048]{1,0:T(8,128)(2,1)S(1)}, bf16[80,2048]{1,0:T(8,128)(2,1)S(1)}, u32[]{:S(2)}, u32[]{:S(2)}) %collective-permute-start.101) | collective-permute-done | bytes 327712 | tf_op jit(solution)/shard_map/ppermute | solution.py:684
  525.6 3.4 copy-done.3
  540.6 8.3 %attend_bwd.3 = (bf16[256,128]{1,0:T(8,128)(2,1)S(1)}, bf16[256,128]{1,0:T(8,128)(2,1)S(1)}, bf16[256,128]{1,0:T(8,128)(2,1)S(1)}, bf16[256,128]{1,0:T(8,128)(2,...) custom-call(s32[5]{0:T(128)S(1)} %stack.50.spot.spot_ref, bf16[256,384]{1,0:T(8,128)(2,1)} %copy-done.61, ...), custom_call_target="tpu_custom_call" | custom-call | flops 4294967296 | bytes 8388608 | tf_op jit(solution)/shard_map/attend_bwd/pallas_call | solution.py:325
  558.7 6.1 collective-permute-done.106.refs_1_
  564.8 10.2 %collective-permute-done.107.refs_2_ = bf16[256,384]{1,0:T(8,128)(2,1)S(1)} collective-permute-done((bf16[256,384]{1,0:T(8,128)(2,1)S(1)}, bf16[256,384]{1,0:T(8,128)(2,1)S(1)}, u32[]{:S(2)}, u32[]{:S(2)}) %collective-permute-start.107) | collective-permute-done | bytes 196640 | tf_op jit(solution)/shard_map/ppermute | solution.py:684
  582.4 12.6 %head_terms.1 = (bf16[1024,2048]{1,0:T(8,128)(2,1)}, f32[1,1536]{1,0:T(1,128)S(1)}) custom-call(s32[5]{0:T(128)S(1)} %stack.50.spot.spot_ref, bf16[256,1024]{1,0:T(8,128)(2,1)} %copy-done.44, bf16[256,1024]{1,0:T(8,128)(2,1)} %copy-done.85, bf16[256,1024]{1,0:T(8,128)(2,1)} %copy-done.45, bf16[256,1024]{1,0:T(8,128)(2,1)} %copy-done.87, ...), custom_call_target="tpu_custom_call" | custom-call | flops 4294967296 | bytes 8388608 | tf_op jit(solution)/shard_map/head_terms/pallas_call | solution.py:325
  602.6 3.3 collective-permute-done.113
  621.3 5.0 collective-permute-done.117
  634.4 7.6 %collective-permute-done.121.far = bf16[256,1024]{1,0:T(8,128)(2,1)S(1)} collective-permute-done((bf16[256,1024]{1,0:T(8,128)(2,1)S(1)}, bf16[256,1024]{1,0:T(8,128)(2,1)S(1)}, u32[]{:S(2)}, u32[]{:S(2)}) %collective-permute-start.121) | collective-permute-done | bytes 524320 | tf_op jit(solution)/shard_map/ppermute | solution.py:684
  653.0 3.6 collective-permute-done.120.p3
  (520 shorter events, 312.0 us)
Async XLA Ops:
  7.2 74.2 %all-gather.3.cloned.1.call-start = ((), (), s32[]{:S(2)}) async-start(), calls=%async_computation.3 | async-start | bytes 9437184 | tf_op jit(solution)/shard_map/all_gather | solution.py:847
  10.7 14.0 %collective-permute-start.1 = (bf16[128,1024]{1,0:T(8,128)(2,1)S(1)}, bf16[128,1024]{1,0:T(8,128)(2,1)S(1)}, u32[]{:S(2)}, u32[]{:S(2)}) collective-permute-start(bf16[128,1024]{1,0:T(8,128)(2,1)S(1)} %pack_heads.1.refs_0_), channel_id=1, source_target_pairs={{0,4},{4,0},{32,36},{36,32},{1,5},{5,1},{33,37},{37,33},{2,6},{6,2... | collective-permute-start | bytes 786440 | tf_op jit(solution)/shard_map/ppermute | solution.py:684
  13.3 13.4 %collective-permute-start.2 = (bf16[128,1024]{1,0:T(8,128)(2,1)S(1)}, bf16[128,1024]{1,0:T(8,128)(2,1)S(1)}, u32[]{:S(2)}, u32[]{:S(2)}) collective-permute-start(bf16[128,1024]{1,0:T(8,128)(2,1)S(1)} %pack_heads.1.refs_0_), channel_id=1, source_target_pairs={{0,36},{4,32},{32,4},{36,0},{1,37},{5,33},{33,5},{37,1},{2,38},{6,... | collective-permute-start | bytes 786440 | tf_op jit(solution)/shard_map/ppermute | solution.py:684
  28.4 148.3 %all-gather.5.cloned.1.call-start = ((), (), s32[]{:S(2)}) async-start(), calls=%async_computation.4 | async-start | bytes 18874368 | tf_op jit(solution)/shard_map/all_gather | solution.py:847
  44.7 14.4 %collective-permute-start.29 = (bf16[128,1024]{1,0:T(8,128)(2,1)S(1)}, bf16[128,1024]{1,0:T(8,128)(2,1)S(1)}, u32[]{:S(2)}, u32[]{:S(2)}) collective-permute-start(bf16[128,1024]{1,0:T(8,128)(2,1)S(1)} %pack.1.refs_4_), channel_id=1, source_target_pairs={{0,4},{4,0},{32,36},{36,32},{1,5},{5,1},{33,37},{37,33},{2,6},{6,2... | collective-permute-start | bytes 786440 | tf_op jit(solution)/shard_map/ppermute | solution.py:684
  46.6 13.5 %collective-permute-start.30 = (bf16[128,1024]{1,0:T(8,128)(2,1)S(1)}, bf16[128,1024]{1,0:T(8,128)(2,1)S(1)}, u32[]{:S(2)}, u32[]{:S(2)}) collective-permute-start(bf16[128,1024]{1,0:T(8,128)(2,1)S(1)} %pack.1.refs_4_), channel_id=1, source_target_pairs={{0,36},{4,32},{32,4},{36,0},{1,37},{5,33},{33,5},{37,1},{2,38},{6,... | collective-permute-start | bytes 786440 | tf_op jit(solution)/shard_map/ppermute | solution.py:684
  55.2 13.0 %collective-permute-start.26 = (bf16[128,1024]{1,0:T(8,128)(2,1)S(1)}, bf16[128,1024]{1,0:T(8,128)(2,1)S(1)}, u32[]{:S(2)}, u32[]{:S(2)}) collective-permute-start(bf16[128,1024]{1,0:T(8,128)(2,1)S(1)} %copy-done.22), channel_id=1, source_target_pairs={{0,4},{4,0},{32,36},{36,32},{1,5},{5,1},{33,37},{37,33},{2,6},{6,2... | collective-permute-start | bytes 786440 | tf_op jit(solution)/shard_map/ppermute | solution.py:684
  55.7 16.2 %collective-permute-start.27 = (bf16[128,1024]{1,0:T(8,128)(2,1)S(1)}, bf16[128,1024]{1,0:T(8,128)(2,1)S(1)}, u32[]{:S(2)}, u32[]{:S(2)}) collective-permute-start(bf16[128,1024]{1,0:T(8,128)(2,1)S(1)} %copy-done.22), channel_id=1, source_target_pairs={{0,36},{4,32},{32,4},{36,0},{1,37},{5,33},{33,5},{37,1},{2,38},{6,... | collective-permute-start | bytes 786440 | tf_op jit(solution)/shard_map/ppermute | solution.py:684
  73.9 552.6 %reduce-scatter.8.cloned.1.call-start = ((), (), s32[]{:S(2)}) async-start(), calls=%async_computation.7 | async-start | bytes 4718592 | tf_op jit(solution)/shard_map/reduce_scatter | solution.py:759
  91.9 15.4 %collective-permute-start.11 = (bf16[256,384]{1,0:T(8,128)(2,1)S(1)}, bf16[256,384]{1,0:T(8,128)(2,1)S(1)}, u32[]{:S(2)}, u32[]{:S(2)}) collective-permute-start(bf16[256,384]{1,0:T(8,128)(2,1)S(1)} %get-tuple-element.232), channel_id=1, source_target_pairs={{0,24},{8,16},{16,8},{24,0},{1,25},{9,17},{17,9},{25,1},{2,26},{10... | collective-permute-start | bytes 589832 | tf_op jit(solution)/shard_map/ppermute | solution.py:684
  92.1 16.7 %collective-permute-start.12 = (bf16[256,384]{1,0:T(8,128)(2,1)S(1)}, bf16[256,384]{1,0:T(8,128)(2,1)S(1)}, u32[]{:S(2)}, u32[]{:S(2)}) collective-permute-start(bf16[256,384]{1,0:T(8,128)(2,1)S(1)} %get-tuple-element.229.refs_0_), channel_id=1, source_target_pairs={{0,64},{64,0},{1,65},{65,1},{2,66},{66,2},{3,67},{67,3},{4,68},{68... | collective-permute-start | bytes 589832 | tf_op jit(solution)/shard_map/ppermute | solution.py:684
  94.1 14.6 %collective-permute-start.13 = (bf16[256,384]{1,0:T(8,128)(2,1)S(1)}, bf16[256,384]{1,0:T(8,128)(2,1)S(1)}, u32[]{:S(2)}, u32[]{:S(2)}) collective-permute-start(bf16[256,384]{1,0:T(8,128)(2,1)S(1)} %collective-permute-done.9.refs_1_), channel_id=1, source_target_pairs={{0,64},{64,0},{1,65},{65,1},{2,66},{66,2},{3,67},{67,3},{4,68},{68... | collective-permute-start | bytes 589832 | tf_op jit(solution)/shard_map/ppermute | solution.py:684
  132.1 14.0 %collective-permute-start.20 = (bf16[64,2048]{1,0:T(8,128)(2,1)S(1)}, bf16[64,2048]{1,0:T(8,128)(2,1)S(1)}, u32[]{:S(2)}, u32[]{:S(2)}) collective-permute-start(bf16[64,2048]{1,0:T(8,128)(2,1)S(1)} %get-tuple-element.242), channel_id=1, source_target_pairs={{0,2},{1,3},{2,0},{3,1},{4,6},{5,7},{6,4},{7,5},{8,10},{9,11},{10,... | collective-permute-start | bytes 786440 | tf_op jit(solution)/shard_map/ppermute | solution.py:684
  135.3 13.5 %collective-permute-start.21 = (bf16[64,2048]{1,0:T(8,128)(2,1)S(1)}, bf16[64,2048]{1,0:T(8,128)(2,1)S(1)}, u32[]{:S(2)}, u32[]{:S(2)}) collective-permute-start(bf16[64,2048]{1,0:T(8,128)(2,1)S(1)} %get-tuple-element.243), channel_id=1, source_target_pairs={{0,3},{1,2},{2,1},{3,0},{4,7},{5,6},{6,5},{7,4},{8,11},{9,10},{10,... | collective-permute-start | bytes 786440 | tf_op jit(solution)/shard_map/ppermute | solution.py:684
  150.6 13.5 %collective-permute-start.24 = (bf16[64,2048]{1,0:T(8,128)(2,1)S(1)}, bf16[64,2048]{1,0:T(8,128)(2,1)S(1)}, u32[]{:S(2)}, u32[]{:S(2)}) collective-permute-start(bf16[64,2048]{1,0:T(8,128)(2,1)S(1)} %get-tuple-element.244.p0), channel_id=1, source_target_pairs={{0,3},{1,2},{2,1},{3,0},{4,7},{5,6},{6,5},{7,4},{8,11},{9,10},{10,... | collective-permute-start | bytes 786440 | tf_op jit(solution)/shard_map/ppermute | solution.py:684
  185.0 26.0 %collective-permute-start.37 = (bf16[256,2048]{1,0:T(8,128)(2,1)S(1)}, bf16[256,2048]{1,0:T(8,128)(2,1)S(1)}, u32[]{:S(2)}, u32[]{:S(2)}) collective-permute-start(bf16[256,2048]{1,0:T(8,128)(2,1)S(1)} %get-tuple-element.247.refs_0_.refs_4_), channel_id=1, source_target_pairs={{0,64},{64,0},{1,65},{65,1},{2,66},{66,2},{3,67},{67,3},{4,68},{68... | collective-permute-start | bytes 3145736 | tf_op jit(solution)/shard_map/ppermute | solution.py:684
  189.3 15.0 %collective-permute-start.32 = (bf16[64,2048]{1,0:T(8,128)(2,1)S(1)}, bf16[64,2048]{1,0:T(8,128)(2,1)S(1)}, u32[]{:S(2)}, u32[]{:S(2)}) collective-permute-start(bf16[64,2048]{1,0:T(8,128)(2,1)S(1)} %get-tuple-element.251), channel_id=1, source_target_pairs={{0,2},{1,3},{2,0},{3,1},{4,6},{5,7},{6,4},{7,5},{8,10},{9,11},{10,... | collective-permute-start | bytes 786440 | tf_op jit(solution)/shard_map/ppermute | solution.py:684
  192.5 18.4 %collective-permute-start.34 = (bf16[256,1024]{1,0:T(8,128)(2,1)S(1)}, bf16[256,1024]{1,0:T(8,128)(2,1)S(1)}, u32[]{:S(2)}, u32[]{:S(2)}) collective-permute-start(bf16[256,1024]{1,0:T(8,128)(2,1)S(1)} %copy-done.53), channel_id=1, source_target_pairs={{0,64},{64,0},{1,65},{65,1},{2,66},{66,2},{3,67},{67,3},{4,68},{68... | collective-permute-start | bytes 1572872 | tf_op jit(solution)/shard_map/ppermute | solution.py:684
  193.3 17.6 %collective-permute-start.36 = (bf16[256,1024]{1,0:T(8,128)(2,1)S(1)}, bf16[256,1024]{1,0:T(8,128)(2,1)S(1)}, u32[]{:S(2)}, u32[]{:S(2)}) collective-permute-start(bf16[256,1024]{1,0:T(8,128)(2,1)S(1)} %get-tuple-element.257), channel_id=1, source_target_pairs={{0,64},{64,0},{1,65},{65,1},{2,66},{66,2},{3,67},{67,3},{4,68},{68... | collective-permute-start | bytes 1572872 | tf_op jit(solution)/shard_map/ppermute | solution.py:684
  196.1 14.4 %collective-permute-start.33 = (bf16[64,2048]{1,0:T(8,128)(2,1)S(1)}, bf16[64,2048]{1,0:T(8,128)(2,1)S(1)}, u32[]{:S(2)}, u32[]{:S(2)}) collective-permute-start(bf16[64,2048]{1,0:T(8,128)(2,1)S(1)} %get-tuple-element.252), channel_id=1, source_target_pairs={{0,3},{1,2},{2,1},{3,0},{4,7},{5,6},{6,5},{7,4},{8,11},{9,10},{10,... | collective-permute-start | bytes 786440 | tf_op jit(solution)/shard_map/ppermute | solution.py:684
  211.9 14.1 %collective-permute-start.40 = (bf16[64,2048]{1,0:T(8,128)(2,1)S(1)}, bf16[64,2048]{1,0:T(8,128)(2,1)S(1)}, u32[]{:S(2)}, u32[]{:S(2)}) collective-permute-start(bf16[64,2048]{1,0:T(8,128)(2,1)S(1)} %get-tuple-element.258.p0), channel_id=1, source_target_pairs={{0,3},{1,2},{2,1},{3,0},{4,7},{5,6},{6,5},{7,4},{8,11},{9,10},{10,... | collective-permute-start | bytes 786440 | tf_op jit(solution)/shard_map/ppermute | solution.py:684
  260.1 13.5 %collective-permute-start.53 = (bf16[64,2048]{1,0:T(8,128)(2,1)S(1)}, bf16[64,2048]{1,0:T(8,128)(2,1)S(1)}, u32[]{:S(2)}, u32[]{:S(2)}) collective-permute-start(bf16[64,2048]{1,0:T(8,128)(2,1)S(1)} %get-tuple-element.269), channel_id=1, source_target_pairs={{0,2},{1,3},{2,0},{3,1},{4,6},{5,7},{6,4},{7,5},{8,10},{9,11},{10,... | collective-permute-start | bytes 786440 | tf_op jit(solution)/shard_map/ppermute | solution.py:684
  263.6 13.4 %collective-permute-start.54 = (bf16[64,2048]{1,0:T(8,128)(2,1)S(1)}, bf16[64,2048]{1,0:T(8,128)(2,1)S(1)}, u32[]{:S(2)}, u32[]{:S(2)}) collective-permute-start(bf16[64,2048]{1,0:T(8,128)(2,1)S(1)} %get-tuple-element.270), channel_id=1, source_target_pairs={{0,3},{1,2},{2,1},{3,0},{4,7},{5,6},{6,5},{7,4},{8,11},{9,10},{10,... | collective-permute-start | bytes 786440 | tf_op jit(solution)/shard_map/ppermute | solution.py:684
  279.0 13.4 %collective-permute-start.57 = (bf16[64,2048]{1,0:T(8,128)(2,1)S(1)}, bf16[64,2048]{1,0:T(8,128)(2,1)S(1)}, u32[]{:S(2)}, u32[]{:S(2)}) collective-permute-start(bf16[64,2048]{1,0:T(8,128)(2,1)S(1)} %get-tuple-element.272.p0), channel_id=1, source_target_pairs={{0,3},{1,2},{2,1},{3,0},{4,7},{5,6},{6,5},{7,4},{8,11},{9,10},{10,... | collective-permute-start | bytes 786440 | tf_op jit(solution)/shard_map/ppermute | solution.py:684
  281.5 22.6 %collective-permute-start.48 = (bf16[64,2048]{1,0:T(8,128)(2,1)S(1)}, bf16[64,2048]{1,0:T(8,128)(2,1)S(1)}, u32[]{:S(2)}, u32[]{:S(2)}) collective-permute-start(bf16[64,2048]{1,0:T(8,128)(2,1)S(1)} %dynamic-slice_bitcast_fusion), channel_id=1, source_target_pairs={{32,64},{64,32},{33,65},{65,33},{34,66},{66,34},{35,67},{67,35},{3... | collective-permute-start | bytes 786440 | tf_op jit(solution)/shard_map/ppermute | solution.py:803
  300.3 13.3 %collective-permute-start.59 = (bf16[64,2048]{1,0:T(8,128)(2,1)S(1)}, bf16[64,2048]{1,0:T(8,128)(2,1)S(1)}, u32[]{:S(2)}, u32[]{:S(2)}) collective-permute-start(bf16[64,2048]{1,0:T(8,128)(2,1)S(1)} %get-tuple-element.277), channel_id=1, source_target_pairs={{0,2},{1,3},{2,0},{3,1},{4,6},{5,7},{6,4},{7,5},{8,10},{9,11},{10,... | collective-permute-start | bytes 786440 | tf_op jit(solution)/shard_map/ppermute | solution.py:684
  303.8 13.4 %collective-permute-start.60 = (bf16[64,2048]{1,0:T(8,128)(2,1)S(1)}, bf16[64,2048]{1,0:T(8,128)(2,1)S(1)}, u32[]{:S(2)}, u32[]{:S(2)}) collective-permute-start(bf16[64,2048]{1,0:T(8,128)(2,1)S(1)} %get-tuple-element.278), channel_id=1, source_target_pairs={{0,3},{1,2},{2,1},{3,0},{4,7},{5,6},{6,5},{7,4},{8,11},{9,10},{10,... | collective-permute-start | bytes 786440 | tf_op jit(solution)/shard_map/ppermute | solution.py:684
  320.9 13.4 %collective-permute-start.63 = (bf16[64,2048]{1,0:T(8,128)(2,1)S(1)}, bf16[64,2048]{1,0:T(8,128)(2,1)S(1)}, u32[]{:S(2)}, u32[]{:S(2)}) collective-permute-start(bf16[64,2048]{1,0:T(8,128)(2,1)S(1)} %get-tuple-element.282.p0), channel_id=1, source_target_pairs={{0,3},{1,2},{2,1},{3,0},{4,7},{5,6},{6,5},{7,4},{8,11},{9,10},{10,... | collective-permute-start | bytes 786440 | tf_op jit(solution)/shard_map/ppermute | solution.py:684
  323.3 41.7 %collective-permute-start.76 = (bf16[256,2048]{1,0:T(8,128)(2,1)S(1)}, bf16[256,2048]{1,0:T(8,128)(2,1)S(1)}, u32[]{:S(2)}, u32[]{:S(2)}) collective-permute-start(bf16[256,2048]{1,0:T(8,128)(2,1)S(1)} %get-tuple-element.274.refs_0_.refs_6_), channel_id=1, source_target_pairs={{0,64},{64,0},{1,65},{65,1},{2,66},{66,2},{3,67},{67,3},{4,68},{68... | collective-permute-start | bytes 3145736 | tf_op jit(solution)/shard_map/ppermute | solution.py:684
  340.4 20.7 %collective-permute-start.73 = (bf16[256,1024]{1,0:T(8,128)(2,1)S(1)}, bf16[256,1024]{1,0:T(8,128)(2,1)S(1)}, u32[]{:S(2)}, u32[]{:S(2)}) collective-permute-start(bf16[256,1024]{1,0:T(8,128)(2,1)S(1)} %get-tuple-element.298), channel_id=1, source_target_pairs={{0,64},{64,0},{1,65},{65,1},{2,66},{66,2},{3,67},{67,3},{4,68},{68... | collective-permute-start | bytes 1572872 | tf_op jit(solution)/shard_map/ppermute | solution.py:684
  346.9 13.4 %collective-permute-start.66 = (bf16[64,2048]{1,0:T(8,128)(2,1)S(1)}, bf16[64,2048]{1,0:T(8,128)(2,1)S(1)}, u32[]{:S(2)}, u32[]{:S(2)}) collective-permute-start(bf16[64,2048]{1,0:T(8,128)(2,1)S(1)} %get-tuple-element.288), channel_id=1, source_target_pairs={{0,3},{1,2},{2,1},{3,0},{4,7},{5,6},{6,5},{7,4},{8,11},{9,10},{10,... | collective-permute-start | bytes 786440 | tf_op jit(solution)/shard_map/ppermute | solution.py:684
  347.1 17.8 %collective-permute-start.75 = (bf16[256,1024]{1,0:T(8,128)(2,1)S(1)}, bf16[256,1024]{1,0:T(8,128)(2,1)S(1)}, u32[]{:S(2)}, u32[]{:S(2)}) collective-permute-start(bf16[256,1024]{1,0:T(8,128)(2,1)S(1)} %get-tuple-element.300), channel_id=1, source_target_pairs={{0,64},{64,0},{1,65},{65,1},{2,66},{66,2},{3,67},{67,3},{4,68},{68... | collective-permute-start | bytes 1572872 | tf_op jit(solution)/shard_map/ppermute | solution.py:684
  361.1 13.3 %collective-permute-start.68 = (bf16[64,2048]{1,0:T(8,128)(2,1)S(1)}, bf16[64,2048]{1,0:T(8,128)(2,1)S(1)}, u32[]{:S(2)}, u32[]{:S(2)}) collective-permute-start(bf16[64,2048]{1,0:T(8,128)(2,1)S(1)} %get-tuple-element.292.p0), channel_id=1, source_target_pairs={{0,2},{1,3},{2,0},{3,1},{4,6},{5,7},{6,4},{7,5},{8,10},{9,11},{10,... | collective-permute-start | bytes 786440 | tf_op jit(solution)/shard_map/ppermute | solution.py:684
  363.2 12.9 %collective-permute-start.69 = (bf16[64,2048]{1,0:T(8,128)(2,1)S(1)}, bf16[64,2048]{1,0:T(8,128)(2,1)S(1)}, u32[]{:S(2)}, u32[]{:S(2)}) collective-permute-start(bf16[64,2048]{1,0:T(8,128)(2,1)S(1)} %get-tuple-element.292.p0), channel_id=1, source_target_pairs={{0,3},{1,2},{2,1},{3,0},{4,7},{5,6},{6,5},{7,4},{8,11},{9,10},{10,... | collective-permute-start | bytes 786440 | tf_op jit(solution)/shard_map/ppermute | solution.py:684
  365.0 18.6 %collective-permute-start.77 = (bf16[64,2048]{1,0:T(8,128)(2,1)S(1)}, bf16[64,2048]{1,0:T(8,128)(2,1)S(1)}, u32[]{:S(2)}, u32[]{:S(2)}) collective-permute-start(bf16[64,2048]{1,0:T(8,128)(2,1)S(1)} %get-tuple-element.315.p0), channel_id=1, source_target_pairs={{0,1},{1,0},{2,3},{3,2},{4,5},{5,4},{6,7},{7,6},{8,9},{9,8},{10,11... | collective-permute-start | bytes 786440 | tf_op jit(solution)/shard_map/ppermute | solution.py:684
  365.0 20.6 %collective-permute-start.78 = (bf16[64,2048]{1,0:T(8,128)(2,1)S(1)}, bf16[64,2048]{1,0:T(8,128)(2,1)S(1)}, u32[]{:S(2)}, u32[]{:S(2)}) collective-permute-start(bf16[64,2048]{1,0:T(8,128)(2,1)S(1)} %get-tuple-element.315.p0), channel_id=1, source_target_pairs={{0,2},{1,3},{2,0},{3,1},{4,6},{5,7},{6,4},{7,5},{8,10},{9,11},{10,... | collective-permute-start | bytes 786440 | tf_op jit(solution)/shard_map/ppermute | solution.py:684
  368.1 19.7 %collective-permute-start.79 = (bf16[64,2048]{1,0:T(8,128)(2,1)S(1)}, bf16[64,2048]{1,0:T(8,128)(2,1)S(1)}, u32[]{:S(2)}, u32[]{:S(2)}) collective-permute-start(bf16[64,2048]{1,0:T(8,128)(2,1)S(1)} %get-tuple-element.315.p0), channel_id=1, source_target_pairs={{0,3},{1,2},{2,1},{3,0},{4,7},{5,6},{6,5},{7,4},{8,11},{9,10},{10,... | collective-permute-start | bytes 786440 | tf_op jit(solution)/shard_map/ppermute | solution.py:684
  402.6 27.1 %collective-permute-start.84 = (bf16[256,2048]{1,0:T(8,128)(2,1)S(1)}, bf16[256,2048]{1,0:T(8,128)(2,1)S(1)}, u32[]{:S(2)}, u32[]{:S(2)}) collective-permute-start(bf16[256,2048]{1,0:T(8,128)(2,1)S(1)} %settle.2), channel_id=1, source_target_pairs={{32,64},{64,32},{33,65},{65,33},{34,66},{66,34},{35,67},{67,35},{3... | collective-permute-start | bytes 3145736 | tf_op jit(solution)/shard_map/ppermute | solution.py:803
  404.7 26.4 %collective-permute-start.85 = (bf16[256,2048]{1,0:T(8,128)(2,1)S(1)}, bf16[256,2048]{1,0:T(8,128)(2,1)S(1)}, u32[]{:S(2)}, u32[]{:S(2)}) collective-permute-start(bf16[256,2048]{1,0:T(8,128)(2,1)S(1)} %settle.2), channel_id=1, source_target_pairs={{0,4},{4,0},{32,68},{36,64},{64,36},{68,32},{96,100},{100,96},{1,5... | collective-permute-start | bytes 3145736 | tf_op jit(solution)/shard_map/ppermute | solution.py:809
  422.7 15.0 %collective-permute-start.87 = (bf16[64,2048]{1,0:T(8,128)(2,1)S(1)}, bf16[64,2048]{1,0:T(8,128)(2,1)S(1)}, u32[]{:S(2)}, u32[]{:S(2)}) collective-permute-start(bf16[64,2048]{1,0:T(8,128)(2,1)S(1)} %get-tuple-element.327), channel_id=1, source_target_pairs={{0,2},{1,3},{2,0},{3,1},{4,6},{5,7},{6,4},{7,5},{8,10},{9,11},{10,... | collective-permute-start | bytes 786440 | tf_op jit(solution)/shard_map/ppermute | solution.py:684
  425.6 14.2 %collective-permute-start.88 = (bf16[64,2048]{1,0:T(8,128)(2,1)S(1)}, bf16[64,2048]{1,0:T(8,128)(2,1)S(1)}, u32[]{:S(2)}, u32[]{:S(2)}) collective-permute-start(bf16[64,2048]{1,0:T(8,128)(2,1)S(1)} %get-tuple-element.328), channel_id=1, source_target_pairs={{0,3},{1,2},{2,1},{3,0},{4,7},{5,6},{6,5},{7,4},{8,11},{9,10},{10,... | collective-permute-start | bytes 786440 | tf_op jit(solution)/shard_map/ppermute | solution.py:684
  442.5 13.4 %collective-permute-start.91 = (bf16[64,2048]{1,0:T(8,128)(2,1)S(1)}, bf16[64,2048]{1,0:T(8,128)(2,1)S(1)}, u32[]{:S(2)}, u32[]{:S(2)}) collective-permute-start(bf16[64,2048]{1,0:T(8,128)(2,1)S(1)} %get-tuple-element.332.p0), channel_id=1, source_target_pairs={{0,3},{1,2},{2,1},{3,0},{4,7},{5,6},{6,5},{7,4},{8,11},{9,10},{10,... | collective-permute-start | bytes 786440 | tf_op jit(solution)/shard_map/ppermute | solution.py:684
  444.3 17.5 %collective-permute-start.93 = (bf16[256,1024]{1,0:T(8,128)(2,1)S(1)}, bf16[256,1024]{1,0:T(8,128)(2,1)S(1)}, u32[]{:S(2)}, u32[]{:S(2)}) collective-permute-start(bf16[256,1024]{1,0:T(8,128)(2,1)S(1)} %get-tuple-element.338), channel_id=1, source_target_pairs={{0,64},{64,0},{1,65},{65,1},{2,66},{66,2},{3,67},{67,3},{4,68},{68... | collective-permute-start | bytes 1572872 | tf_op jit(solution)/shard_map/ppermute | solution.py:684
  471.9 154.6 %reduce-scatter.6.cloned.1.call-start = ((), (), s32[]{:S(2)}) async-start(), calls=%async_computation.6 | async-start | bytes 4718592 | tf_op jit(solution)/shard_map/reduce_scatter | solution.py:765
  471.9 26.0 %collective-permute-start.98 = (bf16[256,2048]{1,0:T(8,128)(2,1)S(1)}, bf16[256,2048]{1,0:T(8,128)(2,1)S(1)}, u32[]{:S(2)}, u32[]{:S(2)}) collective-permute-start(bf16[256,2048]{1,0:T(8,128)(2,1)S(1)} %get-tuple-element.284.refs_0_.refs_6_), channel_id=1, source_target_pairs={{0,64},{64,0},{1,65},{65,1},{2,66},{66,2},{3,67},{67,3},{4,68},{68... | collective-permute-start | bytes 3145736 | tf_op jit(solution)/shard_map/ppermute | solution.py:684
  472.4 25.5 %collective-permute-start.97 = (bf16[256,2048]{1,0:T(8,128)(2,1)S(1)}, bf16[256,2048]{1,0:T(8,128)(2,1)S(1)}, u32[]{:S(2)}, u32[]{:S(2)}) collective-permute-start(bf16[256,2048]{1,0:T(8,128)(2,1)S(1)} %get-tuple-element.341.refs_0_.refs_4_), channel_id=1, source_target_pairs={{0,64},{64,0},{1,65},{65,1},{2,66},{66,2},{3,67},{67,3},{4,68},{68... | collective-permute-start | bytes 3145736 | tf_op jit(solution)/shard_map/ppermute | solution.py:684
  479.1 14.8 %collective-permute-start.95 = (bf16[64,2048]{1,0:T(8,128)(2,1)S(1)}, bf16[64,2048]{1,0:T(8,128)(2,1)S(1)}, u32[]{:S(2)}, u32[]{:S(2)}) collective-permute-start(bf16[64,2048]{1,0:T(8,128)(2,1)S(1)} %get-tuple-element.344), channel_id=1, source_target_pairs={{0,2},{1,3},{2,0},{3,1},{4,6},{5,7},{6,4},{7,5},{8,10},{9,11},{10,... | collective-permute-start | bytes 786440 | tf_op jit(solution)/shard_map/ppermute | solution.py:684
  482.1 13.8 %collective-permute-start.96 = (bf16[64,2048]{1,0:T(8,128)(2,1)S(1)}, bf16[64,2048]{1,0:T(8,128)(2,1)S(1)}, u32[]{:S(2)}, u32[]{:S(2)}) collective-permute-start(bf16[64,2048]{1,0:T(8,128)(2,1)S(1)} %get-tuple-element.345), channel_id=1, source_target_pairs={{0,3},{1,2},{2,1},{3,0},{4,7},{5,6},{6,5},{7,4},{8,11},{9,10},{10,... | collective-permute-start | bytes 786440 | tf_op jit(solution)/shard_map/ppermute | solution.py:684
  507.7 134.3 %reduce-scatter.4.cloned.1.call-start = ((), (), s32[]{:S(2)}) async-start(), calls=%async_computation.5 | async-start | bytes 5242880 | tf_op jit(solution)/shard_map/reduce_scatter | solution.py:784
  507.9 17.7 %collective-permute-start.101 = (bf16[80,2048]{1,0:T(8,128)(2,1)S(1)}, bf16[80,2048]{1,0:T(8,128)(2,1)S(1)}, u32[]{:S(2)}, u32[]{:S(2)}) collective-permute-start(bf16[80,2048]{1,0:T(8,128)(2,1)S(1)} %get-tuple-element.357.p0), channel_id=1, source_target_pairs={{0,3},{1,2},{2,1},{3,0},{4,7},{5,6},{6,5},{7,4},{8,11},{9,10},{10,... | collective-permute-start | bytes 983048 | tf_op jit(solution)/shard_map/ppermute | solution.py:684
  508.9 16.8 %collective-permute-start.99 = (bf16[80,2048]{1,0:T(8,128)(2,1)S(1)}, bf16[80,2048]{1,0:T(8,128)(2,1)S(1)}, u32[]{:S(2)}, u32[]{:S(2)}) collective-permute-start(bf16[80,2048]{1,0:T(8,128)(2,1)S(1)} %get-tuple-element.357.p0), channel_id=1, source_target_pairs={{0,1},{1,0},{2,3},{3,2},{4,5},{5,4},{6,7},{7,6},{8,9},{9,8},{10,11... | collective-permute-start | bytes 983048 | tf_op jit(solution)/shard_map/ppermute | solution.py:684
  553.8 21.3 %collective-permute-start.107 = (bf16[256,384]{1,0:T(8,128)(2,1)S(1)}, bf16[256,384]{1,0:T(8,128)(2,1)S(1)}, u32[]{:S(2)}, u32[]{:S(2)}) collective-permute-start(bf16[256,384]{1,0:T(8,128)(2,1)S(1)} %get-tuple-element.371), channel_id=1, source_target_pairs={{0,16},{8,24},{16,0},{24,8},{1,17},{9,25},{17,1},{25,9},{2,18},{10... | collective-permute-start | bytes 589832 | tf_op jit(solution)/shard_map/ppermute | solution.py:684
  556.9 18.1 %collective-permute-start.108 = (bf16[256,384]{1,0:T(8,128)(2,1)S(1)}, bf16[256,384]{1,0:T(8,128)(2,1)S(1)}, u32[]{:S(2)}, u32[]{:S(2)}) collective-permute-start(bf16[256,384]{1,0:T(8,128)(2,1)S(1)} %get-tuple-element.372), channel_id=1, source_target_pairs={{0,24},{8,16},{16,8},{24,0},{1,25},{9,17},{17,9},{25,1},{2,26},{10... | collective-permute-start | bytes 589832 | tf_op jit(solution)/shard_map/ppermute | solution.py:684
  557.5 23.7 %collective-permute-start.110 = (bf16[256,1536]{1,0:T(8,128)(2,1)S(1)}, bf16[256,1536]{1,0:T(8,128)(2,1)S(1)}, u32[]{:S(2)}, u32[]{:S(2)}) collective-permute-start(bf16[256,1536]{1,0:T(8,128)(2,1)S(1)} %copy-done.43), channel_id=1, source_target_pairs={{0,64},{64,0},{1,65},{65,1},{2,66},{66,2},{3,67},{67,3},{4,68},{68... | collective-permute-start | bytes 2359304 | tf_op jit(solution)/shard_map/ppermute | solution.py:684
  597.3 14.8 %collective-permute-start.115 = (bf16[64,2048]{1,0:T(8,128)(2,1)S(1)}, bf16[64,2048]{1,0:T(8,128)(2,1)S(1)}, u32[]{:S(2)}, u32[]{:S(2)}) collective-permute-start(bf16[64,2048]{1,0:T(8,128)(2,1)S(1)} %get-tuple-element.390), channel_id=1, source_target_pairs={{0,3},{1,2},{2,1},{3,0},{4,7},{5,6},{6,5},{7,4},{8,11},{9,10},{10,... | collective-permute-start | bytes 786440 | tf_op jit(solution)/shard_map/ppermute | solution.py:684
  601.4 16.5 %collective-permute-start.126 = (f32[32,512]{1,0:T(8,128)S(1)}, f32[32,512]{1,0:T(8,128)S(1)}, u32[]{:S(2)}, u32[]{:S(2)}) collective-permute-start(f32[32,512]{1,0:T(8,128)S(1)} %fusion.4), channel_id=1, source_target_pairs={{0,16},{8,24},{16,0},{24,8},{1,17},{9,25},{17,1},{25,9},{2,18},{10... | collective-permute-start | bytes 196616 | tf_op jit(solution)/shard_map/ppermute | solution.py:684
  601.4 16.5 %collective-permute-start.127 = (f32[32,512]{1,0:T(8,128)S(1)}, f32[32,512]{1,0:T(8,128)S(1)}, u32[]{:S(2)}, u32[]{:S(2)}) collective-permute-start(f32[32,512]{1,0:T(8,128)S(1)} %fusion.4), channel_id=1, source_target_pairs={{0,8},{8,0},{16,24},{24,16},{1,9},{9,1},{17,25},{25,17},{2,10},{10... | collective-permute-start | bytes 196616 | tf_op jit(solution)/shard_map/ppermute | solution.py:684
  626.3 19.2 %collective-permute-start.118 = (bf16[2,64,2048]{2,1,0:T(8,128)(2,1)S(1)}, bf16[2,64,2048]{2,1,0:T(8,128)(2,1)S(1)}, u32[]{:S(2)}, u32[]{:S(2)}) collective-permute-start(bf16[2,64,2048]{2,1,0:T(8,128)(2,1)S(1)} %pad_maximum_fusion.p0), channel_id=1, source_target_pairs={{0,1},{1,0},{2,3},{3,2},{4,5},{5,4},{6,7},{7,6},{8,9},{9,8},{10,11... | collective-permute-start | bytes 1572872 | tf_op jit(solution)/shard_map/ppermute | solution.py:684
  628.6 13.4 %collective-permute-start.121 = (bf16[256,1024]{1,0:T(8,128)(2,1)S(1)}, bf16[256,1024]{1,0:T(8,128)(2,1)S(1)}, u32[]{:S(2)}, u32[]{:S(2)}) collective-permute-start(bf16[256,1024]{1,0:T(8,128)(2,1)S(1)} %far_halves.1), channel_id=1, source_target_pairs={{0,4},{4,0},{1,5},{5,1},{2,6},{6,2},{3,7},{7,3},{8,12},{12,8},{9,1... | collective-permute-start | bytes 1572872 | tf_op jit(solution)/shard_map/ppermute | solution.py:684
  629.9 22.3 %collective-permute-start.119 = (bf16[2,64,2048]{2,1,0:T(8,128)(2,1)S(1)}, bf16[2,64,2048]{2,1,0:T(8,128)(2,1)S(1)}, u32[]{:S(2)}, u32[]{:S(2)}) collective-permute-start(bf16[2,64,2048]{2,1,0:T(8,128)(2,1)S(1)} %pad_maximum_fusion.p0), channel_id=1, source_target_pairs={{0,2},{1,3},{2,0},{3,1},{4,6},{5,7},{6,4},{7,5},{8,10},{9,11},{10,... | collective-permute-start | bytes 1572872 | tf_op jit(solution)/shard_map/ppermute | solution.py:684
  631.2 25.4 %collective-permute-start.120 = (bf16[2,64,2048]{2,1,0:T(8,128)(2,1)S(1)}, bf16[2,64,2048]{2,1,0:T(8,128)(2,1)S(1)}, u32[]{:S(2)}, u32[]{:S(2)}) collective-permute-start(bf16[2,64,2048]{2,1,0:T(8,128)(2,1)S(1)} %pad_maximum_fusion.p0), channel_id=1, source_target_pairs={{0,3},{1,2},{2,1},{3,0},{4,7},{5,6},{6,5},{7,4},{8,11},{9,10},{10,... | collective-permute-start | bytes 1572872 | tf_op jit(solution)/shard_map/ppermute | solution.py:684
  644.0 18.6 %collective-permute-start.122 = (bf16[128,1024]{1,0:T(8,128)(2,1)S(1)}, bf16[128,1024]{1,0:T(8,128)(2,1)S(1)}, u32[]{:S(2)}, u32[]{:S(2)}) collective-permute-start(bf16[128,1024]{1,0:T(8,128)(2,1)S(1)} %get-tuple-element.397), channel_id=1, source_target_pairs={{0,32},{4,36},{32,0},{36,4},{1,33},{5,37},{33,1},{37,5},{2,34},{6,... | collective-permute-start | bytes 786440 | tf_op jit(solution)/shard_map/ppermute | solution.py:684
  644.1 18.5 %collective-permute-start.123 = (bf16[128,1024]{1,0:T(8,128)(2,1)S(1)}, bf16[128,1024]{1,0:T(8,128)(2,1)S(1)}, u32[]{:S(2)}, u32[]{:S(2)}) collective-permute-start(bf16[128,1024]{1,0:T(8,128)(2,1)S(1)} %get-tuple-element.398), channel_id=1, source_target_pairs={{0,4},{4,0},{32,36},{36,32},{1,5},{5,1},{33,37},{37,33},{2,6},{6,2... | collective-permute-start | bytes 786440 | tf_op jit(solution)/shard_map/ppermute | solution.py:684
  645.6 17.0 %collective-permute-start.124 = (bf16[128,1024]{1,0:T(8,128)(2,1)S(1)}, bf16[128,1024]{1,0:T(8,128)(2,1)S(1)}, u32[]{:S(2)}, u32[]{:S(2)}) collective-permute-start(bf16[128,1024]{1,0:T(8,128)(2,1)S(1)} %get-tuple-element.399), channel_id=1, source_target_pairs={{0,36},{4,32},{32,4},{36,0},{1,37},{5,33},{33,5},{37,1},{2,38},{6,... | collective-permute-start | bytes 786440 | tf_op jit(solution)/shard_map/ppermute | solution.py:684
  (170 other events, 2115.3 us)
Sparse Core Ops, SparseCore 0:
  28.5 51.3 all-gather.2
  82.2 94.5 all-gather.4
  472.0 51.1 reduce-scatter.7
  525.4 60.9 reduce-scatter.5
  595.2 44.7 reduce-scatter.3
